TPU v7x, 32 devices: a whole 2x2x4 slice. The times are simulated.
32 devices in a mesh: batch: 8 (over y, x, core), fsdp: 4 (over z).
Axes of the slice: x: 2, y: 2, z: 4, core: 2. Of those that a mesh axis runs over, the one named last changes fastest.
Arguments:
- text: bfloat16 [128, 144, 1024], P(('batch', 'fsdp')), may hold values from -6 to 6
- memory: bfloat16 [128, 256, 1024], P(('batch', 'fsdp')), may hold values from -6 to 6
- text_lengths: int32 [128], P(('batch', 'fsdp')), may hold values from 1 to 144, 9216 in all
- memory_mask: int32 [128, 256], P(('batch', 'fsdp')), may hold values 0 or 1
- grad_out: bfloat16 [128, 144, 1024], P(('batch', 'fsdp')), may hold values from -6 to 6
- self_gain: bfloat16 [1024], P('fsdp'), may hold values from 0.5 to 1.5
- self_query: bfloat16 [1024, 1024], P('fsdp'), may hold values from -0.25 to 0.25
- self_key: bfloat16 [1024, 1024], P('fsdp'), may hold values from -0.25 to 0.25
- self_value: bfloat16 [1024, 1024], P('fsdp'), may hold values from -0.1875 to 0.1875
- self_output: bfloat16 [1024, 1024], P('fsdp'), may hold values from -0.5 to 0.5
- cross_gain: bfloat16 [1024], P('fsdp'), may hold values from 0.5 to 1.5
- cross_query: bfloat16 [1024, 1024], P('fsdp'), may hold values from -0.25 to 0.25
- cross_key: bfloat16 [1024, 1024], P('fsdp'), may hold values from -0.25 to 0.25
- cross_value: bfloat16 [1024, 1024], P('fsdp'), may hold values from -0.1875 to 0.1875
- cross_output: bfloat16 [1024, 1024], P('fsdp'), may hold values from -0.5 to 0.5
- mlp_gain: bfloat16 [1024], P('fsdp'), may hold values from 0.5 to 1.5
- mlp_gate: bfloat16 [1024, 2816], P('fsdp'), may hold values from -0.1875 to 0.1875
- mlp_up: bfloat16 [1024, 2816], P('fsdp'), may hold values from -0.1875 to 0.1875
- mlp_down: bfloat16 [2816, 1024], P('fsdp'), may hold values from -0.15625 to 0.15625
Outputs:
- block_out: bfloat16 [128, 144, 1024], P(('batch', 'fsdp'))
- grad_text: float32 [128, 144, 1024], P(('batch', 'fsdp'))
- grad_memory: float32 [128, 256, 1024], P(('batch', 'fsdp'))
- grad_self_gain: float32 [1024], P('fsdp')
- grad_self_query: float32 [1024, 1024], P('fsdp')
- grad_self_key: float32 [1024, 1024], P('fsdp')
- grad_self_value: float32 [1024, 1024], P('fsdp')
- grad_self_output: float32 [1024, 1024], P('fsdp')
- grad_cross_gain: float32 [1024], P('fsdp')
- grad_cross_query: float32 [1024, 1024], P('fsdp')
- grad_cross_key: float32 [1024, 1024], P('fsdp')
- grad_cross_value: float32 [1024, 1024], P('fsdp')
- grad_cross_output: float32 [1024, 1024], P('fsdp')
- grad_mlp_gain: float32 [1024], P('fsdp')
- grad_mlp_gate: float32 [1024, 2816], P('fsdp')
- grad_mlp_up: float32 [1024, 2816], P('fsdp')
- grad_mlp_down: float32 [2816, 1024], P('fsdp')
Inputs may be any that keep to these rules, and one draw needn't show every extreme that they name: `text_lengths`: text slots at or past an item's length are padding; they are still computed.
All inputs are finite; a program needn't handle non-finite values. No bound on the sum of `text_lengths` or of `memory_mask` on one device may be relied on, other than what follows from the above.
Results may differ from a plain program's by a relative error of at most 0.028.
Values may be sent and summed in bfloat16 or wider, within the bound.
No kernel may reach another device: no remote copies, remote signals or barrier semaphores. Data moves between devices by JAX's collectives and lax.ppermute only.
A program may use at most 384 MiB of HBM per device.

v0:
```python
import jax
import jax.numpy as jnp
from jax import lax
from jax.sharding import PartitionSpec as P

HEADS = 16


epsilon = 1e-06
masked_score = -1e30
score_scale = 0.125


def normalize(value, gain):
    factor = lax.rsqrt(jnp.mean(value * value, axis=-1, keepdims=True) + epsilon)
    return value * factor * gain


def gated_unit(gate, up_value):
    return jax.nn.gelu(gate, approximate=True) * up_value


def matmul_low(left, right):
    return jnp.dot(left, right, preferred_element_type=jnp.float32)


def project_back(grad_low, weight):
    return jnp.einsum("re,de->rd", grad_low, weight, preferred_element_type=jnp.float32)


def weight_grad(left, grad_low):
    return jnp.einsum("rd,re->de", left, grad_low, preferred_element_type=jnp.float32)


def norm_back(value, gain, grad_normed):
    _, pullback = jax.vjp(normalize, value, gain.astype(jnp.float32))
    return pullback(grad_normed)


def split_heads(value):
    return value.reshape(value.shape[0], value.shape[1], HEADS, value.shape[2] // HEADS)


def masked_scores(query_heads, key_heads, allowed):
    scores = (
        jnp.einsum("iqhd,ikhd->ihqk", query_heads, key_heads, preferred_element_type=jnp.float32)
        * score_scale
    )
    return jnp.where(allowed[:, None], scores, masked_score)


def attend_forward(query, keys, values, allowed):
    scores = masked_scores(split_heads(query), split_heads(keys), allowed)
    row_max = jnp.max(scores, axis=-1, keepdims=True)
    lifted = jnp.exp(scores - row_max)
    row_total = jnp.sum(lifted, axis=-1, keepdims=True)
    weights = (lifted / row_total).astype(jnp.bfloat16)
    mixed = jnp.einsum(
        "ihqk,ikhd->iqhd", weights, split_heads(values), preferred_element_type=jnp.float32
    )
    return (mixed.astype(jnp.bfloat16).reshape(query.shape), row_max + jnp.log(row_total))


def attend_backward(query, keys, values, allowed, log_total, grad_mixed):
    query_heads = split_heads(query)
    key_heads = split_heads(keys)
    value_heads = split_heads(values)
    grad_heads = split_heads(grad_mixed)
    probs = jnp.exp(masked_scores(query_heads, key_heads, allowed) - log_total)
    grad_values = jnp.einsum(
        "ihqk,iqhd->ikhd",
        probs.astype(jnp.bfloat16),
        grad_heads,
        preferred_element_type=jnp.float32,
    )
    grad_probs = jnp.einsum(
        "iqhd,ikhd->ihqk", grad_heads, value_heads, preferred_element_type=jnp.float32
    )
    inner_total = jnp.sum(grad_probs * probs, axis=-1, keepdims=True)
    grad_scores = jnp.where(allowed[:, None], probs * (grad_probs - inner_total), 0.0).astype(
        jnp.bfloat16
    )
    grad_query = (
        jnp.einsum("ihqk,ikhd->iqhd", grad_scores, key_heads, preferred_element_type=jnp.float32)
        * score_scale
    )
    grad_keys = (
        jnp.einsum("ihqk,iqhd->ikhd", grad_scores, query_heads, preferred_element_type=jnp.float32)
        * score_scale
    )
    return (
        grad_query.astype(jnp.bfloat16).reshape(-1, query.shape[2]),
        grad_keys.astype(jnp.bfloat16).reshape(-1, keys.shape[2]),
        grad_values.astype(jnp.bfloat16).reshape(-1, values.shape[2]),
    )


def gather_self(gain, query, key, value, output):
    return (
        lax.all_gather(gain, "fsdp", axis=0, tiled=True),
        lax.all_gather(query, "fsdp", axis=0, tiled=True),
        lax.all_gather(key, "fsdp", axis=0, tiled=True),
        lax.all_gather(value, "fsdp", axis=0, tiled=True),
        lax.all_gather(output, "fsdp", axis=0, tiled=True),
    )


def gather_cross(gain, query, key, value, output):
    return (
        lax.all_gather(gain, "fsdp", axis=0, tiled=True),
        lax.all_gather(query, "fsdp", axis=0, tiled=True),
        lax.all_gather(key, "fsdp", axis=0, tiled=True),
        lax.all_gather(value, "fsdp", axis=0, tiled=True),
        lax.all_gather(output, "fsdp", axis=0, tiled=True),
    )


def gather_mlp(gain, gate, up_weight, down):
    return (
        lax.all_gather(gain, "fsdp", axis=0, tiled=True),
        lax.all_gather(gate, "fsdp", axis=0, tiled=True),
        lax.all_gather(up_weight, "fsdp", axis=0, tiled=True),
        lax.all_gather(down, "fsdp", axis=0, tiled=True),
    )


def run_forward(text, memory, allowed_self, allowed_cross, self_part, cross_part, mlp_part):
    item_count, text_rows, features = text.shape
    shape_text = (item_count, text_rows, features)
    flat_text = text.reshape(-1, features).astype(jnp.float32)
    flat_memory = memory.reshape(-1, features)
    normed_one = normalize(flat_text, self_part[0].astype(jnp.float32)).astype(jnp.bfloat16)
    query_one = matmul_low(normed_one, self_part[1]).astype(jnp.bfloat16).reshape(shape_text)
    key_one = matmul_low(normed_one, self_part[2]).astype(jnp.bfloat16).reshape(shape_text)
    value_one = matmul_low(normed_one, self_part[3]).astype(jnp.bfloat16).reshape(shape_text)
    mixed_one, total_one = attend_forward(query_one, key_one, value_one, allowed_self)
    mixed_one = mixed_one.reshape(-1, features)
    hidden_one = flat_text + matmul_low(mixed_one, self_part[4])
    normed_two = normalize(hidden_one, cross_part[0].astype(jnp.float32)).astype(jnp.bfloat16)
    query_two = matmul_low(normed_two, cross_part[1]).astype(jnp.bfloat16).reshape(shape_text)
    key_two = matmul_low(flat_memory, cross_part[2]).astype(jnp.bfloat16).reshape(memory.shape)
    value_two = matmul_low(flat_memory, cross_part[3]).astype(jnp.bfloat16).reshape(memory.shape)
    mixed_two, total_two = attend_forward(query_two, key_two, value_two, allowed_cross)
    mixed_two = mixed_two.reshape(-1, features)
    hidden_two = hidden_one + matmul_low(mixed_two, cross_part[4])
    normed_three = normalize(hidden_two, mlp_part[0].astype(jnp.float32)).astype(jnp.bfloat16)
    gate = matmul_low(normed_three, mlp_part[1])
    up_value = matmul_low(normed_three, mlp_part[2])
    inner = gated_unit(gate, up_value).astype(jnp.bfloat16)
    output = hidden_two + matmul_low(inner, mlp_part[3])
    return {
        "flat_text": flat_text,
        "normed_one": normed_one,
        "query_one": query_one,
        "key_one": key_one,
        "value_one": value_one,
        "total_one": total_one,
        "mixed_one": mixed_one,
        "hidden_one": hidden_one,
        "normed_two": normed_two,
        "query_two": query_two,
        "key_two": key_two,
        "value_two": value_two,
        "total_two": total_two,
        "mixed_two": mixed_two,
        "hidden_two": hidden_two,
        "normed_three": normed_three,
        "gate": gate,
        "up_value": up_value,
        "inner": inner,
        "output": output,
    }


def on_device(
    text,
    memory,
    text_lengths,
    memory_mask,
    grad_out,
    self_gain,
    self_query,
    self_key,
    self_value,
    self_output,
    cross_gain,
    cross_query,
    cross_key,
    cross_value,
    cross_output,
    mlp_gain,
    mlp_gate,
    mlp_up,
    mlp_down,
):
    item_count, text_rows, features = text.shape
    positions = lax.iota(jnp.int32, text_rows)
    causal = positions[:, None] >= positions[None, :]
    allowed_self = causal[None] & (positions[None, None, :] < text_lengths[:, None, None])
    allowed_cross = (memory_mask > 0)[:, None, :]
    self_part = gather_self(self_gain, self_query, self_key, self_value, self_output)
    cross_part = gather_cross(cross_gain, cross_query, cross_key, cross_value, cross_output)
    mlp_part = gather_mlp(mlp_gain, mlp_gate, mlp_up, mlp_down)
    saved = run_forward(text, memory, allowed_self, allowed_cross, self_part, cross_part, mlp_part)
    block_out = saved["output"].astype(jnp.bfloat16).reshape(text.shape)
    self_part = gather_self(self_gain, self_query, self_key, self_value, self_output)
    cross_part = gather_cross(cross_gain, cross_query, cross_key, cross_value, cross_output)
    mlp_part = gather_mlp(mlp_gain, mlp_gate, mlp_up, mlp_down)
    saved = run_forward(text, memory, allowed_self, allowed_cross, self_part, cross_part, mlp_part)
    flat_memory = memory.reshape(-1, features)
    grad_low = grad_out.reshape(-1, features)
    grad_mlp_down = weight_grad(saved["inner"], grad_low)
    grad_inner = project_back(grad_low, mlp_part[3])
    _, pullback = jax.vjp(gated_unit, saved["gate"], saved["up_value"])
    grad_gate, grad_up = pullback(grad_inner)
    low_gate = grad_gate.astype(jnp.bfloat16)
    low_up = grad_up.astype(jnp.bfloat16)
    grad_mlp_gate = weight_grad(saved["normed_three"], low_gate)
    grad_mlp_up = weight_grad(saved["normed_three"], low_up)
    grad_normed = project_back(low_gate, mlp_part[1]) + project_back(low_up, mlp_part[2])
    grad_hidden, grad_mlp_gain = norm_back(saved["hidden_two"], mlp_part[0], grad_normed)
    grad_two = grad_low.astype(jnp.float32) + grad_hidden
    low_two = grad_two.astype(jnp.bfloat16)
    grad_cross_output = weight_grad(saved["mixed_two"], low_two)
    grad_mixed = project_back(low_two, cross_part[4]).astype(jnp.bfloat16).reshape(text.shape)
    grad_query, grad_keys, grad_values = attend_backward(
        saved["query_two"],
        saved["key_two"],
        saved["value_two"],
        allowed_cross,
        saved["total_two"],
        grad_mixed,
    )
    grad_cross_query = weight_grad(saved["normed_two"], grad_query)
    grad_cross_key = weight_grad(flat_memory, grad_keys)
    grad_cross_value = weight_grad(flat_memory, grad_values)
    grad_memory = project_back(grad_keys, cross_part[2]) + project_back(grad_values, cross_part[3])
    grad_normed = project_back(grad_query, cross_part[1])
    grad_hidden, grad_cross_gain = norm_back(saved["hidden_one"], cross_part[0], grad_normed)
    grad_one = grad_two + grad_hidden
    low_one = grad_one.astype(jnp.bfloat16)
    grad_self_output = weight_grad(saved["mixed_one"], low_one)
    grad_mixed = project_back(low_one, self_part[4]).astype(jnp.bfloat16).reshape(text.shape)
    grad_query, grad_keys, grad_values = attend_backward(
        saved["query_one"],
        saved["key_one"],
        saved["value_one"],
        allowed_self,
        saved["total_one"],
        grad_mixed,
    )
    grad_self_query = weight_grad(saved["normed_one"], grad_query)
    grad_self_key = weight_grad(saved["normed_one"], grad_keys)
    grad_self_value = weight_grad(saved["normed_one"], grad_values)
    grad_normed = (
        project_back(grad_query, self_part[1])
        + project_back(grad_keys, self_part[2])
        + project_back(grad_values, self_part[3])
    )
    grad_hidden, grad_self_gain = norm_back(saved["flat_text"], self_part[0], grad_normed)
    grad_text = grad_one + grad_hidden
    shards = (
        lax.psum_scatter(
            grad_self_gain.astype(jnp.bfloat16), "fsdp", scatter_dimension=0, tiled=True
        ).astype(jnp.float32),
        lax.psum_scatter(
            grad_self_query.astype(jnp.bfloat16), "fsdp", scatter_dimension=0, tiled=True
        ).astype(jnp.float32),
        lax.psum_scatter(
            grad_self_key.astype(jnp.bfloat16), "fsdp", scatter_dimension=0, tiled=True
        ).astype(jnp.float32),
        lax.psum_scatter(
            grad_self_value.astype(jnp.bfloat16), "fsdp", scatter_dimension=0, tiled=True
        ).astype(jnp.float32),
        lax.psum_scatter(
            grad_self_output.astype(jnp.bfloat16), "fsdp", scatter_dimension=0, tiled=True
        ).astype(jnp.float32),
        lax.psum_scatter(
            grad_cross_gain.astype(jnp.bfloat16), "fsdp", scatter_dimension=0, tiled=True
        ).astype(jnp.float32),
        lax.psum_scatter(
            grad_cross_query.astype(jnp.bfloat16), "fsdp", scatter_dimension=0, tiled=True
        ).astype(jnp.float32),
        lax.psum_scatter(
            grad_cross_key.astype(jnp.bfloat16), "fsdp", scatter_dimension=0, tiled=True
        ).astype(jnp.float32),
        lax.psum_scatter(
            grad_cross_value.astype(jnp.bfloat16), "fsdp", scatter_dimension=0, tiled=True
        ).astype(jnp.float32),
        lax.psum_scatter(
            grad_cross_output.astype(jnp.bfloat16), "fsdp", scatter_dimension=0, tiled=True
        ).astype(jnp.float32),
        lax.psum_scatter(
            grad_mlp_gain.astype(jnp.bfloat16), "fsdp", scatter_dimension=0, tiled=True
        ).astype(jnp.float32),
        lax.psum_scatter(
            grad_mlp_gate.astype(jnp.bfloat16), "fsdp", scatter_dimension=0, tiled=True
        ).astype(jnp.float32),
        lax.psum_scatter(
            grad_mlp_up.astype(jnp.bfloat16), "fsdp", scatter_dimension=0, tiled=True
        ).astype(jnp.float32),
        lax.psum_scatter(
            grad_mlp_down.astype(jnp.bfloat16), "fsdp", scatter_dimension=0, tiled=True
        ).astype(jnp.float32),
    )
    totals = (
        lax.psum(shards[0].astype(jnp.bfloat16), "batch").astype(jnp.float32),
        lax.psum(shards[1].astype(jnp.bfloat16), "batch").astype(jnp.float32),
        lax.psum(shards[2].astype(jnp.bfloat16), "batch").astype(jnp.float32),
        lax.psum(shards[3].astype(jnp.bfloat16), "batch").astype(jnp.float32),
        lax.psum(shards[4].astype(jnp.bfloat16), "batch").astype(jnp.float32),
        lax.psum(shards[5].astype(jnp.bfloat16), "batch").astype(jnp.float32),
        lax.psum(shards[6].astype(jnp.bfloat16), "batch").astype(jnp.float32),
        lax.psum(shards[7].astype(jnp.bfloat16), "batch").astype(jnp.float32),
        lax.psum(shards[8].astype(jnp.bfloat16), "batch").astype(jnp.float32),
        lax.psum(shards[9].astype(jnp.bfloat16), "batch").astype(jnp.float32),
        lax.psum(shards[10].astype(jnp.bfloat16), "batch").astype(jnp.float32),
        lax.psum(shards[11].astype(jnp.bfloat16), "batch").astype(jnp.float32),
        lax.psum(shards[12].astype(jnp.bfloat16), "batch").astype(jnp.float32),
        lax.psum(shards[13].astype(jnp.bfloat16), "batch").astype(jnp.float32),
    )
    return (
        block_out,
        grad_text.reshape(text.shape),
        grad_memory.reshape(memory.shape),
        totals[0],
        totals[1],
        totals[2],
        totals[3],
        totals[4],
        totals[5],
        totals[6],
        totals[7],
        totals[8],
        totals[9],
        totals[10],
        totals[11],
        totals[12],
        totals[13],
    )


def solution(mesh):
    placed = (
        P(("batch", "fsdp"), None, None),
        P(("batch", "fsdp"), None, None),
        P(("batch", "fsdp")),
        P(("batch", "fsdp"), None),
        P(("batch", "fsdp"), None, None),
        P("fsdp"),
        P("fsdp", None),
        P("fsdp", None),
        P("fsdp", None),
        P("fsdp", None),
        P("fsdp"),
        P("fsdp", None),
        P("fsdp", None),
        P("fsdp", None),
        P("fsdp", None),
        P("fsdp"),
        P("fsdp", None),
        P("fsdp", None),
        P("fsdp", None),
    )
    return jax.shard_map(
        on_device,
        mesh=mesh,
        in_specs=placed,
        out_specs=(
            P(("batch", "fsdp"), None, None),
            P(("batch", "fsdp"), None, None),
            P(("batch", "fsdp"), None, None),
            P("fsdp"),
            P("fsdp", None),
            P("fsdp", None),
            P("fsdp", None),
            P("fsdp", None),
            P("fsdp"),
            P("fsdp", None),
            P("fsdp", None),
            P("fsdp", None),
            P("fsdp", None),
            P("fsdp"),
            P("fsdp", None),
            P("fsdp", None),
            P("fsdp", None),
        ),
        check_vma=False,
    )
```

profile of v0, /device:TPU:0, one launch (start us, length us, event | category | flops | bytes accessed | tf_op | source)
XLA Modules:
  0.0 1666.1 jit_solution(11085581069819125912)
XLA Ops:
  16.5 12.8 all-gather
  29.3 7.7 all-gather.1
  37.1 10.0 all-gather.2
  48.6 9.9 all-gather.19.cloned.1.call-done
  71.9 32.8 %all-gather.17.cloned.1.call-done = bf16[1024,1024]{1,0:T(8,128)(2,1)} async-done(((bf16[256,1024]{1,0:T(8,128)(2,1)}), bf16[1024,1024]{1,0:T(8,128)(2,1)}) %all-gather.17.cloned.1.call-update) | async-done | bytes 2097168 | tf_op jit(solution)/shard_map/all_gather | solution.py:101
  118.0 33.0 %all-gather.15.cloned.1.call-done = bf16[1024,1024]{1,0:T(8,128)(2,1)} async-done(((bf16[256,1024]{1,0:T(8,128)(2,1)}), bf16[1024,1024]{1,0:T(8,128)(2,1)}) %all-gather.15.cloned.1.call-update) | async-done | bytes 2097168 | tf_op jit(solution)/shard_map/all_gather | solution.py:103
  183.2 14.2 all-gather.21.cloned.1.call-done
  202.3 41.2 %all-gather.25.cloned.1.call-done = bf16[1024,1024]{1,0:T(8,128)(2,1)} async-done(((bf16[256,1024]{1,0:T(8,128)(2,1)}), bf16[1024,1024]{1,0:T(8,128)(2,1)}) %all-gather.25.cloned.1.call-update) | async-done | bytes 2097168 | tf_op jit(solution)/shard_map/all_gather | solution.py:111
  254.8 34.8 %all-gather.27.cloned.1.call-done = bf16[1024,1024]{1,0:T(8,128)(2,1)} async-done(((bf16[256,1024]{1,0:T(8,128)(2,1)}), bf16[1024,1024]{1,0:T(8,128)(2,1)}) %all-gather.27.cloned.1.call-update) | async-done | bytes 2097168 | tf_op jit(solution)/shard_map/all_gather | solution.py:112
  289.6 5.2 convolution_convert_fusion.3
  294.9 6.4 reshape.257
  301.2 5.9 copy.108
  307.1 28.8 %all-gather.23.cloned.1.call-done = bf16[1024,1024]{1,0:T(8,128)(2,1)} async-done(((bf16[256,1024]{1,0:T(8,128)(2,1)}), bf16[1024,1024]{1,0:T(8,128)(2,1)}) %all-gather.23.cloned.1.call-update) | async-done | bytes 2097168 | tf_op jit(solution)/shard_map/all_gather | solution.py:113
  335.9 5.2 convolution_convert_fusion.4
  341.1 6.7 reshape.255
  347.9 5.8 copy.109
  353.7 5.8 fusion.14
  359.5 5.0 fusion.5
  376.2 5.9 all-gather.29.cloned.1.call-done
  388.7 100.5 %all-gather.33.cloned.1.call-done = bf16[1024,2816]{1,0:T(8,128)(2,1)} async-done(((bf16[256,2816]{1,0:T(8,128)(2,1)}), bf16[1024,2816]{1,0:T(8,128)(2,1)}) %all-gather.33.cloned.1.call-update) | async-done | bytes 5767184 | tf_op jit(solution)/shard_map/all_gather | solution.py:122
  489.2 9.4 fusion.100
  498.6 97.1 %all-gather.31.cloned.1.call-done = bf16[1024,2816]{1,0:T(8,128)(2,1)} async-done(((bf16[256,2816]{1,0:T(8,128)(2,1)}), bf16[1024,2816]{1,0:T(8,128)(2,1)}) %all-gather.31.cloned.1.call-update) | async-done | bytes 5767184 | tf_op jit(solution)/shard_map/all_gather | solution.py:121
  595.7 9.4 fusion.99
  605.0 97.2 %all-gather.35.cloned.1.call-done = bf16[2816,1024]{1,0:T(8,128)(2,1)} async-done(((bf16[704,1024]{1,0:T(8,128)(2,1)}), bf16[2816,1024]{1,0:T(8,128)(2,1)}) %all-gather.35.cloned.1.call-update) | async-done | bytes 5767184 | tf_op jit(solution)/shard_map/all_gather | solution.py:123
  702.3 14.9 multiply_convert_fusion
  720.8 6.7 multiply_reduce_fusion.2
  740.9 7.3 fusion.102
  748.2 66.1 %fusion.48 = bf16[4,144,16,64]{1,3,2,0:T(8,128)(2,1)} fusion(bf16[4,256,16,64]{1,3,2,0:T(8,128)(2,1)} %copy.108, f32[4,16,144,256]{3,2,1,0:T(8,128)} %fusion.102, pred[4,256]{1,0:T(4,128)(4,1)S(1)} %copy-done.55, f32[4,16,144]{2,1,0:T(8,128)S(1)} %copy-done.45, f32[4,16,144,256]{3,2,1,0:T(8,128)} %copy-done.5), kind=kOutput, calls=%fused_computation.78 | convolution fusion | flops 329131264 | bytes 22189056 | tf_op jit(solution)/shard_map/ihqk,ikhd->iqhd/dot_general | solution.py:84
  823.7 5.4 convolution_convert_fusion.6
  829.4 6.5 convert_bitcast_fusion.2
  848.4 65.7 %fusion.51 = bf16[4,256,16,64]{1,3,2,0:T(8,128)(2,1)} fusion(bf16[4,144,16,64]{1,3,2,0:T(8,128)(2,1)} %copy.107, f32[4,16,144,256]{3,2,1,0:T(8,128)} %fusion.102, pred[4,256]{1,0:T(4,128)(4,1)S(1)} %copy-done.55, f32[4,16,144]{2,1,0:T(8,128)S(1)} %copy-done.45, f32[4,16,144,256]{3,2,1,0:T(8,128)} %copy-done.5), kind=kOutput, calls=%fused_computation.81 | convolution fusion | flops 330048768 | bytes 22189056 | tf_op jit(solution)/shard_map/ihqk,iqhd->ikhd/dot_general | solution.py:88
  941.1 7.4 fusion.103
  948.5 19.1 %fusion.50 = bf16[4,144,16,64]{1,3,2,0:T(8,128)(2,1)} fusion(bf16[4,144,16,64]{1,3,2,0:T(8,128)(2,1)} %copy.99, f32[4,16,144,144]{2,3,1,0:T(8,128)} %fusion.103, pred[4,144,144]{1,2,0:T(8,128)(4,1)S(1)} %copy-done.23, f32[4,16,144]{2,1,0:T(8,128)S(1)} %log_add_fusion, f32[4,16,144,144]{2,3,1,0:T(8,128)} %copy-done.4), kind=kOutput, calls=%fused_computation.80 | convolution fusion | flops 185656464 | bytes 13095936 | tf_op jit(solution)/shard_map/ihqk,iqhd->ikhd/dot_general | solution.py:88
  976.9 5.0 convolution_convert_fusion.9
  987.0 17.3 %fusion.49 = bf16[4,144,16,64]{1,3,2,0:T(8,128)(2,1)} fusion(bf16[4,144,16,64]{1,3,2,0:T(8,128)(2,1)} %copy.100, f32[4,16,144,144]{2,3,1,0:T(8,128)} %fusion.103, pred[4,144,144]{1,2,0:T(8,128)(4,1)S(1)} %copy-done.23, f32[4,16,144]{2,1,0:T(8,128)S(1)} %log_add_fusion, f32[4,16,144,144]{2,3,1,0:T(8,128)} %copy-done.4), kind=kOutput, calls=%fused_computation.79 | convolution fusion | flops 185656464 | bytes 13095936 | tf_op jit(solution)/shard_map/ihqk,ikhd->iqhd/dot_general | solution.py:84
  1017.8 6.7 convert_bitcast_fusion.3
  1036.2 9.5 convolution_convert_fusion.2
  1045.8 9.5 convolution_convert_fusion.1
  1055.7 9.4 convolution_convert_fusion
  1067.1 31.8 %reduce-scatter.18.cloned.1.call-done = bf16[256,1024]{1,0:T(8,128)(2,1)} async-done(((bf16[1024,1024]{1,0:T(8,128)(2,1)}), bf16[256,1024]{1,0:T(8,128)(2,1)}) %reduce-scatter.18.cloned.1.call-update) | async-done | bytes 524304 | tf_op jit(solution)/shard_map/reduce_scatter | solution.py:275
  1098.9 45.4 %reduce-scatter.12.cloned.1.call-done = bf16[256,1024]{1,0:T(8,128)(2,1)} async-done(((bf16[1024,1024]{1,0:T(8,128)(2,1)}), bf16[256,1024]{1,0:T(8,128)(2,1)}) %reduce-scatter.12.cloned.1.call-update) | async-done | bytes 524304 | tf_op jit(solution)/shard_map/reduce_scatter | solution.py:266
  1144.3 46.2 %reduce-scatter.16.cloned.1.call-done = bf16[256,1024]{1,0:T(8,128)(2,1)} async-done(((bf16[1024,1024]{1,0:T(8,128)(2,1)}), bf16[256,1024]{1,0:T(8,128)(2,1)}) %reduce-scatter.16.cloned.1.call-update) | async-done | bytes 524304 | tf_op jit(solution)/shard_map/reduce_scatter | solution.py:272
  1190.5 103.8 %reduce-scatter.28.cloned.1.call-done = bf16[256,2816]{1,0:T(8,128)(2,1)} async-done(((bf16[1024,2816]{1,0:T(8,128)(2,1)}), bf16[256,2816]{1,0:T(8,128)(2,1)}) %reduce-scatter.28.cloned.1.call-update) | async-done | bytes 1441808 | tf_op jit(solution)/shard_map/reduce_scatter | solution.py:296
  1294.2 105.1 %reduce-scatter.30.cloned.1.call-done = bf16[256,2816]{1,0:T(8,128)(2,1)} async-done(((bf16[1024,2816]{1,0:T(8,128)(2,1)}), bf16[256,2816]{1,0:T(8,128)(2,1)}) %reduce-scatter.30.cloned.1.call-update) | async-done | bytes 1441808 | tf_op jit(solution)/shard_map/reduce_scatter | solution.py:299
  1399.4 105.1 %reduce-scatter.32.cloned.1.call-done = bf16[704,1024]{1,0:T(8,128)(2,1)} async-done(((bf16[2816,1024]{1,0:T(8,128)(2,1)}), bf16[704,1024]{1,0:T(8,128)(2,1)}) %reduce-scatter.32.cloned.1.call-update) | async-done | bytes 1441808 | tf_op jit(solution)/shard_map/reduce_scatter | solution.py:302
  1513.6 11.1 all-reduce.5
  1524.9 12.9 all-reduce.3
  1555.6 87.8 %all-reduce.8.cloned.1.call-done = (bf16[256,1024]{0,1:T(8,128)(2,1)}, bf16[256,1024]{0,1:T(8,128)(2,1)}, bf16[256,1024]{1,0:T(8,128)(2,1)}, bf16[256,1024]{1,0:...) async-done(((bf16[256,1024]{0,1:T(8,128)(2,1)}, ...) | async-done | bytes 8519696 | tf_op jit(solution)/shard_map/psum | solution.py:314
  (299 shorter events, 254.2 us)
Async XLA Ops:
  7.2 282.4 %copy-start = (bf16[4,256,1024]{2,1,0:T(8,128)(2,1)S(1)}, bf16[4,256,1024]{2,1,0:T(8,128)(2,1)}, u32[]{:S(2)}) copy-start(bf16[4,256,1024]{2,1,0:T(8,128)(2,1)} %param.20) | copy-start | bytes 6291460
  7.2 51.2 %all-gather.19.cloned.1.call-start = ((), (), s32[]{:S(2)}) async-start(), calls=%async_computation.13 | async-start | bytes 2621440 | tf_op jit(solution)/shard_map/all_gather | solution.py:102
  7.9 96.7 %all-gather.17.cloned.1.call-start = ((), (), s32[]{:S(2)}) async-start(), calls=%async_computation.12 | async-start | bytes 2621440 | tf_op jit(solution)/shard_map/all_gather | solution.py:101
  8.7 142.2 %all-gather.15.cloned.1.call-start = ((), (), s32[]{:S(2)}) async-start(), calls=%async_computation.11 | async-start | bytes 2621440 | tf_op jit(solution)/shard_map/all_gather | solution.py:103
  9.4 188.0 %all-gather.21.cloned.1.call-start = ((), (), s32[]{:S(2)}) async-start(), calls=%async_computation.14 | async-start | bytes 2621440 | tf_op jit(solution)/shard_map/all_gather | solution.py:104
  10.0 233.5 %all-gather.25.cloned.1.call-start = ((), (), s32[]{:S(2)}) async-start(), calls=%async_computation.16 | async-start | bytes 2621440 | tf_op jit(solution)/shard_map/all_gather | solution.py:111
  10.6 279.0 %all-gather.27.cloned.1.call-start = ((), (), s32[]{:S(2)}) async-start(), calls=%async_computation.17 | async-start | bytes 2621440 | tf_op jit(solution)/shard_map/all_gather | solution.py:112
  11.2 324.7 %all-gather.23.cloned.1.call-start = ((), (), s32[]{:S(2)}) async-start(), calls=%async_computation.15 | async-start | bytes 2621440 | tf_op jit(solution)/shard_map/all_gather | solution.py:113
  11.9 370.2 %all-gather.29.cloned.1.call-start = ((), (), s32[]{:S(2)}) async-start(), calls=%async_computation.18 | async-start | bytes 2621440 | tf_op jit(solution)/shard_map/all_gather | solution.py:114
  12.7 476.5 %all-gather.33.cloned.1.call-start = ((), (), s32[]{:S(2)}) async-start(), calls=%async_computation.20 | async-start | bytes 7208960 | tf_op jit(solution)/shard_map/all_gather | solution.py:122
  13.4 15.8 copy-start.65
  13.4 15.9 copy-start.66
  13.4 23.6 %copy-start.56 = (s32[4,256]{1,0:T(4,128)S(1)}, s32[4,256]{1,0:T(4,128)}, u32[]{:S(2)}) copy-start(s32[4,256]{1,0:T(4,128)} %param.22) | copy-start | bytes 12292
  13.5 23.6 %copy-start.67 = (bf16[256]{0:T(256)(128)(2,1)S(1)}, bf16[256]{0:T(256)(128)(2,1)}, u32[]{:S(2)}) copy-start(bf16[256]{0:T(256)(128)(2,1)} %param.34) | copy-start | bytes 1540
  13.5 582.2 %all-gather.31.cloned.1.call-start = ((), (), s32[]{:S(2)}) async-start(), calls=%async_computation.19 | async-start | bytes 7208960 | tf_op jit(solution)/shard_map/all_gather | solution.py:121
  14.0 688.2 %all-gather.35.cloned.1.call-start = ((), (), s32[]{:S(2)}) async-start(), calls=%async_computation.21 | async-start | bytes 7208960 | tf_op jit(solution)/shard_map/all_gather | solution.py:123
  14.8 1052.2 %reduce-scatter.20.cloned.1.call-start = ((), (), s32[]{:S(2)}) async-start(), calls=%async_computation.26 | async-start | bytes 2621440 | tf_op jit(solution)/shard_map/reduce_scatter | solution.py:281
  15.9 31.2 %copy-start.43 = (f32[576]{0:T(1024)}, f32[576]{0:T(1024)S(1)}, u32[]{:S(2)}) copy-start(f32[576]{0:T(1024)S(1)} %rsqrt.39) | copy-start | bytes 6916
  29.2 17.8 %copy-start.41 = (f32[4,1,256]{2,1,0:T(1,128)}, f32[4,1,256]{2,1,0:T(1,128)S(1)}, u32[]{:S(2)}) copy-start(f32[4,1,256]{2,1,0:T(1,128)S(1)} %convert_element_type.366) | copy-start | bytes 12292
  37.0 316.7 %copy-start.53 = (pred[4,256]{1,0:T(4,128)(4,1)}, pred[4,256]{1,0:T(4,128)(4,1)S(1)}, u32[]{:S(2)}) copy-start(pred[4,256]{1,0:T(4,128)(4,1)S(1)} %broadcast_compare_fusion) | copy-start | bytes 3076
  48.6 122.7 %copy-start.22 = (pred[4,144,144]{1,2,0:T(8,128)(4,1)}, pred[4,144,144]{1,2,0:T(8,128)(4,1)S(1)}, u32[]{:S(2)}) copy-start(pred[4,144,144]{1,2,0:T(8,128)(4,1)S(1)} %broadcast_and_fusion) | copy-start | bytes 248836
  202.3 45.0 %copy-start.49 = (f32[576]{0:T(1024)}, f32[576]{0:T(1024)S(1)}, u32[]{:S(2)}) copy-start(f32[576]{0:T(1024)S(1)} %get-tuple-element.98) | copy-start | bytes 6916
  359.5 5.1 copy-start.5
  359.5 5.1 copy-start.6
  359.5 5.1 copy-start.54
  702.3 14.9 copy-start.58
  720.8 6.7 copy-start.52
  720.8 6.7 copy-start.28
  740.9 7.3 copy-start.45
  740.9 7.3 copy-start.55
  829.2 237.9 %reduce-scatter.24.cloned.1.call-start = ((), (), s32[]{:S(2)}) async-start(), calls=%async_computation.28 | async-start | bytes 2621440 | tf_op jit(solution)/shard_map/reduce_scatter | solution.py:287
  843.2 223.9 %reduce-scatter.26.cloned.1.call-start = ((), (), s32[]{:S(2)}) async-start(), calls=%async_computation.29 | async-start | bytes 2621440 | tf_op jit(solution)/shard_map/reduce_scatter | solution.py:290
  848.1 219.0 %reduce-scatter.22.cloned.1.call-start = ((), (), s32[]{:S(2)}) async-start(), calls=%async_computation.27 | async-start | bytes 2621440 | tf_op jit(solution)/shard_map/reduce_scatter | solution.py:284
  923.0 144.1 %reduce-scatter.14.cloned.1.call-start = ((), (), s32[]{:S(2)}) async-start(), calls=%async_computation.23 | async-start | bytes 2621440 | tf_op jit(solution)/shard_map/reduce_scatter | solution.py:269
  941.1 7.4 copy-start.23
  976.9 5.1 copy-start.24
  982.0 117.0 %reduce-scatter.18.cloned.1.call-start = ((), (), s32[]{:S(2)}) async-start(), calls=%async_computation.25 | async-start | bytes 2621440 | tf_op jit(solution)/shard_map/reduce_scatter | solution.py:275
  986.9 157.4 %reduce-scatter.12.cloned.1.call-start = ((), (), s32[]{:S(2)}) async-start(), calls=%async_computation.22 | async-start | bytes 2621440 | tf_op jit(solution)/shard_map/reduce_scatter | solution.py:266
  1012.8 4.9 copy-start.25
  1017.8 172.7 %reduce-scatter.16.cloned.1.call-start = ((), (), s32[]{:S(2)}) async-start(), calls=%async_computation.24 | async-start | bytes 2621440 | tf_op jit(solution)/shard_map/reduce_scatter | solution.py:272
  1036.2 258.1 %reduce-scatter.28.cloned.1.call-start = ((), (), s32[]{:S(2)}) async-start(), calls=%async_computation.30 | async-start | bytes 7208960 | tf_op jit(solution)/shard_map/reduce_scatter | solution.py:296
  1045.7 353.6 %reduce-scatter.30.cloned.1.call-start = ((), (), s32[]{:S(2)}) async-start(), calls=%async_computation.31 | async-start | bytes 7208960 | tf_op jit(solution)/shard_map/reduce_scatter | solution.py:299
  1055.2 449.2 %reduce-scatter.32.cloned.1.call-start = ((), (), s32[]{:S(2)}) async-start(), calls=%async_computation.32 | async-start | bytes 7208960 | tf_op jit(solution)/shard_map/reduce_scatter | solution.py:302
  1065.1 578.2 %all-reduce.8.cloned.1.call-start = ((), (), s32[]{:S(2)}) async-start(), calls=%async_computation.33 | async-start | bytes 17039360 | tf_op jit(solution)/shard_map/psum | solution.py:314
  1510.2 29.3 %copy-start.47 = (f32[576]{0:T(1024)S(1)}, f32[576]{0:T(1024)}, u32[]{:S(2)}) copy-start(f32[576]{0:T(1024)} %copy-done.46) | copy-start | bytes 6916
  1539.5 4.7 copy-start.18
  1539.5 4.7 copy-start.59
  1544.2 6.9 slice-start
  (49 other events, 140.4 us)
Sparse Core Ops, SparseCore 0:
  9.6 48.7 all-gather.18
  60.0 44.6 all-gather.16
  106.2 44.6 all-gather.14
  152.4 45.0 all-gather.20
  198.8 44.6 all-gather.24
  245.0 44.6 all-gather.26
  291.2 44.6 all-gather.22
  337.5 44.6 all-gather.28
  383.7 105.4 all-gather.32
  490.6 104.9 all-gather.30
  597.2 104.9 all-gather.34
  829.3 41.8 reduce-scatter.19
  873.5 43.2 reduce-scatter.23
  919.0 43.5 reduce-scatter.25
  964.9 43.1 reduce-scatter.21
  1010.2 43.1 reduce-scatter.13
  1055.7 43.1 reduce-scatter.17
  1101.1 43.1 reduce-scatter.11
  1147.3 43.1 reduce-scatter.15
  1192.6 101.5 reduce-scatter.27
  1296.6 102.7 reduce-scatter.29
  1401.7 102.7 reduce-scatter.31
  1510.2 133.1 all-reduce.7
where the time goes:
time: 1670 us
  waiting for transfers between devices  1030 us (62%)
  matrix products  387 us (23%)
  local copies, waits for them, and re-layouts  144 us (9%)
  blocking collectives  54.4 us (3%)
  other arithmetic  34.7 us (2%)
    reduce_scatter x1, waiting for transfers between devices, on_device(): lax.psum_scatter(grad_mlp_up.astype(jnp.bfloat16), 'fsdp', scatter_dimens...  105 us
    reduce_scatter x1, waiting for transfers between devices, on_device(): lax.psum_scatter(grad_mlp_down.astype(jnp.bfloat16), 'fsdp', scatter_dime...  105 us
    reduce_scatter x1, waiting for transfers between devices, on_device(): lax.psum_scatter(grad_mlp_gate.astype(jnp.bfloat16), 'fsdp', scatter_dime...  104 us
    all_gather x1, waiting for transfers between devices, gather_mlp(): lax.all_gather(up_weight, 'fsdp', axis=0, tiled=True)  100 us
    all_gather x1, waiting for transfers between devices, gather_mlp(): lax.all_gather(down, 'fsdp', axis=0, tiled=True)  97.2 us
    all_gather x1, waiting for transfers between devices, gather_mlp(): lax.all_gather(gate, 'fsdp', axis=0, tiled=True)  97.1 us
    psum x1, waiting for transfers between devices, on_device(): lax.psum(shards[7].astype(jnp.bfloat16), 'batch').astype(jnp.float32)  87.8 us
    dot_general x2, matrix products, attend_backward(): jnp.einsum('ihqk,iqhd->ikhd', grad_scores, query_heads, preferred_element...  84.8 us
  transfers between devices with their start and end apart: 23, of which 18 were waited for; matrix products, arithmetic and copies ran while one was open for 25% of the time, Pallas kernels for 0%

commit v1 on v0

v1 whole, which is shorter than its diff:
```python
import functools

import jax
import jax.numpy as jnp
from jax import lax
from jax.experimental import pallas as pl
from jax.experimental.pallas import tpu as pltpu
from jax.sharding import PartitionSpec as P

HEAD_DIM = 64
QUAD = 4
WIDE = HEAD_DIM * QUAD
EPSILON = 1e-06
MASKED = -1e30
SCALE = 0.125
VMEM_LIMIT = 56 * 1024 * 1024

BF16 = jnp.bfloat16
F32 = jnp.float32


def params():
    return pltpu.CompilerParams(vmem_limit_bytes=VMEM_LIMIT)


def dot(a, b, dims):
    return lax.dot_general(a, b, (dims, ((), ())), preferred_element_type=F32)


def stack_heads(value):
    lane = lax.broadcasted_iota(jnp.int32, value.shape, 1) // HEAD_DIM
    zero = jnp.zeros_like(value)
    return jnp.concatenate([jnp.where(lane == j, value, zero) for j in range(QUAD)], axis=0)


def join_heads(stacked):
    rows = stacked.shape[0] // QUAD
    lane = lax.broadcasted_iota(jnp.int32, (rows, WIDE), 1) // HEAD_DIM
    out = stacked[:rows]
    for j in range(1, QUAD):
        out = jnp.where(lane == j, stacked[j * rows : (j + 1) * rows], out)
    return out


def causal_mask(rows, keys, length):
    t = lax.broadcasted_iota(jnp.int32, (rows, keys), 0)
    u = lax.broadcasted_iota(jnp.int32, (rows, keys), 1)
    one = (u <= t) & (u < length)
    return jnp.concatenate([one] * QUAD, axis=0)


def forward_quad(q, k, v, allowed):
    stacked = stack_heads(q)
    scores = dot(stacked, k, ((1,), (1,))) * SCALE
    scores = jnp.where(allowed, scores, MASKED)
    top = jnp.max(scores, axis=-1, keepdims=True)
    lifted = jnp.exp(scores - top)
    total = jnp.sum(lifted, axis=-1, keepdims=True)
    probs = (lifted / total).astype(BF16)
    mixed = join_heads(dot(probs, v, ((1,), (0,))))
    return probs, mixed.astype(BF16)


def backward_quad(q, k, v, probs, grad, allowed):
    q_stack = stack_heads(q)
    g_stack = stack_heads(grad)
    grad_v = dot(probs, g_stack, ((0,), (0,)))
    grad_p = dot(g_stack, v, ((1,), (1,)))
    p = probs.astype(F32)
    inner = jnp.sum(grad_p * p, axis=-1, keepdims=True)
    grad_s = p * (grad_p - inner)
    if allowed is not None:
        grad_s = jnp.where(allowed, grad_s, 0.0)
    grad_s = grad_s.astype(BF16)
    grad_q = join_heads(dot(grad_s, k, ((1,), (0,)))) * SCALE
    grad_k = dot(grad_s, q_stack, ((0,), (0,))) * SCALE
    return grad_q.astype(BF16), grad_k.astype(BF16), grad_v.astype(BF16)


def self_forward_kernel(lengths, qkv_ref, o_ref, p_ref):
    rows, width = o_ref.shape[1], o_ref.shape[2]
    allowed = causal_mask(rows, rows, lengths[pl.program_id(0)])
    for h in range(width // WIDE):
        c = h * WIDE
        probs, mixed = forward_quad(
            qkv_ref[0, :, c : c + WIDE],
            qkv_ref[0, :, width + c : width + c + WIDE],
            qkv_ref[0, :, 2 * width + c : 2 * width + c + WIDE],
            allowed,
        )
        o_ref[0, :, c : c + WIDE] = mixed
        p_ref[0, h] = probs


def self_forward(qkv, lengths):
    items, rows, width3 = qkv.shape
    width = width3 // 3
    quads = width // WIDE
    return pl.pallas_call(
        self_forward_kernel,
        grid_spec=pltpu.PrefetchScalarGridSpec(
            num_scalar_prefetch=1,
            grid=(items,),
            in_specs=[pl.BlockSpec((1, rows, width3), lambda i, s: (i, 0, 0))],
            out_specs=[
                pl.BlockSpec((1, rows, width), lambda i, s: (i, 0, 0)),
                pl.BlockSpec((1, quads, QUAD * rows, rows), lambda i, s: (i, 0, 0, 0)),
            ],
        ),
        out_shape=[
            jax.ShapeDtypeStruct((items, rows, width), BF16),
            jax.ShapeDtypeStruct((items, quads, QUAD * rows, rows), BF16),
        ],
        compiler_params=params(),
        cost_estimate=pl.CostEstimate(
            flops=8 * items * quads * QUAD * rows * 256 * 256,
            bytes_accessed=2 * items * rows * (4 * width + 16 * rows),
            transcendentals=0,
        ),
    )(lengths, qkv)


def self_backward_kernel(qkv_ref, p_ref, g_ref, d_ref):
    width = g_ref.shape[2]
    for h in range(width // WIDE):
        c = h * WIDE
        grad_q, grad_k, grad_v = backward_quad(
            qkv_ref[0, :, c : c + WIDE],
            qkv_ref[0, :, width + c : width + c + WIDE],
            qkv_ref[0, :, 2 * width + c : 2 * width + c + WIDE],
            p_ref[0, h],
            g_ref[0, :, c : c + WIDE],
            None,
        )
        d_ref[0, :, c : c + WIDE] = grad_q
        d_ref[0, :, width + c : width + c + WIDE] = grad_k
        d_ref[0, :, 2 * width + c : 2 * width + c + WIDE] = grad_v


def self_backward(qkv, probs, grad):
    items, rows, width3 = qkv.shape
    width = width3 // 3
    quads = width // WIDE
    return pl.pallas_call(
        self_backward_kernel,
        grid=(items,),
        in_specs=[
            pl.BlockSpec((1, rows, width3), lambda i: (i, 0, 0)),
            pl.BlockSpec((1, quads, QUAD * rows, rows), lambda i: (i, 0, 0, 0)),
            pl.BlockSpec((1, rows, width), lambda i: (i, 0, 0)),
        ],
        out_specs=pl.BlockSpec((1, rows, width3), lambda i: (i, 0, 0)),
        out_shape=jax.ShapeDtypeStruct((items, rows, width3), BF16),
        compiler_params=params(),
        cost_estimate=pl.CostEstimate(
            flops=20 * items * quads * QUAD * rows * 256 * 256,
            bytes_accessed=2 * items * rows * (7 * width + 16 * rows),
            transcendentals=0,
        ),
    )(qkv, probs, grad)


def cross_forward_kernel(q_ref, kv_ref, m_ref, o_ref, p_ref):
    rows, width = o_ref.shape[1], o_ref.shape[2]
    allowed = m_ref[0] > 0
    for h in range(width // WIDE):
        c = h * WIDE
        probs, mixed = forward_quad(
            q_ref[0, :, c : c + WIDE],
            kv_ref[0, :, c : c + WIDE],
            kv_ref[0, :, width + c : width + c + WIDE],
            allowed,
        )
        o_ref[0, :, c : c + WIDE] = mixed
        p_ref[0, h] = probs


def cross_forward(q, kv, mask):
    items, rows, width = q.shape
    keys = kv.shape[1]
    quads = width // WIDE
    return pl.pallas_call(
        cross_forward_kernel,
        grid=(items,),
        in_specs=[
            pl.BlockSpec((1, rows, width), lambda i: (i, 0, 0)),
            pl.BlockSpec((1, keys, 2 * width), lambda i: (i, 0, 0)),
            pl.BlockSpec((1, 1, keys), lambda i: (i, 0, 0)),
        ],
        out_specs=[
            pl.BlockSpec((1, rows, width), lambda i: (i, 0, 0)),
            pl.BlockSpec((1, quads, QUAD * rows, keys), lambda i: (i, 0, 0, 0)),
        ],
        out_shape=[
            jax.ShapeDtypeStruct((items, rows, width), BF16),
            jax.ShapeDtypeStruct((items, quads, QUAD * rows, keys), BF16),
        ],
        compiler_params=params(),
        cost_estimate=pl.CostEstimate(
            flops=8 * items * quads * QUAD * rows * 256 * 256,
            bytes_accessed=2 * items * rows * (6 * width + 16 * keys),
            transcendentals=0,
        ),
    )(q, kv, mask)


def cross_backward_kernel(q_ref, kv_ref, p_ref, g_ref, m_ref, dq_ref, dkv_ref):
    width = g_ref.shape[2]
    allowed = m_ref[0] > 0
    for h in range(width // WIDE):
        c = h * WIDE
        grad_q, grad_k, grad_v = backward_quad(
            q_ref[0, :, c : c + WIDE],
            kv_ref[0, :, c : c + WIDE],
            kv_ref[0, :, width + c : width + c + WIDE],
            p_ref[0, h],
            g_ref[0, :, c : c + WIDE],
            allowed,
        )
        dq_ref[0, :, c : c + WIDE] = grad_q
        dkv_ref[0, :, c : c + WIDE] = grad_k
        dkv_ref[0, :, width + c : width + c + WIDE] = grad_v


def cross_backward(q, kv, probs, grad, mask):
    items, rows, width = q.shape
    keys = kv.shape[1]
    quads = width // WIDE
    return pl.pallas_call(
        cross_backward_kernel,
        grid=(items,),
        in_specs=[
            pl.BlockSpec((1, rows, width), lambda i: (i, 0, 0)),
            pl.BlockSpec((1, keys, 2 * width), lambda i: (i, 0, 0)),
            pl.BlockSpec((1, quads, QUAD * rows, keys), lambda i: (i, 0, 0, 0)),
            pl.BlockSpec((1, rows, width), lambda i: (i, 0, 0)),
            pl.BlockSpec((1, 1, keys), lambda i: (i, 0, 0)),
        ],
        out_specs=[
            pl.BlockSpec((1, rows, width), lambda i: (i, 0, 0)),
            pl.BlockSpec((1, keys, 2 * width), lambda i: (i, 0, 0)),
        ],
        out_shape=[
            jax.ShapeDtypeStruct((items, rows, width), BF16),
            jax.ShapeDtypeStruct((items, keys, 2 * width), BF16),
        ],
        compiler_params=params(),
        cost_estimate=pl.CostEstimate(
            flops=20 * items * quads * QUAD * rows * 256 * 256,
            bytes_accessed=2 * items * rows * (10 * width + 16 * keys),
            transcendentals=0,
        ),
    )(q, kv, probs, grad, mask)


def factor_of(value):
    return lax.rsqrt(jnp.mean(value * value, axis=-1, keepdims=True) + EPSILON)


def norm_back(value, factor, gain, grad):
    scaled = gain * grad
    along = jnp.mean(scaled * value, axis=-1, keepdims=True)
    grad_value = factor * scaled - value * (factor * factor * factor * along)
    return grad_value, jnp.sum(grad * value * factor, axis=0)


def matmul(left, right):
    return jnp.dot(left, right, preferred_element_type=F32)


def matmul_t(left, right):
    return jnp.einsum("re,de->rd", left, right, preferred_element_type=F32)


def weight_grad(left, right):
    return jnp.einsum("rd,re->de", left, right, preferred_element_type=F32).astype(BF16)


def gather(shard, spot):
    rows = shard.shape[0] // 8
    piece = lax.dynamic_slice_in_dim(shard, (spot % 8) * rows, rows, 0)
    groups = lax.axis_size("batch") // 8
    if groups > 1:
        inner = lax.all_gather(
            piece,
            "batch",
            axis=0,
            tiled=True,
            axis_index_groups=[[8 * g + j for j in range(8)] for g in range(groups)],
        )
        return lax.all_gather(inner, "fsdp", axis=0, tiled=True)
    return lax.all_gather(piece, ("fsdp", "batch"), axis=0, tiled=True)


def scatter(grad):
    batch = lax.axis_size("batch")
    if batch > 8:
        part = lax.psum_scatter(grad, "fsdp", scatter_dimension=0, tiled=True)
        return lax.psum(part, "batch").astype(F32)
    part = lax.psum_scatter(grad, ("fsdp", "batch"), scatter_dimension=0, tiled=True)
    return lax.all_gather(part, "batch", axis=0, tiled=True).astype(F32)


def on_device(
    text,
    memory,
    text_lengths,
    memory_mask,
    grad_out,
    self_gain,
    self_query,
    self_key,
    self_value,
    self_output,
    cross_gain,
    cross_query,
    cross_key,
    cross_value,
    cross_output,
    mlp_gain,
    mlp_gate,
    mlp_up,
    mlp_down,
):
    items, rows, width = text.shape
    keys = memory.shape[1]
    spot = lax.axis_index("batch")

    gains = lax.all_gather(jnp.stack([self_gain, cross_gain, mlp_gain]), "fsdp", axis=1, tiled=True)
    gains = gains.astype(F32)
    w_self = gather(
        jnp.concatenate([self_query, self_key, self_value, self_output], axis=1), spot
    )
    w_cross = gather(
        jnp.concatenate([cross_key, cross_value, cross_query, cross_output], axis=1), spot
    )
    w_down = gather(mlp_down, spot)
    w_wide = gather(jnp.concatenate([mlp_gate, mlp_up], axis=1), spot)
    w_qkv, w_so = w_self[:, : 3 * width], w_self[:, 3 * width :]
    w_kv = w_cross[:, : 2 * width]
    w_cq, w_co = w_cross[:, 2 * width : 3 * width], w_cross[:, 3 * width :]
    hidden = w_down.shape[0]

    x = text.reshape(-1, width).astype(F32)
    flat_memory = memory.reshape(-1, width)
    e3 = grad_out.reshape(-1, width)
    mask = memory_mask[:, None, :]

    c1 = factor_of(x)
    a1 = (x * c1 * gains[0]).astype(BF16)
    qkv = matmul(a1, w_qkv).astype(BF16).reshape(items, rows, 3 * width)
    o1, p1 = self_forward(qkv, text_lengths)
    o1 = o1.reshape(-1, width)
    h1 = x + matmul(o1, w_so)
    c2 = factor_of(h1)
    a2 = (h1 * c2 * gains[1]).astype(BF16)
    kv = matmul(flat_memory, w_kv).astype(BF16).reshape(items, keys, 2 * width)
    q2 = matmul(a2, w_cq).astype(BF16).reshape(items, rows, width)
    o2, p2 = cross_forward(q2, kv, mask)
    o2 = o2.reshape(-1, width)
    h2 = h1 + matmul(o2, w_co)
    c3 = factor_of(h2)
    a3 = (h2 * c3 * gains[2]).astype(BF16)
    d_inner = matmul_t(e3, w_down)
    gate = matmul(a3, w_wide[:, :hidden])
    up = matmul(a3, w_wide[:, hidden:])
    act, pull = jax.vjp(lambda g, u: jax.nn.gelu(g, approximate=True) * u, gate, up)
    inner = act.astype(BF16)
    d_gate, d_up = pull(d_inner)
    d_gate, d_up = d_gate.astype(BF16), d_up.astype(BF16)
    g_down = scatter(weight_grad(inner, e3))
    g_gate = scatter(weight_grad(a3, d_gate))
    g_up = scatter(weight_grad(a3, d_up))
    block_out = (h2 + matmul(inner, w_down)).astype(BF16)

    d_a3 = matmul_t(d_gate, w_wide[:, :hidden]) + matmul_t(d_up, w_wide[:, hidden:])
    back, gg3 = norm_back(h2, c3, gains[2], d_a3)
    d_h2 = e3.astype(F32) + back
    e2 = d_h2.astype(BF16)
    g_co = weight_grad(o2, e2)
    d_o2 = matmul_t(e2, w_co).astype(BF16).reshape(items, rows, width)
    d_q2, d_kv = cross_backward(q2, kv, p2, d_o2, mask)
    d_q2 = d_q2.reshape(-1, width)
    d_kv = d_kv.reshape(-1, 2 * width)
    g_cq = weight_grad(a2, d_q2)
    g_kv = weight_grad(flat_memory, d_kv)
    g_cross = scatter(jnp.concatenate([g_kv, g_cq, g_co], axis=1))
    grad_memory = matmul_t(d_kv, w_kv)
    d_a2 = matmul_t(d_q2, w_cq)
    back, gg2 = norm_back(h1, c2, gains[1], d_a2)
    d_h1 = d_h2 + back
    e1 = d_h1.astype(BF16)
    g_so = weight_grad(o1, e1)
    d_o1 = matmul_t(e1, w_so).astype(BF16).reshape(items, rows, width)
    d_qkv = self_backward(qkv, p1, d_o1).reshape(-1, 3 * width)
    g_qkv = weight_grad(a1, d_qkv)
    g_self = scatter(jnp.concatenate([g_qkv, g_so], axis=1))
    d_a1 = matmul_t(d_qkv, w_qkv)
    back, gg1 = norm_back(x, c1, gains[0], d_a1)
    grad_text = d_h1 + back

    gg = lax.psum(jnp.stack([gg1, gg2, gg3]), ("batch", "fsdp"))
    own = lax.axis_index("fsdp") * self_gain.shape[0]
    gg = lax.dynamic_slice_in_dim(gg, own, self_gain.shape[0], 1)
    cut = lambda g, j: g[:, j * width : (j + 1) * width]
    return (
        block_out.reshape(text.shape),
        grad_text.reshape(text.shape),
        grad_memory.reshape(memory.shape),
        gg[0],
        cut(g_self, 0),
        cut(g_self, 1),
        cut(g_self, 2),
        cut(g_self, 3),
        gg[1],
        cut(g_cross, 2),
        cut(g_cross, 0),
        cut(g_cross, 1),
        cut(g_cross, 3),
        gg[2],
        g_gate,
        g_up,
        g_down,
    )


def solution(mesh):
    rows = P(("batch", "fsdp"), None, None)
    gain, weight = P("fsdp"), P("fsdp", None)
    weights = (gain, weight, weight, weight, weight) * 2 + (gain, weight, weight, weight)
    return jax.shard_map(
        on_device,
        mesh=mesh,
        in_specs=(rows, rows, P(("batch", "fsdp")), P(("batch", "fsdp"), None), rows) + weights,
        out_specs=(rows, rows, rows) + weights,
        check_vma=False,
    )
```

time: 1670 us -> 1240 us (0.74)
  matrix products: 387 us -> 154 us
  waiting for transfers between devices: 1030 us -> 905 us
  local copies, waits for them, and re-layouts: 144 us -> 29.7 us
  Pallas kernels: 0 us -> 44.2 us
    dot_general x45 -> x24, matrix products: 387 us -> 154 us  [the longest x8 57.5 us: matmul(): return jnp.dot(left, right, preferred_element_type=F32)]
    all_gather x11 -> x9, waiting for transfers between devices: 495 us -> 305 us  [the longest x4 248 us: gather(): return lax.all_gather(piece, ('fsdp', 'batch'), axis=0, tiled=True)]
    reduce_scatter x11 -> x5, waiting for transfers between devices: 437 us -> 600 us  [scatter(): lax.psum_scatter(grad, ('fsdp', 'batch'), scatter_dimension=0, tiled=True)]
    psum x1 -> x0, waiting for transfers between devices: 87.8 us -> none  [on_device(): lax.psum(shards[7].astype(jnp.bfloat16), 'batch').astype(jnp.float32)]
    another operation x18 -> x3, local copies, waits for them, and re-layouts: 84.4 us -> 0.01 us  [on_device(): jnp.stack([self_gain, cross_gain, mlp_gain])]
    pallas_call x0 -> x4, Pallas kernels: none -> 44.2 us  [the longest x1 13.7 us: cross_backward(): pl.pallas_call(cross_backward_kernel, grid=(items,), in_specs=[pl.BlockSp...]
    convert_element_type x8 -> x0, local copies, waits for them, and re-layouts: 28.5 us -> none  [the longest x2 9.45 us: attend_backward(): grad_query.astype(jnp.bfloat16).reshape(-1, query.shape[2])]
    psum x1, blocking collectives: 12.9 us -> 37.4 us  [on_device(): gg = lax.psum(jnp.stack([gg1, gg2, gg3]), ('batch', 'fsdp'))]
  transfers between devices with their start and end apart: 23 -> 14, of which waited for: 18 -> 12; matrix products, arithmetic and copies ran while one was open for 25% -> 14% of each run, Pallas kernels for 0% -> 4%
where the time goes in v1:
time: 1240 us; the launch traced here: 1230 us
  waiting for transfers between devices  905 us (73%)
  matrix products  154 us (12%)
  blocking collectives  50.9 us (4%)
  Pallas kernels  44.2 us (4%)
  other arithmetic  32.6 us (3%)
  local copies, waits for them, and re-layouts  29.7 us (2%)
  between operations  14.9 us (1%)
    reduce_scatter x5, waiting for transfers between devices, scatter(): lax.psum_scatter(grad, ('fsdp', 'batch'), scatter_dimension=0, tiled=True)  600 us
    all_gather x4, waiting for transfers between devices, gather(): return lax.all_gather(piece, ('fsdp', 'batch'), axis=0, tiled=True)  248 us
    dot_general x8, matrix products, matmul(): return jnp.dot(left, right, preferred_element_type=F32)  57.5 us
    all_gather x5, waiting for transfers between devices, scatter(): return lax.all_gather(part, 'batch', axis=0, tiled=True).astype(F32)  57.1 us
    dot_general x8, matrix products, matmul_t(): return jnp.einsum('re,de->rd', left, right, preferred_element_type=F32)  49.9 us
    dot_general x8, matrix products, weight_grad(): jnp.einsum('rd,re->de', left, right, preferred_element_type=F32)  46.2 us
    psum x1, blocking collectives, on_device(): gg = lax.psum(jnp.stack([gg1, gg2, gg3]), ('batch', 'fsdp'))  37.4 us
  transfers between devices with their start and end apart: 14, of which 12 were waited for; matrix products, arithmetic and copies ran while one was open for 14% of the time, Pallas kernels for 4%

profile of v1, /device:TPU:0, one launch (start us, length us, event | category | flops | bytes accessed | tf_op | source)
XLA Modules:
  0.0 1231.7 jit_solution(4649599544242097879)
XLA Ops:
  15.7 13.6 %all_gather.30 = bf16[3,1024]{1,0:T(4,128)(2,1)S(1)} all-gather(bf16[3,256]{1,0:T(4,128)(2,1)S(1)} %pad_maximum_fusion.3), channel_id=1, replica_groups=mesh['batch'=8,'fsdp'=4] {'fsdp'}, dimensions={1}, use_global_device_ids=true | all-gather | bytes 7680 | tf_op jit(solution)/shard_map/all_gather | solution.py:329
  29.2 52.1 %all-gather.16.cloned.1.call-done = bf16[2816,1024]{1,0:T(8,128)(2,1)} async-done(((bf16[88,1024]{1,0:T(8,128)(2,1)}), bf16[2816,1024]{1,0:T(8,128)(2,1)}) %all-gather.16.cloned.1.call-update) | async-done | bytes 5767184 | tf_op jit(solution)/shard_map/all_gather | solution.py:292
  81.4 9.1 fusion.82
  90.5 70.7 %all-gather.10.cloned.1.call-done = bf16[1024,4096]{1,0:T(8,128)(2,1)} async-done(((bf16[32,4096]{1,0:T(8,128)(2,1)}), bf16[1024,4096]{1,0:T(8,128)(2,1)}) %all-gather.10.cloned.1.call-update) | async-done | bytes 8388624 | tf_op jit(solution)/shard_map/all_gather | solution.py:292
  161.3 8.4 fusion.20
  169.6 9.6 shard_map.314
  179.2 4.8 multiply_reduce_fusion.7
  184.0 56.8 %all-gather.12.cloned.1.call-done = bf16[1024,4096]{1,0:T(8,128)(2,1)} async-done(((bf16[32,4096]{1,0:T(8,128)(2,1)}), bf16[1024,4096]{1,0:T(8,128)(2,1)}) %all-gather.12.cloned.1.call-update) | async-done | bytes 8388624 | tf_op jit(solution)/shard_map/all_gather | solution.py:292
  240.8 4.9 fusion.52
  245.7 6.0 convolution_convert_fusion.3
  251.7 9.0 shard_map.315
  260.7 3.5 multiply_reduce_fusion.6
  265.8 68.0 %all-gather.14.cloned.1.call-done = bf16[1024,5632]{1,0:T(8,128)(2,1)} async-done(((bf16[32,5632]{1,0:T(8,128)(2,1)}), bf16[1024,5632]{1,0:T(8,128)(2,1)}) %all-gather.14.cloned.1.call-update) | async-done | bytes 11534352 | tf_op jit(solution)/shard_map/all_gather | solution.py:292
  333.8 8.1 fusion.14
  342.0 13.5 %fusion.6 = (bf16[576,2816]{1,0:T(8,128)(2,1)S(1)}, bf16[576,2816]{1,0:T(8,128)(2,1)}, bf16[576,2816]{1,0:T(8,128)(2,1)}) fusion(f32[576,2816]{1,0:T(8,128)} %fusion.14, f32[2816,576]{0,1:T(8,128)} %fusion.82, bf16[576,1024]{1,0:T(8,128)(2,1)S(1)} %multiply_convert_fusion.2, bf16[1024,5632]{1,0:T(8,128)(2,1)S(1)} %copy-done.23), kind=kOutput, calls=%fused_computation.12 | convolution fusion | flops 3364061184 | bytes 29655040 | tf_op jit(solution)/shard_map/dot_general | solution.py:268
  357.2 6.6 convolution_convert_fusion.2
  363.9 8.4 convolution_convert_fusion.1
  373.6 8.5 convolution_convert_fusion
  382.1 6.9 fusion.12
  389.1 6.1 multiply_reduce_fusion
  398.4 4.0 fusion.55
  402.4 13.7 %shard_map.316 = (bf16[4,144,1024]{2,1,0:T(8,128)(2,1)}, bf16[4,256,2048]{2,1,0:T(8,128)(2,1)}) custom-call(bf16[4,144,1024]{2,1,0:T(8,128)(2,1)} %bitcast.108, bf16[4,256,2048]{2,1,0:T(8,128)(2,1)} %bitcast.101, bf16[4,4,576,256]{3,2,1,0:T(8,128)(2,1)} %get-tuple-element.25.p_ref, bf16[4,144,1024]{2,1,0:T(8,128)(2,1)} %bitcast.114, ...), custom_call_target="tpu_custom_call" | custom-call | flops 12079595520 | bytes 16515072 | tf_op jit(solution)/shard_map/pallas_call | solution.py:229
  416.1 3.3 convolution_convert_fusion.5
  419.4 5.1 fusion.27
  424.6 4.1 pad_maximum_fusion.1
  428.7 11.8 copy.47
  441.8 4.2 multiply_reduce_fusion.1
  447.3 3.2 convolution_convert_fusion.6
  450.5 4.1 fusion.49
  454.6 11.9 shard_map.317
  466.5 9.2 bitcast_convert_fusion
  475.7 7.6 pad_maximum_fusion
  483.4 22.8 %reduce-scatter.10.cloned.1.call-done = bf16[32,2816]{1,0:T(8,128)(2,1)} async-done(((bf16[1024,2816]{1,0:T(8,128)(2,1)}), bf16[32,2816]{1,0:T(8,128)(2,1)}) %reduce-scatter.10.cloned.1.call-update) | async-done | bytes 180240 | tf_op jit(solution)/shard_map/reduce_scatter | solution.py:300
  506.3 141.8 %reduce-scatter.12.cloned.1.call-done = bf16[32,2816]{1,0:T(8,128)(2,1)} async-done(((bf16[1024,2816]{1,0:T(8,128)(2,1)}), bf16[32,2816]{1,0:T(8,128)(2,1)}) %reduce-scatter.12.cloned.1.call-update) | async-done | bytes 180240 | tf_op jit(solution)/shard_map/reduce_scatter | solution.py:300
  648.2 142.0 %reduce-scatter.14.cloned.1.call-done = bf16[88,1024]{1,0:T(8,128)(2,1)} async-done(((bf16[2816,1024]{1,0:T(8,128)(2,1)}), bf16[88,1024]{1,0:T(8,128)(2,1)}) %reduce-scatter.14.cloned.1.call-update) | async-done | bytes 180240 | tf_op jit(solution)/shard_map/reduce_scatter | solution.py:300
  790.2 146.8 %reduce-scatter.16.cloned.1.call-done = bf16[32,4096]{1,0:T(8,128)(2,1)} async-done(((bf16[1024,4096]{1,0:T(8,128)(2,1)}), bf16[32,4096]{1,0:T(8,128)(2,1)}) %reduce-scatter.16.cloned.1.call-update) | async-done | bytes 262160 | tf_op jit(solution)/shard_map/reduce_scatter | solution.py:300
  937.1 146.9 %reduce-scatter.8.cloned.1.call-done = bf16[32,4096]{1,0:T(8,128)(2,1)} async-done(((bf16[1024,4096]{1,0:T(8,128)(2,1)}), bf16[32,4096]{1,0:T(8,128)(2,1)}) %reduce-scatter.8.cloned.1.call-update) | async-done | bytes 262160 | tf_op jit(solution)/shard_map/reduce_scatter | solution.py:300
  1084.1 9.4 multiply_reduce_fusion.2
  1093.5 37.4 %psum.7 = f32[3,1024]{1,0:T(4,128)S(1)} all-reduce(f32[3,1024]{1,0:T(4,128)S(1)} %pad_maximum_fusion.2), channel_id=1, replica_groups=mesh['batch'=8,'fsdp'=4] {'batch','fsdp'}, use_global_device_ids=true, to_apply=%region_9.10 | all-reduce | flops 3072 | bytes 24576 | tf_op jit(solution)/shard_map/psum | solution.py:402
  1131.5 4.5 subtract_add_fusion
  1136.0 8.3 add_convert_fusion
  1144.3 6.1 fusion.23
  1156.7 4.8 all-gather.26.cloned.1.call-done
  1161.5 3.3 convert_element_type.140
  1164.8 26.5 %all-gather.20.cloned.1.call-done = bf16[256,4096]{1,0:T(8,128)(2,1)} async-done(((bf16[32,4096]{1,0:T(8,128)(2,1)}), bf16[256,4096]{1,0:T(8,128)(2,1)}) %all-gather.20.cloned.1.call-update) | async-done | bytes 2097168 | tf_op jit(solution)/shard_map/all_gather | solution.py:301
  1191.3 3.9 fusion.77
  1195.2 25.8 %all-gather.18.cloned.1.call-done = bf16[256,4096]{1,0:T(8,128)(2,1)} async-done(((bf16[32,4096]{1,0:T(8,128)(2,1)}), bf16[256,4096]{1,0:T(8,128)(2,1)}) %all-gather.18.cloned.1.call-update) | async-done | bytes 2097168 | tf_op jit(solution)/shard_map/all_gather | solution.py:301
  1221.0 3.7 fusion.78
  (131 shorter events, 26.0 us)
Async XLA Ops:
  7.2 238.5 %copy-start = (bf16[4,256,1024]{2,1,0:T(8,128)(2,1)S(1)}, bf16[4,256,1024]{2,1,0:T(8,128)(2,1)}, u32[]{:S(2)}) copy-start(bf16[4,256,1024]{2,1,0:T(8,128)(2,1)} %param.20) | copy-start | bytes 6291460
  7.2 3.7 copy-start.15
  7.2 3.7 copy-start.14
  7.2 74.1 %all-gather.16.cloned.1.call-start = ((), (), s32[]{:S(2)}) async-start(), calls=%async_computation.8 | async-start | bytes 5947392 | tf_op jit(solution)/shard_map/all_gather | solution.py:292
  9.1 152.2 %all-gather.10.cloned.1.call-start = ((), (), s32[]{:S(2)}) async-start(), calls=%async_computation.5 | async-start | bytes 8650752 | tf_op jit(solution)/shard_map/all_gather | solution.py:292
  10.8 229.9 %all-gather.12.cloned.1.call-start = ((), (), s32[]{:S(2)}) async-start(), calls=%async_computation.6 | async-start | bytes 8650752 | tf_op jit(solution)/shard_map/all_gather | solution.py:292
  12.5 2.0 copy-start.25
  12.5 2.1 copy-start.26
  12.5 2.1 copy-start.27
  12.5 2.1 copy-start.8
  12.5 2.5 copy-start.22
  12.5 321.3 %all-gather.14.cloned.1.call-start = ((), (), s32[]{:S(2)}) async-start(), calls=%async_computation.7 | async-start | bytes 11894784 | tf_op jit(solution)/shard_map/all_gather | solution.py:292
  14.5 491.7 %reduce-scatter.10.cloned.1.call-start = ((), (), s32[]{:S(2)}) async-start(), calls=%async_computation.12 | async-start | bytes 5947392 | tf_op jit(solution)/shard_map/reduce_scatter | solution.py:300
  15.0 146.2 %copy-start.16 = (f32[576]{0:T(1024)}, f32[576]{0:T(1024)S(1)}, u32[]{:S(2)}) copy-start(f32[576]{0:T(1024)S(1)} %rsqrt.38) | copy-start | bytes 6916
  29.2 132.0 %copy-start.18 = (f32[1,1024]{1,0:T(1,128)}, f32[1,1024]{1,0:T(1,128)S(1)}, u32[]{:S(2)}) copy-start(f32[1,1024]{1,0:T(1,128)S(1)} %get-tuple-element.68) | copy-start | bytes 12292
  240.8 4.9 copy-start.24
  251.7 9.0 copy-start.10
  264.1 1.4 copy-start.5
  333.8 8.1 copy-start.23
  355.5 1.7 copy-start.31
  363.8 284.3 %reduce-scatter.12.cloned.1.call-start = ((), (), s32[]{:S(2)}) async-start(), calls=%async_computation.14 | async-start | bytes 5947392 | tf_op jit(solution)/shard_map/reduce_scatter | solution.py:300
  372.3 417.9 %reduce-scatter.14.cloned.1.call-start = ((), (), s32[]{:S(2)}) async-start(), calls=%async_computation.16 | async-start | bytes 5947392 | tf_op jit(solution)/shard_map/reduce_scatter | solution.py:300
  382.0 555.0 %reduce-scatter.16.cloned.1.call-start = ((), (), s32[]{:S(2)}) async-start(), calls=%async_computation.18 | async-start | bytes 8650752 | tf_op jit(solution)/shard_map/reduce_scatter | solution.py:300
  382.1 7.0 copy-start.6
  382.1 7.0 copy-start.32
  395.2 1.3 copy-start.29
  396.5 1.9 copy-start.3
  402.4 13.7 %copy-start.11 = (f32[576,1024]{1,0:T(8,128)S(1)}, f32[576,1024]{1,0:T(8,128)}, u32[]{:S(2)}) copy-start(f32[576,1024]{1,0:T(8,128)} %get-tuple-element.70) | copy-start | bytes 7077892
  416.1 3.3 copy-start.33
  440.6 643.5 %reduce-scatter.8.cloned.1.call-start = ((), (), s32[]{:S(2)}) async-start(), calls=%async_computation.9 | async-start | bytes 8650752 | tf_op jit(solution)/shard_map/reduce_scatter | solution.py:300
  441.8 4.2 copy-start.4
  441.8 4.2 copy-start.12
  446.0 1.3 copy-start.28
  447.3 3.2 copy-start.2
  454.6 11.9 copy-start.9
  454.6 11.9 copy-start.19
  454.6 11.9 copy-start.21
  483.3 600.8 %copy-start.17 = (f32[576]{0:T(1024)S(1)}, f32[576]{0:T(1024)}, u32[]{:S(2)}) copy-start(f32[576]{0:T(1024)} %copy-done.16) | copy-start | bytes 6916
  483.4 667.0 %all-gather.22.cloned.1.call-start = ((), (), s32[]{:S(2)}) async-start(), calls=%async_computation.13 | async-start | bytes 1622016 | tf_op jit(solution)/shard_map/all_gather | solution.py:301
  506.2 647.3 %all-gather.24.cloned.1.call-start = ((), (), s32[]{:S(2)}) async-start(), calls=%async_computation.15 | async-start | bytes 1622016 | tf_op jit(solution)/shard_map/all_gather | solution.py:301
  648.1 513.3 %all-gather.26.cloned.1.call-start = ((), (), s32[]{:S(2)}) async-start(), calls=%async_computation.17 | async-start | bytes 1622016 | tf_op jit(solution)/shard_map/all_gather | solution.py:301
  790.2 401.1 %all-gather.20.cloned.1.call-start = ((), (), s32[]{:S(2)}) async-start(), calls=%async_computation.11 | async-start | bytes 2359296 | tf_op jit(solution)/shard_map/all_gather | solution.py:301
  937.1 283.9 %all-gather.18.cloned.1.call-start = ((), (), s32[]{:S(2)}) async-start(), calls=%async_computation.10 | async-start | bytes 2359296 | tf_op jit(solution)/shard_map/all_gather | solution.py:301
  1131.5 4.5 copy-start.7
  1131.5 12.8 %slice-start = ((s8[8388608]{0:T(1024)(128)(4,1)}), s8[4194304]{0:T(1024)(128)(4,1)S(1)}, s32[]{:S(2)}) async-start(s8[8388608]{0:T(1024)(128)(4,1)} %bitcast.98), calls=%async_computation.19 | async-start | bytes 8388608
  1136.0 8.3 slice-start.1
  1136.0 8.3 copy-start.34
  1191.3 33.4 %copy-start.1 = (bf16[4,256,1024]{2,1,0:T(8,128)(2,1)S(1)}, bf16[4,256,1024]{2,1,0:T(8,128)(2,1)}, u32[]{:S(2)}) copy-start(bf16[4,256,1024]{2,1,0:T(8,128)(2,1)} %param.20) | copy-start | bytes 6291460
  (3 other events, 3.3 us)
Sparse Core Ops, SparseCore 0:
  11.5 69.8 all-gather.15
  84.8 76.4 all-gather.9
  164.7 76.0 all-gather.11
  244.0 89.7 all-gather.13
  363.9 142.2 reduce-scatter.9
  508.4 139.7 reduce-scatter.11
  650.4 139.7 reduce-scatter.13
  792.5 144.5 reduce-scatter.15
  939.4 144.6 reduce-scatter.7
  1085.8 21.4 all-gather.21
  1109.2 25.4 all-gather.23
  1136.5 24.9 all-gather.25
  1163.4 27.8 all-gather.19
  1193.0 27.8 all-gather.17

commit v2 on v1

--- a/solution.py
+++ b/solution.py
@@ -120,7 +120,8 @@
     )(lengths, qkv)
 
 
-def self_backward_kernel(qkv_ref, p_ref, g_ref, d_ref):
+def self_backward_kernel(qkv_ref, p_ref, g_ref, *refs):
+    d_ref = refs[-1]
     width = g_ref.shape[2]
     for h in range(width // WIDE):
         c = h * WIDE
@@ -137,27 +138,26 @@
         d_ref[0, :, 2 * width + c : 2 * width + c + WIDE] = grad_v
 
 
-def self_backward(qkv, probs, grad):
+def self_backward(order, qkv, probs, grad):
     items, rows, width3 = qkv.shape
     width = width3 // 3
     quads = width // WIDE
-    return pl.pallas_call(
+    waits = order.take()
+    out = pl.pallas_call(
         self_backward_kernel,
         grid=(items,),
         in_specs=[
             pl.BlockSpec((1, rows, width3), lambda i: (i, 0, 0)),
             pl.BlockSpec((1, quads, QUAD * rows, rows), lambda i: (i, 0, 0, 0)),
             pl.BlockSpec((1, rows, width), lambda i: (i, 0, 0)),
-        ],
+        ]
+        + [pl.BlockSpec(memory_space=pl.ANY)] * len(waits),
         out_specs=pl.BlockSpec((1, rows, width3), lambda i: (i, 0, 0)),
         out_shape=jax.ShapeDtypeStruct((items, rows, width3), BF16),
         compiler_params=params(),
-        cost_estimate=pl.CostEstimate(
-            flops=20 * items * quads * QUAD * rows * 256 * 256,
-            bytes_accessed=2 * items * rows * (7 * width + 16 * rows),
-            transcendentals=0,
-        ),
-    )(qkv, probs, grad)
+        cost_estimate=cost(11.5),
+    )(qkv, probs, grad, *waits)
+    return order.after(out)
 
 
 def cross_forward_kernel(q_ref, kv_ref, m_ref, o_ref, p_ref):
@@ -204,7 +204,8 @@
     )(q, kv, mask)
 
 
-def cross_backward_kernel(q_ref, kv_ref, p_ref, g_ref, m_ref, dq_ref, dkv_ref):
+def cross_backward_kernel(q_ref, kv_ref, p_ref, g_ref, m_ref, *refs):
+    dq_ref, dkv_ref = refs[-2:]
     width = g_ref.shape[2]
     allowed = m_ref[0] > 0
     for h in range(width // WIDE):
@@ -222,11 +223,12 @@
         dkv_ref[0, :, width + c : width + c + WIDE] = grad_v
 
 
-def cross_backward(q, kv, probs, grad, mask):
+def cross_backward(order, q, kv, probs, grad, mask):
     items, rows, width = q.shape
     keys = kv.shape[1]
     quads = width // WIDE
-    return pl.pallas_call(
+    waits = order.take()
+    out = pl.pallas_call(
         cross_backward_kernel,
         grid=(items,),
         in_specs=[
@@ -235,7 +237,8 @@
             pl.BlockSpec((1, quads, QUAD * rows, keys), lambda i: (i, 0, 0, 0)),
             pl.BlockSpec((1, rows, width), lambda i: (i, 0, 0)),
             pl.BlockSpec((1, 1, keys), lambda i: (i, 0, 0)),
-        ],
+        ]
+        + [pl.BlockSpec(memory_space=pl.ANY)] * len(waits),
         out_specs=[
             pl.BlockSpec((1, rows, width), lambda i: (i, 0, 0)),
             pl.BlockSpec((1, keys, 2 * width), lambda i: (i, 0, 0)),
@@ -245,60 +248,749 @@
             jax.ShapeDtypeStruct((items, keys, 2 * width), BF16),
         ],
         compiler_params=params(),
-        cost_estimate=pl.CostEstimate(
-            flops=20 * items * quads * QUAD * rows * 256 * 256,
-            bytes_accessed=2 * items * rows * (10 * width + 16 * keys),
-            transcendentals=0,
-        ),
-    )(q, kv, probs, grad, mask)
+        cost_estimate=cost(13.5),
+    )(q, kv, probs, grad, mask, *waits)
+    order.after(out[0])
+    return out
 
 
 def factor_of(value):
     return lax.rsqrt(jnp.mean(value * value, axis=-1, keepdims=True) + EPSILON)
 
 
-def norm_back(value, factor, gain, grad):
-    scaled = gain * grad
-    along = jnp.mean(scaled * value, axis=-1, keepdims=True)
-    grad_value = factor * scaled - value * (factor * factor * factor * along)
-    return grad_value, jnp.sum(grad * value * factor, axis=0)
-
-
 def matmul(left, right):
     return jnp.dot(left, right, preferred_element_type=F32)
 
 
-def matmul_t(left, right):
-    return jnp.einsum("re,de->rd", left, right, preferred_element_type=F32)
-
-
-def weight_grad(left, right):
-    return jnp.einsum("rd,re->de", left, right, preferred_element_type=F32).astype(BF16)
-
-
-def gather(shard, spot):
-    rows = shard.shape[0] // 8
-    piece = lax.dynamic_slice_in_dim(shard, (spot % 8) * rows, rows, 0)
-    groups = lax.axis_size("batch") // 8
-    if groups > 1:
-        inner = lax.all_gather(
-            piece,
-            "batch",
-            axis=0,
-            tiled=True,
-            axis_index_groups=[[8 * g + j for j in range(8)] for g in range(groups)],
+AXES = {1: "core", 2: "x", 4: "y"}
+
+
+def swap(value, bit):
+    return lax.ppermute(value, AXES[bit], [(0, 1), (1, 0)])
+
+
+class Order:
+    def __init__(self):
+        self.waits = []
+
+    def take(self):
+        waits, self.waits = self.waits, []
+        return waits
+
+    def after(self, array):
+        self.waits.append(array)
+        return array
+
+
+def hold_kernel(*refs):
+    pass
+
+
+def hold(order, array):
+    whole = pl.BlockSpec(memory_space=pl.ANY)
+    waits = order.take()
+    out = pl.pallas_call(
+        hold_kernel,
+        in_specs=[whole] * (1 + len(waits)),
+        out_specs=whole,
+        out_shape=jax.ShapeDtypeStruct(array.shape, array.dtype),
+        input_output_aliases={0: 0},
+        compiler_params=pltpu.CompilerParams(vmem_limit_bytes=1024 * 1024),
+        cost_estimate=cost(0.5),
+    )(array, *waits)
+    return order.after(out)
+
+
+SHARE = 0.5
+
+
+def cost(micros):
+    return pl.CostEstimate(
+        flops=int(SHARE * micros * 1.15e9),
+        bytes_accessed=int(SHARE * micros * 3.6e6),
+        transcendentals=0,
+    )
+
+
+def put_split(value, flag, axis, give_ref, keep_ref):
+    half = value.shape[axis] // 2
+    low, high = (value[:half], value[half:]) if axis == 0 else (value[:, :half], value[:, half:])
+
+    @pl.when(flag == 0)
+    def _():
+        keep_ref[...] = low
+        give_ref[...] = high
+
+    @pl.when(flag > 0)
+    def _():
+        keep_ref[...] = high
+        give_ref[...] = low
+
+
+def product_kernel(jobs, has_add, axis, halves, flags, *refs):
+    outs = refs[-halves * 2 :] if has_add else refs[-1:]
+    add_ref = refs[sum(count + 1 for count, _, _ in jobs)]
+    at = 0
+    total = sum(steps for _, _, steps in jobs)
+    for count, start, steps in jobs:
+        lefts, right = refs[at : at + count], refs[at + count]
+        at += count + 1
+
+        def work(lefts=lefts, right=right, start=start):
+            left = jnp.concatenate([r[...] for r in lefts], axis=1)
+            value = right[0] if len(right.shape) == 3 else right[...]
+            out = dot(left, value, ((0,), (0,)))
+            if not has_add:
+                outs[0][...] = out.astype(BF16)
+                return
+            out = (out + add_ref[...].astype(F32)).astype(BF16)
+            if axis == 1:
+                put_split(out, flags[1], 1, *outs)
+                return
+            which = 2 * start // total if halves > 1 else 0
+            give, keep = outs[2 * which : 2 * which + 2]
+            for z in range(give.shape[0]):
+                part = out[128 * z : 128 * z + 128]
+                put_split(part, flags[1 + which], 0, give.at[z], keep.at[z])
+
+        if len(jobs) == 1:
+            work()
+        else:
+            step = pl.program_id(0)
+            pl.when((step >= start) & (step < start + steps))(work)
+
+
+def call_product(order, axis, grid, jobs, flags, specs, operands, out_specs, out_shapes):
+    waits = order.take()
+    has_add = len(out_shapes) > 1
+    out = pl.pallas_call(
+        functools.partial(product_kernel, jobs, has_add, axis, len(out_shapes) // 2),
+        grid_spec=pltpu.PrefetchScalarGridSpec(
+            num_scalar_prefetch=1,
+            grid=grid,
+            in_specs=specs + [pl.BlockSpec(memory_space=pl.ANY)] * len(waits),
+            out_specs=out_specs,
+        ),
+        out_shape=out_shapes,
+        compiler_params=params(),
+        cost_estimate=cost(3 + 2e-6 * sum(v.size for v in out_shapes)),
+    )(flags, *operands, *waits)
+    order.after(out[0])
+    return out
+
+
+def grad_rows(order, pairs, flags, add=None):
+    count = pairs[0][0].shape[1] // 256
+    total = sum(columns for _, _, _, columns in pairs)
+    tile = next(t for t in (1408, 1024) if all(c % t == 0 for _, _, _, c in pairs))
+    specs, operands, jobs, start = [], [], [], 0
+    for left, right, place, columns in pairs:
+        rows, steps = left.shape[0], columns // tile
+        specs += [
+            pl.BlockSpec((rows, 128), lambda j, f, z=z: (0, 2 * z + f[0])) for z in range(count)
+        ]
+        block = lambda j, f, start=start, steps=steps: jnp.clip(j - start, 0, steps - 1)
+        if right.ndim == 3:
+            specs.append(
+                pl.BlockSpec((1, rows, tile), lambda j, f, b=block, p=place: (p, 0, b(j, f)))
+            )
+        else:
+            specs.append(
+                pl.BlockSpec((rows, tile), lambda j, f, b=block, p=place: (0, p + b(j, f)))
+            )
+        operands += [left] * count + [right]
+        jobs.append((count, start, steps))
+        start += steps
+    block = pl.BlockSpec((count * 128, tile), lambda j, f: (0, j))
+    if add is None:
+        shapes, outs = [jax.ShapeDtypeStruct((count * 128, total), BF16)], [block]
+    else:
+        specs.append(block)
+        operands.append(add)
+        halves = flags.shape[0] - 1
+        shapes = [jax.ShapeDtypeStruct((count, 64, total // halves), BF16)] * (2 * halves)
+        outs, most = [], start // halves
+        for i in range(halves):
+            place = lambda j, f, i=i: (0, 0, jnp.clip(j - i * most, 0, most - 1))
+            outs += [pl.BlockSpec((count, 64, tile), place)] * 2
+    return call_product(order, 0, (start,), jobs, flags, specs, operands, outs, shapes)
+
+
+def grad_columns(order, left, right, flags, add=None):
+    rows, width = left.shape
+    half = right.shape[1] // 2
+    tile = next(t for t in (1408, 1024) if width % t == 0)
+    block = lambda columns: pl.BlockSpec((tile, columns), lambda j, f: (j, 0))
+    specs = [
+        pl.BlockSpec((rows, tile), lambda j, f: (0, j)),
+        pl.BlockSpec((rows, half), lambda j, f: (0, f[0])),
+    ]
+    operands = [left, right]
+    if add is None:
+        shapes, outs = [jax.ShapeDtypeStruct((width, half), BF16)], [block(half)]
+    else:
+        specs.append(block(half))
+        operands.append(add)
+        shapes = [jax.ShapeDtypeStruct((width, half // 2), BF16)] * 2
+        outs = [block(half // 2)] * 2
+    steps = width // tile
+    return call_product(
+        order, 1, (steps,), [(1, 0, steps)], flags, specs, operands, outs, shapes
+    )
+
+
+def land_kernel(count, axis, flags, *refs):
+    outs = refs[len(refs) - (2 * count if axis is not None else 1) :]
+    column = 0
+    for i in range(count):
+        total = refs[2 * i][...] + refs[2 * i + 1][...]
+        if axis is None:
+            columns = total.shape[-1]
+            outs[0][..., column : column + columns] = total
+            column += columns
+        elif axis == 1:
+            put_split(total, flags[i], 1, *outs[2 * i : 2 * i + 2])
+        else:
+            for z in range(total.shape[0]):
+                put_split(
+                    total[z], flags[i], 0, outs[2 * i].at[z], outs[2 * i + 1].at[z]
+                )
+
+
+def land_sums(order, pairs, flags, axis):
+    waits = order.take()
+    steps = 2
+    block = lambda shape: pl.BlockSpec(
+        (shape[0] // steps, *shape[1:]), lambda j, f: (j,) + (0,) * (len(shape) - 1)
+    )
+    specs, operands, shapes = [], [], []
+    for keep, got in pairs:
+        specs += [block(keep.shape)] * 2
+        operands += [keep, got]
+        shape = list(keep.shape)
+        if axis is not None:
+            shape[-2 if axis == 0 else -1] //= 2
+            shapes += [tuple(shape)] * 2
+    if axis is None:
+        total = sum(keep.shape[-1] for keep, _ in pairs)
+        shapes = [(*pairs[0][0].shape[:-1], total)]
+    out = pl.pallas_call(
+        functools.partial(land_kernel, len(pairs), axis),
+        grid_spec=pltpu.PrefetchScalarGridSpec(
+            num_scalar_prefetch=1,
+            grid=(steps,),
+            in_specs=specs + [pl.BlockSpec(memory_space=pl.ANY)] * len(waits),
+            out_specs=[block(shape) for shape in shapes],
+        ),
+        out_shape=[jax.ShapeDtypeStruct(shape, BF16) for shape in shapes],
+        compiler_params=params(),
+        cost_estimate=cost(1.5 + 1.7e-6 * sum(k.size for k, _ in pairs)),
+    )(jnp.stack(flags), *operands, *waits)
+    order.after(out[0])
+    return out
+
+
+def join_kernel(count, pieces, flags, *refs):
+    outs = refs[len(refs) - count * pieces :]
+    for i in range(count):
+        own, got = refs[2 * i], refs[2 * i + 1]
+        half, columns = own.shape[0], own.shape[1] // pieces
+        for k in range(pieces):
+            out = outs[i * pieces + k]
+            at = slice(k * columns, (k + 1) * columns)
+
+            def put(low, high, out=out, at=at, half=half):
+                out[:half] = low[:, at].astype(out.dtype)
+                out[half:] = high[:, at].astype(out.dtype)
+
+            pl.when(flags[i] == 0)(functools.partial(put, own, got))
+            pl.when(flags[i] > 0)(functools.partial(put, got, own))
+
+
+def land_joins(order, pairs, flags, pieces, kind):
+    waits = order.take()
+    whole = lambda shape: pl.BlockSpec(shape, lambda j, f: (0, 0))
+    specs, operands, shapes = [], [], []
+    for own, got in pairs:
+        specs += [whole(own.shape)] * 2
+        operands += [own, got]
+        shapes += [(2 * own.shape[0], own.shape[1] // pieces)] * pieces
+    out = pl.pallas_call(
+        functools.partial(join_kernel, len(pairs), pieces),
+        grid_spec=pltpu.PrefetchScalarGridSpec(
+            num_scalar_prefetch=1,
+            grid=(1,),
+            in_specs=specs + [pl.BlockSpec(memory_space=pl.ANY)] * len(waits),
+            out_specs=[whole(shape) for shape in shapes],
+        ),
+        out_shape=[jax.ShapeDtypeStruct(shape, kind) for shape in shapes],
+        compiler_params=params(),
+        cost_estimate=cost(2 + 1.5e-6 * sum(v.size for v, _ in pairs)),
+    )(jnp.stack(flags), *operands, *waits)
+    order.after(out[0])
+    return out
+
+
+def segment_kernel(steps, has_next, waits, *refs):
+    x_ref, w_ref, v_ref, b_ref, g_ref = refs[:5]
+    n_ref = refs[5] if has_next else None
+    refs = refs[5 + has_next + waits :]
+    if has_next:
+        d_ref, gg_ref, e_ref, o_ref, acc = refs
+    else:
+        d_ref, gg_ref, acc = refs
+    step = pl.program_id(0)
+    x = x_ref[0] if len(x_ref.shape) == 3 else x_ref[...]
+    partial = dot(x, w_ref[...], ((1,), (1,)))
+
+    @pl.when(step == 0)
+    def _():
+        acc[...] = partial
+
+    @pl.when(step > 0)
+    def _():
+        acc[...] += partial
+
+    @pl.when(step == steps - 1)
+    def _():
+        gain = g_ref[...]
+        rows, chunk = acc.shape[0], 144
+        gg_ref[...] = jnp.zeros_like(gg_ref)
+
+        @pl.loop(0, rows // chunk)
+        def _(i):
+            at = pl.ds(pl.multiple_of(i * chunk, chunk), chunk)
+            grad = acc[at, :]
+            value = v_ref[at, :].astype(F32)
+            factor = lax.rsqrt(jnp.mean(value * value, axis=-1, keepdims=True) + EPSILON)
+            scaled = gain * grad
+            along = jnp.mean(scaled * value, axis=-1, keepdims=True)
+            back = factor * scaled - value * (factor * factor * factor * along)
+            gg_ref[...] += jnp.sum(grad * value * factor, axis=0, keepdims=True)
+            total = b_ref[at, :].astype(F32) + back
+            d_ref[at, :] = total
+            if has_next:
+                e_ref[at, :] = total.astype(BF16)
+
+        if has_next:
+            o_ref[...] = dot(e_ref[...], n_ref[...], ((1,), (1,))).astype(BF16)
+
+
+def segment(order, x, w, column, tile, value, base, gain, after=None):
+    rows, width = value.shape
+    steps = x.shape[-1] * (x.shape[0] if x.ndim == 3 else 1) // tile
+    if x.ndim == 3:
+        per = x.shape[-1] // tile
+        x_spec = pl.BlockSpec((1, rows, tile), lambda k: (k // per, 0, k % per))
+    else:
+        x_spec = pl.BlockSpec((rows, tile), lambda k: (0, k))
+    whole = pl.BlockSpec((rows, width), lambda k: (0, 0))
+    line = pl.BlockSpec((1, width), lambda k: (0, 0))
+    specs = [x_spec, pl.BlockSpec((width, tile), lambda k: (0, k + column)), whole, whole, line]
+    operands = [x, w, value, base, gain.reshape(1, width)]
+    shapes = [
+        jax.ShapeDtypeStruct((rows, width), F32),
+        jax.ShapeDtypeStruct((1, width), F32),
+    ]
+    outs = [whole, line]
+    if after is not None:
+        matrix, at = after
+        specs.append(pl.BlockSpec((width, width), lambda k: (0, at)))
+        operands.append(matrix)
+        shapes += [jax.ShapeDtypeStruct((rows, width), BF16)] * 2
+        outs += [whole, whole]
+    waits = order.take()
+    out = pl.pallas_call(
+        functools.partial(segment_kernel, steps, after is not None, len(waits)),
+        grid=(steps,),
+        in_specs=specs + [pl.BlockSpec(memory_space=pl.ANY)] * len(waits),
+        out_specs=outs,
+        out_shape=shapes,
+        scratch_shapes=[pltpu.VMEM((rows, width), F32)],
+        compiler_params=params(),
+        cost_estimate=cost(5 + x.size * width / 2.6e8),
+    )(*operands, *waits)
+    order.after(out[1])
+    return out
+
+
+def mlp_kernel(a_ref, e_ref, wg_ref, wu_ref, wd_ref, i_ref, d_ref):
+    grad = dot(e_ref[...], wd_ref[...], ((1,), (1,)))
+    gate = dot(a_ref[...], wg_ref[...], ((1,), (0,)))
+    up = dot(a_ref[...], wu_ref[...], ((1,), (0,)))
+    slope, cubic = 0.7978845608028654, 0.044715
+    square = gate * gate
+    bend = jnp.tanh(slope * gate * (1.0 + cubic * square))
+    half = 0.5 * (1.0 + bend)
+    act = gate * half
+    turn = half + 0.5 * gate * (1.0 - bend * bend) * slope * (1.0 + 3.0 * cubic * square)
+    i_ref[...] = (act * up).astype(BF16)
+    d_ref[0] = (grad * up * turn).astype(BF16)
+    d_ref[1] = (grad * act).astype(BF16)
+
+
+def mlp(a3, e3, w_wide, w_down):
+    rows, width = a3.shape
+    hidden = w_down.shape[0]
+    tile = 256
+    count = hidden // tile
+    whole = pl.BlockSpec((rows, width), lambda j: (0, 0))
+    return pl.pallas_call(
+        mlp_kernel,
+        grid=(count,),
+        in_specs=[
+            whole,
+            whole,
+            pl.BlockSpec((width, tile), lambda j: (0, j)),
+            pl.BlockSpec((width, tile), lambda j: (0, count + j)),
+            pl.BlockSpec((tile, width), lambda j: (j, 0)),
+        ],
+        out_specs=[
+            pl.BlockSpec((rows, tile), lambda j: (0, j)),
+            pl.BlockSpec((2, rows, tile), lambda j: (0, 0, j)),
+        ],
+        out_shape=[
+            jax.ShapeDtypeStruct((rows, hidden), BF16),
+            jax.ShapeDtypeStruct((2, rows, hidden), BF16),
+        ],
+        compiler_params=params(),
+        cost_estimate=cost(20),
+    )(a3, e3, w_wide, w_wide, w_down)
+
+
+def forward_out_kernel(steps, waits, x_ref, w_ref, b_ref, *refs):
+    o_ref, acc = refs[waits:]
+    step = pl.program_id(0)
+    partial = dot(x_ref[...], w_ref[...], ((1,), (0,)))
+
+    @pl.when(step == 0)
+    def _():
+        acc[...] = partial + b_ref[...]
+
+    @pl.when(step > 0)
+    def _():
+        acc[...] += partial
+
+    @pl.when(step == steps - 1)
+    def _():
+        o_ref[...] = acc[...].astype(BF16)
+
+
+def forward_out(order, x, w, base):
+    rows, width = base.shape
+    tile = next(t for t in (1408, 1024) if w.shape[0] % t == 0)
+    steps = w.shape[0] // tile
+    whole = pl.BlockSpec((rows, width), lambda k: (0, 0))
+    waits = order.take()
+    out = pl.pallas_call(
+        functools.partial(forward_out_kernel, steps, len(waits)),
+        grid=(steps,),
+        in_specs=[
+            pl.BlockSpec((rows, tile), lambda k: (0, k)),
+            pl.BlockSpec((tile, width), lambda k: (k, 0)),
+            whole,
+        ]
+        + [pl.BlockSpec(memory_space=pl.ANY)] * len(waits),
+        out_specs=whole,
+        out_shape=jax.ShapeDtypeStruct((rows, width), BF16),
+        scratch_shapes=[pltpu.VMEM((rows, width), F32)],
+        compiler_params=params(),
+        cost_estimate=cost(8),
+    )(x, w, base, *waits)
+    return order.after(out)
+
+
+def back_product_kernel(waits, x_ref, w_ref, *refs):
+    refs[-1][...] = dot(x_ref[...], w_ref[...], ((1,), (1,)))
+
+
+def back_product(order, x, w):
+    rows, depth = x.shape
+    width = w.shape[0]
+    tile = 256
+    waits = order.take()
+    out = pl.pallas_call(
+        functools.partial(back_product_kernel, len(waits)),
+        grid=(width // tile,),
+        in_specs=[
+            pl.BlockSpec((rows, depth), lambda j: (0, 0)),
+            pl.BlockSpec((tile, depth), lambda j: (j, 0)),
+        ]
+        + [pl.BlockSpec(memory_space=pl.ANY)] * len(waits),
+        out_specs=pl.BlockSpec((rows, tile), lambda j: (0, j)),
+        out_shape=jax.ShapeDtypeStruct((rows, width), F32),
+        compiler_params=params(),
+        cost_estimate=cost(9),
+    )(x, w, *waits)
+    return order.after(out)
+
+
+def bit_of(spot, bit):
+    return (spot // bit) % 2
+
+
+class Sum:
+    def __init__(self, order, spot, axis, product, first, second):
+        self.order, self.axis, self.product = order, axis, product
+        self.first, self.second = first, second
+        self.bits = bit_of(spot, 1), bit_of(spot, first), bit_of(spot, second)
+        core, one, _ = self.bits
+        (give,) = product(jnp.stack([1 - core, one]))
+        self.flight = swap(give, 1)
+
+    def core(self):
+        core, one, _ = self.bits
+        give, self.keep = self.product(jnp.stack([core, one]), self.flight)
+        self.flight = swap(give, self.first)
+
+
+class Part:
+    def __init__(self, spot, first, second):
+        self.first, self.second, self.axis = first, second, 0
+        self.bits = bit_of(spot, 1), bit_of(spot, first), bit_of(spot, second)
+
+
+class Pair:
+    def __init__(self, order, spot, pairs):
+        self.product = functools.partial(grad_rows, order, pairs)
+        self.parts = [Part(spot, 2, 4), Part(spot, 4, 2)]
+        self.flags = [bit_of(spot, b) for b in (1, 2, 4)]
+        core, one, two = self.flags
+        (give,) = self.product(jnp.stack([1 - core, one, two]))
+        self.flight = swap(give, 1)
+
+    def core(self):
+        core, one, two = self.flags
+        out = self.product(jnp.stack([core, one, two]), self.flight)
+        for i, part in enumerate(self.parts):
+            part.keep = out[2 * i + 1]
+            part.flight = swap(out[2 * i], part.first)
+        return self.parts
+
+
+def region(axis, first, cross):
+    return (first, cross) if axis == 0 else (cross, first)
+
+
+def either(flag, put, one, two):
+    pl.when(flag == 0)(lambda: put(one, two))
+    pl.when(flag > 0)(lambda: put(two, one))
+
+
+def cut_kernel(axis, z_ref, *refs):
+    a_ref, b_ref = refs[-2:]
+    half = z_ref.shape[2 - axis] // 2
+    a_ref[0] = z_ref.at[0][region(axis, slice(None), slice(0, half))]
+    b_ref[0] = z_ref.at[0][region(axis, slice(None), slice(half, None))]
+
+
+def pairs_kernel(axis, flags, *refs):
+    ins, outs = refs[:4], refs[-2:]
+    for i in range(2):
+        size = ins[2 * i].shape[1 + axis]
+
+        def put(low, high, out=outs[i], size=size):
+            out.at[0][region(axis, slice(0, size), slice(None))] = low[0]
+            out.at[0][region(axis, slice(size, None), slice(None))] = high[0]
+
+        either(flags[i], put, ins[2 * i], ins[2 * i + 1])
+
+
+def quads_kernel(axis, flags, *refs):
+    a_own, a_got, b_own, b_got = refs[:4]
+    out = refs[-1].at[0]
+    two, half = a_own.shape[1 + axis], a_own.shape[2 - axis]
+    n = two // 2
+
+    def put_a(low, high):
+        out[region(axis, slice(0, two), slice(0, half))] = low[0]
+        out[region(axis, slice(two, None), slice(0, half))] = high[0]
+
+    def put_b(low, high):
+        for y in range(2):
+            for x, ref in enumerate((low, high)):
+                at = (2 * y + x) * n
+                out[region(axis, slice(at, at + n), slice(half, None))] = ref.at[0][
+                    region(axis, slice(y * n, y * n + n), slice(None))
+                ]
+
+    either(flags[1], put_a, a_own, a_got)
+    either(flags[0], put_b, b_own, b_got)
+
+
+def cores_kernel(axis, flags, own_ref, got_ref, *refs):
+    out = refs[-1].at[0]
+    size = own_ref.shape[1 + axis]
+
+    def put(low, high):
+        out[region(axis, slice(0, size), slice(None))] = low[0]
+        out[region(axis, slice(size, None), slice(None))] = high[0]
+
+    either(flags[2], put, own_ref, got_ref)
+
+
+def by_shard(order, kernel, axis, flags, operands, shapes):
+    waits = order.take()
+    block = lambda shape: pl.BlockSpec((1, *shape[1:]), lambda j, *f: (j, 0, 0))
+    out = pl.pallas_call(
+        functools.partial(kernel, axis),
+        grid_spec=pltpu.PrefetchScalarGridSpec(
+            num_scalar_prefetch=len(flags),
+            grid=(operands[0].shape[0],),
+            in_specs=[block(v.shape) for v in operands]
+            + [pl.BlockSpec(memory_space=pl.ANY)] * len(waits),
+            out_specs=[block(shape) for shape in shapes],
+        ),
+        out_shape=[jax.ShapeDtypeStruct(shape, BF16) for shape in shapes],
+        compiler_params=params(),
+        cost_estimate=cost(2.5 + 1.1e-6 * sum(v.size for v in operands)),
+    )(*flags, *operands, *waits)
+    order.after(out[0])
+    return out
+
+
+class Gather:
+    def __init__(self, order, spot, shard, axis):
+        self.order, self.axis = order, axis
+        self.flags = [jnp.stack([bit_of(spot, b) for b in (2, 4, 1)])]
+        size = shard.shape[axis] // 8
+        seat = 4 * bit_of(spot, 1) + 2 * bit_of(spot, 4) + bit_of(spot, 2)
+        piece = lax.dynamic_slice_in_dim(shard, seat * size, size, axis)
+        self.value = lax.all_gather(piece, "fsdp", axis=0)
+
+    def scaled(self, shape, along, across):
+        shape = list(shape)
+        shape[1 + self.axis] = shape[1 + self.axis] * along
+        shape[2 - self.axis] = shape[2 - self.axis] * across // 2
+        return tuple(shape)
+
+    def run(self, kernel, flags, operands, shapes):
+        return by_shard(self.order, kernel, self.axis, flags, operands, shapes)
+
+    def one(self):
+        shape = self.scaled(self.value.shape, 1, 1)
+        self.a, self.b = self.run(cut_kernel, [], [self.value], [shape] * 2)
+        self.got = swap(self.a, 2), swap(self.b, 4)
+
+    def two(self):
+        shape = self.scaled(self.a.shape, 2, 2)
+        self.a, self.b = self.run(
+            pairs_kernel, self.flags, [self.a, self.got[0], self.b, self.got[1]], [shape] * 2
         )
-        return lax.all_gather(inner, "fsdp", axis=0, tiled=True)
-    return lax.all_gather(piece, ("fsdp", "batch"), axis=0, tiled=True)
-
-
-def scatter(grad):
-    batch = lax.axis_size("batch")
-    if batch > 8:
-        part = lax.psum_scatter(grad, "fsdp", scatter_dimension=0, tiled=True)
-        return lax.psum(part, "batch").astype(F32)
-    part = lax.psum_scatter(grad, ("fsdp", "batch"), scatter_dimension=0, tiled=True)
-    return lax.all_gather(part, "batch", axis=0, tiled=True).astype(F32)
+        self.got = swap(self.a, 4), swap(self.b, 2)
+
+    def three(self):
+        shape = self.scaled(self.a.shape, 2, 4)
+        (self.half,) = self.run(
+            quads_kernel, self.flags, [self.a, self.got[0], self.b, self.got[1]], [shape]
+        )
+        self.got = swap(self.half, 1)
+
+    def four(self):
+        shape = self.scaled(self.half.shape, 2, 2)
+        (whole,) = self.run(cores_kernel, self.flags, [self.half, self.got], [shape])
+        return whole.reshape(-1, whole.shape[-1])
+
+
+def land_first(order, *sums):
+    out = land_sums(
+        order, [(s.keep, s.flight) for s in sums], [s.bits[2] for s in sums], sums[0].axis
+    )
+    for i, s in enumerate(sums):
+        s.keep = out[2 * i + 1]
+        s.flight = swap(out[2 * i], s.second)
+
+
+def land_second(order, *sums):
+    (out,) = land_sums(
+        order, [(s.keep, s.flight) for s in sums], [s.bits[2] for s in sums], None
+    )
+    return out.reshape(-1, out.shape[-1])
+
+
+class Spread:
+    def __init__(self, order, spot, values):
+        self.order, self.spot = order, spot
+        self.values = values
+        self.bits = [(4, 2), (2, 4), (1, 1)]
+        self.send()
+
+    def send(self):
+        self.flights = [swap(v, b) for v, b in zip(self.values, self.bits[0])]
+
+    def land(self):
+        flags = [bit_of(self.spot, b) for b in self.bits.pop(0)]
+        pairs = list(zip(self.values, self.flights))
+        last = not self.bits
+        self.values = land_joins(
+            self.order, pairs, flags, 2 if last else 1, F32 if last else BF16
+        )
+        if not last:
+            self.send()
+
+
+def unpack_rows_kernel(v_ref, *refs):
+    gate_ref, up_ref = refs[-2:]
+    columns = gate_ref.shape[1]
+    gate_ref[...] = v_ref[0, :, :columns].astype(F32)
+    up_ref[...] = v_ref[0, :, columns:].astype(F32)
+
+
+def unpack_rows(order, value):
+    count, n, both = value.shape
+    c = both // 2
+    waits = order.take()
+    out = pl.pallas_call(
+        unpack_rows_kernel,
+        grid=(count,),
+        in_specs=[pl.BlockSpec((1, n, both), lambda j: (j, 0, 0))]
+        + [pl.BlockSpec(memory_space=pl.ANY)] * len(waits),
+        out_specs=[
+            pl.BlockSpec((n, c), lambda j: (4 * (j % 2) + 2 * (j // 2 % 2) + j // 4, 0)),
+            pl.BlockSpec((n, c), lambda j: (4 * (j % 2) + j // 2, 0)),
+        ],
+        out_shape=[jax.ShapeDtypeStruct((count * n, c), F32)] * 2,
+        compiler_params=params(),
+        cost_estimate=cost(6),
+    )(value, *waits)
+    order.after(out[0])
+    return out
+
+
+def unpack_columns_kernel(v_ref, *refs):
+    out_ref = refs[-1]
+    out_ref[...] = v_ref[0, : out_ref.shape[0], :].astype(F32)
+
+
+def unpack_columns(order, value, n):
+    count, held, c = value.shape
+    waits = order.take()
+    out = pl.pallas_call(
+        unpack_columns_kernel,
+        grid=(count,),
+        in_specs=[pl.BlockSpec((1, held, c), lambda j: (j, 0, 0))]
+        + [pl.BlockSpec(memory_space=pl.ANY)] * len(waits),
+        out_specs=pl.BlockSpec((n, c), lambda j: (0, 4 * (j % 2) + 2 * (j // 2 % 2) + j // 4)),
+        out_shape=jax.ShapeDtypeStruct((n, count * c), F32),
+        compiler_params=params(),
+        cost_estimate=cost(6),
+    )(value, *waits)
+    return order.after(out)
+
+
+def from_group(value):
+    return lax.all_gather(value, ("y", "x", "core"), axis=0)
+
+
+def over_groups(value):
+    value = lax.psum_scatter(value, "fsdp", scatter_dimension=0, tiled=True)
+    size = lax.axis_size("group")
+    ring = [(i, (i + 1) % size) for i in range(size)]
+    total = step = value
+    for _ in range(size - 1):
+        step = lax.ppermute(step, "group", ring)
+        total = total + step
+    return total
 
 
 def on_device(
@@ -324,99 +1016,152 @@
 ):
     items, rows, width = text.shape
     keys = memory.shape[1]
-    spot = lax.axis_index("batch")
+    spot = 4 * lax.axis_index("y") + 2 * lax.axis_index("x") + lax.axis_index("core")
 
     gains = lax.all_gather(jnp.stack([self_gain, cross_gain, mlp_gain]), "fsdp", axis=1, tiled=True)
     gains = gains.astype(F32)
-    w_self = gather(
-        jnp.concatenate([self_query, self_key, self_value, self_output], axis=1), spot
-    )
-    w_cross = gather(
-        jnp.concatenate([cross_key, cross_value, cross_query, cross_output], axis=1), spot
-    )
-    w_down = gather(mlp_down, spot)
-    w_wide = gather(jnp.concatenate([mlp_gate, mlp_up], axis=1), spot)
-    w_qkv, w_so = w_self[:, : 3 * width], w_self[:, 3 * width :]
-    w_kv = w_cross[:, : 2 * width]
-    w_cq, w_co = w_cross[:, 2 * width : 3 * width], w_cross[:, 3 * width :]
-    hidden = w_down.shape[0]
+    order = Order()
+    gather = lambda shard, axis=0: Gather(order, spot, shard, axis)
+    join = lambda *parts: jnp.concatenate(parts, axis=1)
+    g_down = gather(mlp_down, 1)
+    g_self = gather(join(self_query, self_key, self_value, self_output))
+    g_cross = gather(join(cross_key, cross_value, cross_query, cross_output))
+    g_wide = gather(join(mlp_gate, mlp_up))
+    hidden = mlp_gate.shape[1]
 
     x = text.reshape(-1, width).astype(F32)
     flat_memory = memory.reshape(-1, width)
     e3 = grad_out.reshape(-1, width)
     mask = memory_mask[:, None, :]
 
+    g_down.one()
+    g_down.two()
+    g_self.one()
+    g_down.three()
+    g_self.two()
+    w_down = g_down.four()
+    g_cross.one()
+    g_self.three()
+    g_cross.two()
+    w_self = g_self.four()
+    w_qkv, w_so = w_self[:, : 3 * width], w_self[:, 3 * width :]
     c1 = factor_of(x)
     a1 = (x * c1 * gains[0]).astype(BF16)
     qkv = matmul(a1, w_qkv).astype(BF16).reshape(items, rows, 3 * width)
     o1, p1 = self_forward(qkv, text_lengths)
-    o1 = o1.reshape(-1, width)
+    o1 = order.after(o1).reshape(-1, width)
+    g_wide.one()
+    g_cross.three()
+    g_wide.two()
     h1 = x + matmul(o1, w_so)
     c2 = factor_of(h1)
     a2 = (h1 * c2 * gains[1]).astype(BF16)
+    order.after(a2)
+    w_cross = g_cross.four()
+    w_kv = w_cross[:, : 2 * width]
+    w_cq, w_co = w_cross[:, 2 * width : 3 * width], w_cross[:, 3 * width :]
     kv = matmul(flat_memory, w_kv).astype(BF16).reshape(items, keys, 2 * width)
     q2 = matmul(a2, w_cq).astype(BF16).reshape(items, rows, width)
     o2, p2 = cross_forward(q2, kv, mask)
-    o2 = o2.reshape(-1, width)
+    o2 = order.after(o2).reshape(-1, width)
+    g_wide.three()
     h2 = h1 + matmul(o2, w_co)
     c3 = factor_of(h2)
     a3 = (h2 * c3 * gains[2]).astype(BF16)
-    d_inner = matmul_t(e3, w_down)
-    gate = matmul(a3, w_wide[:, :hidden])
-    up = matmul(a3, w_wide[:, hidden:])
-    act, pull = jax.vjp(lambda g, u: jax.nn.gelu(g, approximate=True) * u, gate, up)
-    inner = act.astype(BF16)
-    d_gate, d_up = pull(d_inner)
-    d_gate, d_up = d_gate.astype(BF16), d_up.astype(BF16)
-    g_down = scatter(weight_grad(inner, e3))
-    g_gate = scatter(weight_grad(a3, d_gate))
-    g_up = scatter(weight_grad(a3, d_up))
-    block_out = (h2 + matmul(inner, w_down)).astype(BF16)
-
-    d_a3 = matmul_t(d_gate, w_wide[:, :hidden]) + matmul_t(d_up, w_wide[:, hidden:])
-    back, gg3 = norm_back(h2, c3, gains[2], d_a3)
-    d_h2 = e3.astype(F32) + back
-    e2 = d_h2.astype(BF16)
-    g_co = weight_grad(o2, e2)
-    d_o2 = matmul_t(e2, w_co).astype(BF16).reshape(items, rows, width)
-    d_q2, d_kv = cross_backward(q2, kv, p2, d_o2, mask)
+    order.after(a3)
+    w_wide = g_wide.four()
+    inner, d_wide = mlp(a3, e3, w_wide, w_down)
+    order.take()
+
+    sum_of = lambda first, second, pairs: Sum(
+        order, spot, 0, functools.partial(grad_rows, order, pairs), first, second
+    )
+    s_gate = sum_of(2, 4, [(a3, d_wide, 0, hidden)])
+    s_up = sum_of(4, 2, [(a3, d_wide, 1, hidden)])
+    s_down = Sum(order, spot, 1, functools.partial(grad_columns, order, inner, e3), 2, 4)
+    s_gate.core()
+    s_up.core()
+    d_h2, gg3, e2, d_o2 = segment(
+        order, d_wide, w_wide, 0, hidden // 2, h2, e3, gains[2], (w_cross, 3)
+    )
+    s_down.core()
+    d_q2, d_kv = cross_backward(order, q2, kv, p2, d_o2.reshape(text.shape), mask)
     d_q2 = d_q2.reshape(-1, width)
     d_kv = d_kv.reshape(-1, 2 * width)
-    g_cq = weight_grad(a2, d_q2)
-    g_kv = weight_grad(flat_memory, d_kv)
-    g_cross = scatter(jnp.concatenate([g_kv, g_cq, g_co], axis=1))
-    grad_memory = matmul_t(d_kv, w_kv)
-    d_a2 = matmul_t(d_q2, w_cq)
-    back, gg2 = norm_back(h1, c2, gains[1], d_a2)
-    d_h1 = d_h2 + back
-    e1 = d_h1.astype(BF16)
-    g_so = weight_grad(o1, e1)
-    d_o1 = matmul_t(e1, w_so).astype(BF16).reshape(items, rows, width)
-    d_qkv = self_backward(qkv, p1, d_o1).reshape(-1, 3 * width)
-    g_qkv = weight_grad(a1, d_qkv)
-    g_self = scatter(jnp.concatenate([g_qkv, g_so], axis=1))
-    d_a1 = matmul_t(d_qkv, w_qkv)
-    back, gg1 = norm_back(x, c1, gains[0], d_a1)
-    grad_text = d_h1 + back
-
-    gg = lax.psum(jnp.stack([gg1, gg2, gg3]), ("batch", "fsdp"))
-    own = lax.axis_index("fsdp") * self_gain.shape[0]
-    gg = lax.dynamic_slice_in_dim(gg, own, self_gain.shape[0], 1)
-    cut = lambda g, j: g[:, j * width : (j + 1) * width]
+    land_first(order, s_gate, s_up)
+    s_cross = Pair(
+        order,
+        spot,
+        [
+            (flat_memory, d_kv, 0, 2 * width),
+            (a2, d_q2, 0, width),
+            (o2, e2, 0, width),
+        ],
+    )
+    d_h1, gg2, e1, d_o1 = segment(
+        order, d_q2, w_cross, 4, width // 2, h1, d_h2, gains[1], (w_self, 3)
+    )
+    z_wide = over_groups(land_second(order, s_gate, s_up))
+    land_first(order, s_down)
+    cross = s_cross.core()
+    d_qkv = self_backward(order, qkv, p1, d_o1.reshape(text.shape)).reshape(-1, 3 * width)
+    z_down = over_groups(land_second(order, s_down))
+    s_self = Pair(
+        order,
+        spot,
+        [
+            (a1, d_qkv, 0, 2 * width),
+            (a1, d_qkv, 2, width),
+            (o1, e1, 0, width),
+        ],
+    )
+    land_first(order, *cross)
+    z_wide = hold(order, z_wide)
+    all_wide = from_group(z_wide)
+    both = s_self.core()
+    grad_text, gg1 = segment(order, d_qkv, w_self, 0, width, x, d_h1, gains[0])
+    lines = jnp.concatenate([gg1, gg2, gg3]).astype(BF16).reshape(-1, width // 8)
+    z_down = hold(order, jnp.concatenate([z_down, jnp.pad(lines, ((0, 8), (0, 0)))]))
+    all_down = from_group(z_down)
+    z_cross = over_groups(land_second(order, *cross))
+    land_first(order, *both)
+    grad_memory = back_product(order, d_kv, w_cross)
+    g_gate, g_up = unpack_rows(order, all_wide)
+    block_out = forward_out(order, inner, w_down, h2)
+    g_down = unpack_columns(order, all_down, mlp_down.shape[0])
+    lines = jnp.sum(all_down[:, mlp_down.shape[0] : -8].astype(F32), axis=0)
+    shards, own = lax.axis_size("fsdp"), self_gain.shape[0]
+    lines = lines.reshape(3, shards, own).transpose(1, 0, 2).reshape(shards, -1)
+    lines = jnp.pad(lines, ((0, 0), (0, 32 * 128 - 3 * own))).astype(BF16).reshape(-1, 128)
+    z_self = over_groups(jnp.concatenate([land_second(order, *both), lines], axis=1))
+    z_cross = hold(order, z_cross)
+    t_cross = Spread(order, spot, [z_cross[:, : 2 * width], z_cross[:, 2 * width :]])
+    t_cross.land()
+    t_cross.land()
+    t_cross.land()
+    g_ck, g_cv, g_cq, g_co = t_cross.values
+    z_self = hold(order, z_self)
+    t_self = Spread(order, spot, [z_self[:, : 2 * width], z_self[:, 2 * width : 4 * width]])
+    gg = z_self[:, 4 * width :].reshape(-1)[: 3 * own].reshape(3, own).astype(F32)
+    t_self.land()
+    t_self.land()
+    t_self.land()
+    g_sq, g_sk, g_sv, g_so = t_self.values
+
     return (
         block_out.reshape(text.shape),
         grad_text.reshape(text.shape),
         grad_memory.reshape(memory.shape),
         gg[0],
-        cut(g_self, 0),
-        cut(g_self, 1),
-        cut(g_self, 2),
-        cut(g_self, 3),
+        g_sq,
+        g_sk,
+        g_sv,
+        g_so,
         gg[1],
-        cut(g_cross, 2),
-        cut(g_cross, 0),
-        cut(g_cross, 1),
-        cut(g_cross, 3),
+        g_cq,
+        g_ck,
+        g_cv,
+        g_co,
         gg[2],
         g_gate,
         g_up,
@@ -425,13 +1170,19 @@
 
 
 def solution(mesh):
-    rows = P(("batch", "fsdp"), None, None)
+    shape = mesh.devices.shape
+    mesh = jax.sharding.Mesh(
+        mesh.devices.reshape(shape[0] // 8, 2, 2, 2, shape[1]),
+        ("group", "y", "x", "core", "fsdp"),
+    )
+    every = ("group", "y", "x", "core", "fsdp")
+    rows = P(every, None, None)
     gain, weight = P("fsdp"), P("fsdp", None)
     weights = (gain, weight, weight, weight, weight) * 2 + (gain, weight, weight, weight)
     return jax.shard_map(
         on_device,
         mesh=mesh,
-        in_specs=(rows, rows, P(("batch", "fsdp")), P(("batch", "fsdp"), None), rows) + weights,
+        in_specs=(rows, rows, P(every), P(every, None), rows) + weights,
         out_specs=(rows, rows, rows) + weights,
         check_vma=False,
     )

time: 1240 us -> 695 us (0.56)
  waiting for transfers between devices: 905 us -> 170 us
  Pallas kernels: 44.2 us -> 346 us
  matrix products: 154 us -> 27.2 us
  starting transfers between devices: 0.57 us -> 41.7 us
  blocking collectives: 50.9 us -> 38.1 us
  other arithmetic: 32.6 us -> 20.1 us
    reduce_scatter x5 -> x4, waiting for transfers between devices: 600 us -> 0.04 us  [over_groups(): value = lax.psum_scatter(value, 'fsdp', scatter_dimension=0, tiled=True)]
    all_gather x9 -> x5, waiting for transfers between devices: 305 us -> 2.27 us  [the longest x3 2.27 us: __init__(): self.value = lax.all_gather(piece, 'fsdp', axis=0)]
    pallas_call x0 -> x52, Pallas kernels: none -> 302 us  [the longest x16 85.6 us: by_shard(): pl.pallas_call(functools.partial(kernel, axis), grid_spec=pltpu.PrefetchS...]
    ppermute x0 -> x51, waiting for transfers between devices: none -> 167 us  [swap(): return lax.ppermute(value, AXES[bit], [(0, 1), (1, 0)])]
    dot_general x16 -> x0, matrix products: 96.1 us -> none  [the longest x8 49.9 us: matmul_t(): return jnp.einsum('re,de->rd', left, right, preferred_element_type=F32)]
    ppermute x0 -> x51, starting transfers between devices: none -> 41.4 us  [swap(): return lax.ppermute(value, AXES[bit], [(0, 1), (1, 0)])]
    psum x1 -> x0, blocking collectives: 37.4 us -> none  [on_device(): gg = lax.psum(jnp.stack([gg1, gg2, gg3]), ('batch', 'fsdp'))]
    dot_general x8 -> x5, matrix products: 57.5 us -> 27.2 us  [matmul(): return jnp.dot(left, right, preferred_element_type=F32)]
  transfers between devices with their start and end apart: 14 -> 60, of which waited for: 12 -> 31; matrix products, arithmetic and copies ran while one was open for 14% -> 7% of each run, Pallas kernels for 4% -> 38%
where the time goes in v2:
time: 695 us; the launch traced here: 690 us
  Pallas kernels  346 us (50%)
  waiting for transfers between devices  170 us (24%)
  starting transfers between devices  41.7 us (6%)
  blocking collectives  38.1 us (5%)
  local copies, waits for them, and re-layouts  32.2 us (5%)
  matrix products  27.2 us (4%)
  other arithmetic  20.1 us (3%)
  between operations  14.9 us (2%)
    ppermute x51, waiting for transfers between devices, swap(): return lax.ppermute(value, AXES[bit], [(0, 1), (1, 0)])  167 us
    pallas_call x16, Pallas kernels, by_shard(): pl.pallas_call(functools.partial(kernel, axis), grid_spec=pltpu.PrefetchS...  85.6 us
    pallas_call x10, Pallas kernels, call_product(): pl.pallas_call(functools.partial(product_kernel, jobs, has_add, axis, len...  79 us
    ppermute x51, starting transfers between devices, swap(): return lax.ppermute(value, AXES[bit], [(0, 1), (1, 0)])  41.4 us
    pallas_call x3, Pallas kernels, segment(): pl.pallas_call(functools.partial(segment_kernel, steps, after is not None...  40.1 us
    unnamed x178, local copies, waits for them, and re-layouts  30.8 us
    pallas_call x8, Pallas kernels, land_sums(): pl.pallas_call(functools.partial(land_kernel, len(pairs), axis), grid_spe...  27.3 us
    dot_general x5, matrix products, matmul(): return jnp.dot(left, right, preferred_element_type=F32)  27.2 us
  transfers between devices with their start and end apart: 60, of which 31 were waited for; matrix products, arithmetic and copies ran while one was open for 7% of the time, Pallas kernels for 38%

profile of v2, /device:TPU:0, one launch (start us, length us, event | category | flops | bytes accessed | tf_op | source)
XLA Modules:
  0.0 689.7 jit_solution(12566564680089020010)
XLA Ops:
  9.2 25.5 %all-gather.1 = bf16[2816,128]{1,0:T(8,128)(2,1)} all-gather(bf16[704,128]{1,0:T(8,128)(2,1)S(1)} %constant_dynamic-slice_fusion), channel_id=3, replica_groups=mesh['group'=1,'y'=2,'x'=2,'core'=2,'fsdp'=4] {'fsdp'}, dimensions={0}, use_global_device_ids=true | all-gather | bytes 901120 | tf_op jit(solution)/shard_map/all_gather | solution.py:859
  57.8 7.0 %collective-permute-done.4.refs_1_ = bf16[4,352,256]{2,1,0:T(8,128)(2,1)S(1)} collective-permute-done((bf16[4,352,256]{2,1,0:T(8,128)(2,1)}, bf16[4,352,256]{2,1,0:T(8,128)(2,1)S(1)}, u32[]{:S(2)}, u32[]{:S(2)}) %collective-permute-start.4) | collective-permute-done | bytes 720928 | tf_op jit(solution)/shard_map/ppermute | solution.py:269
  67.0 5.1 shard_map.317.refs_4_.own_ref
  74.5 11.9 %collective-permute-done.2.refs_1_ = bf16[4,32,2048]{2,1,0:T(8,128)(2,1)S(1)} collective-permute-done((bf16[4,32,2048]{2,1,0:T(8,128)(2,1)S(1)}, bf16[4,32,2048]{2,1,0:T(8,128)(2,1)S(1)}, u32[]{:S(2)}, u32[]{:S(2)}) %collective-permute-start.2) | collective-permute-done | bytes 524320 | tf_op jit(solution)/shard_map/ppermute | solution.py:269
  88.2 4.5 shard_map.318
  94.2 6.3 shard_map.319.refs_0_
  106.1 11.5 %collective-permute-done.6.refs_1_ = bf16[4,64,2048]{2,1,0:T(8,128)(2,1)S(1)} collective-permute-done((bf16[4,64,2048]{2,1,0:T(8,128)(2,1)}, bf16[4,64,2048]{2,1,0:T(8,128)(2,1)S(1)}, u32[]{:S(2)}, u32[]{:S(2)}) %collective-permute-start.6) | collective-permute-done | bytes 1048608 | tf_op jit(solution)/shard_map/ppermute | solution.py:269
  118.9 5.5 shard_map.321.refs_4_.own_ref
  128.7 12.6 %all_gather.39 = bf16[3,1024]{1,0:T(4,128)(2,1)S(1)} all-gather(bf16[3,256]{1,0:T(4,128)(2,1)S(1)} %pad_maximum_fusion.2), channel_id=1, replica_groups=mesh['group'=1,'y'=2,'x'=2,'core'=2,'fsdp'=4] {'fsdp'}, dimensions={1}, use_global_device_ids=true | all-gather | bytes 7680 | tf_op jit(solution)/shard_map/all_gather | solution.py:1021
  143.1 4.5 shard_map.322
  149.2 7.7 %shard_map.323.refs_0_ = bf16[4,256,4096]{2,1,0:T(8,128)(2,1)} custom-call(s32[3]{0:T(128)} %pad_add_fusion.flags, bf16[4,128,4096]{2,1,0:T(8,128)(2,1)} %shard_map.321.refs_4_.own_ref, bf16[4,128,4096]{2,1,0:T(8,128)(2,1)} %collective-permute-done.9.got_ref, bf16[4,64,2048]{2,1,0:T(8,128)(2,1)} %get-tuple-element.107.refs_0_), custom_call_target="tpu_custom_call" | custom-call | flops 4090397184 | bytes 12804721 | tf_op jit(solution)/shard_map/pallas_call | solution.py:835
  156.9 8.0 %fusion.2 = bf16[576,3072]{1,0:T(8,128)(2,1)} fusion(bf16[576,1024]{1,0:T(8,128)(2,1)S(1)} %get-tuple-element.177.refs_0_.refs_1_.refs_2_.refs_3_.refs_5_.refs_6_.refs_7_.refs_8_, bf16[1024,4096]{1,0:T(8,128)(2,1)} %bitcast.86), kind=kOutput, calls=%fused_computation.2 | convolution fusion | flops 3625648128 | bytes 11010048 | tf_op jit(solution)/shard_map/dot_general | solution.py:262
  164.9 9.6 %shard_map.324 = (bf16[4,144,1024]{2,1,0:T(8,128)(2,1)}, bf16[4,4,576,144]{3,2,1,0:T(8,128)(2,1)}) custom-call(s32[4]{0:T(128)} %lengths.1, bf16[4,144,3072]{2,1,0:T(8,128)(2,1)} %bitcast.130), custom_call_target="tpu_custom_call" | custom-call | flops 4831838208 | bytes 7372800 | tf_op jit(solution)/shard_map/pallas_call | solution.py:99
  179.9 5.7 shard_map.326.refs_4_.own_ref
  194.5 10.6 %collective-permute-done.15.refs_1_ = bf16[4,32,2816]{2,1,0:T(8,128)(2,1)} collective-permute-done((bf16[4,32,2816]{2,1,0:T(8,128)(2,1)}, bf16[4,32,2816]{2,1,0:T(8,128)(2,1)}, u32[]{:S(2)}, u32[]{:S(2)}) %collective-permute-start.15) | collective-permute-done | bytes 720928 | tf_op jit(solution)/shard_map/ppermute | solution.py:269
  205.9 4.8 shard_map.327
  215.1 7.7 %shard_map.328.refs_4_ = bf16[4,256,4096]{2,1,0:T(8,128)(2,1)} custom-call(s32[3]{0:T(128)} %pad_add_fusion.flags, bf16[4,128,4096]{2,1,0:T(8,128)(2,1)} %shard_map.326.refs_4_.own_ref, bf16[4,128,4096]{2,1,0:T(8,128)(2,1)} %copy-done.18, bf16[4,64,2816]{2,1,0:T(8,128)(2,1)} %get-tuple-element.112.refs_0_, ...), custom_call_target="tpu_custom_call" | custom-call | flops 4090397184 | bytes 12804721 | tf_op jit(solution)/shard_map/pallas_call | solution.py:835
  227.0 8.2 %fusion.7 = bf16[2048,1024]{0,1:T(8,128)(2,1)} fusion(bf16[1024,1024]{1,0:T(8,128)(2,1)S(1)} %bitcast.62, bf16[1024,4096]{1,0:T(8,128)(2,1)} %bitcast.91), kind=kOutput, calls=%fused_computation.5 | convolution fusion | flops 4297064448 | bytes 10485760 | tf_op jit(solution)/shard_map/dot_general | solution.py:262
  235.2 8.9 %shard_map.329 = (bf16[4,144,1024]{2,1,0:T(8,128)(2,1)}, bf16[4,4,576,256]{3,2,1,0:T(8,128)(2,1)}) custom-call(bf16[4,144,1024]{2,1,0:T(8,128)(2,1)} %bitcast.134, bf16[4,256,2048]{2,1,0:T(8,128)(2,1)} %bitcast.128, s32[4,1,256]{2,1,0:T(1,128)} %broadcast_in_dim.2.m_ref), custom_call_target="tpu_custom_call" | custom-call | flops 4831838208 | bytes 11796480 | tf_op jit(solution)/shard_map/pallas_call | solution.py:182
  245.2 6.5 shard_map.330.own_ref.refs_0_
  261.5 9.4 %shard_map.331 = bf16[4,256,5632]{2,1,0:T(8,128)(2,1)} custom-call(s32[3]{0:T(128)} %pad_add_fusion.flags, bf16[4,128,5632]{2,1,0:T(8,128)(2,1)} %shard_map.330.own_ref.refs_0_, bf16[4,128,5632]{2,1,0:T(8,128)(2,1)} %collective-permute-done.19.got_ref, bf16[4,128,5632]{2,1,0:T(8,128)(2,1)} %shard_map.330.own_ref.refs_0_, ...), custom_call_target="tpu_custom_call" | custom-call | flops 5085233664 | bytes 15918992 | tf_op jit(solution)/shard_map/pallas_call | solution.py:835
  271.0 20.0 %shard_map.332 = (bf16[576,2816]{1,0:T(8,128)(2,1)}, bf16[2,576,2816]{2,1,0:T(8,128)(2,1)}) custom-call(bf16[576,1024]{1,0:T(8,128)(2,1)} %multiply_convert_fusion.refs_1_.a_ref.refs_0_.refs_2_.refs_3_, bf16[576,1024]{1,0:T(8,128)(2,1)} %bitcast.121, bf16[1024,5632]{1,0:T(8,128)(2,1)} %bitcast.101, bf16[1024,5632]{1,0:T(8,128)(2,1)} %bitcast.102, ...), custom_call_target="tpu_custom_call" | custom-call | flops 11500000256 | bytes 36000000 | tf_op jit(solution)/shard_map/pallas_call | solution.py:638
  291.0 6.2 shard_map.333.refs_5_
  297.9 6.2 shard_map.334.refs_2_
  304.4 6.0 shard_map.335.refs_6_
  314.5 7.1 %shard_map.336 = (bf16[4,64,2816]{2,1,0:T(8,128)(2,1)}, bf16[4,64,2816]{2,1,0:T(8,128)(2,1)}) custom-call(s32[2]{0:T(128)} %pad_add_fusion.6.flags, bf16[576,1024]{1,0:T(8,128)(2,1)} %multiply_convert_fusion.refs_1_.a_ref.refs_0_.refs_2_.refs_3_, bf16[576,1024]{1,0:T(8,128)(2,1)} %multiply_convert_fusion.refs_1_.a_ref.refs_0_.refs_2_.refs_3_, ...), custom_call_target="tpu_custom_call" | custom-call | flops 3383060736 | bytes 10590451 | tf_op jit(solution)/shard_map/pallas_call | solution.py:366
  324.4 7.0 %shard_map.337 = (bf16[4,64,2816]{2,1,0:T(8,128)(2,1)}, bf16[4,64,2816]{2,1,0:T(8,128)(2,1)}) custom-call(s32[2]{0:T(128)} %pad_add_fusion.7.flags, bf16[576,1024]{1,0:T(8,128)(2,1)} %multiply_convert_fusion.refs_1_.a_ref.refs_0_.refs_2_.refs_3_, bf16[576,1024]{1,0:T(8,128)(2,1)} %multiply_convert_fusion.refs_1_.a_ref.refs_0_.refs_2_.refs_3_, ...), custom_call_target="tpu_custom_call" | custom-call | flops 3383060736 | bytes 10590451 | tf_op jit(solution)/shard_map/pallas_call | solution.py:366
  332.3 18.1 %shard_map.338 = (f32[576,1024]{1,0:T(8,128)}, f32[1,1024]{1,0:T(1,128)}, bf16[576,1024]{1,0:T(8,128)(2,1)}, bf16[576,1024]{1,0:T(8,128)(2,1)}) custom-call(bf16[2,576,2816]{2,1,0:T(8,128)(2,1)} %get-tuple-element.116.refs_4_.refs_0_, bf16[1024,5632]{1,0:T(8,128)(2,1)} %bitcast.103, f32[576,1024]{1,0:T(8,128)} %copy-done.22, bf16[576,1024]{1,0:T(8,128)(2,1)} %bitcast.123, ...), custom_call_target="tpu_custom_call" | custom-call | flops 10221485056 | bytes 31997692 | tf_op jit(solution)/shard_map/pallas_call | solution.py:603
  350.4 6.8 shard_map.339
  357.2 13.5 %shard_map.340 = (bf16[4,144,1024]{2,1,0:T(8,128)(2,1)}, bf16[4,256,2048]{2,1,0:T(8,128)(2,1)}) custom-call(bf16[4,144,1024]{2,1,0:T(8,128)(2,1)} %bitcast.135, bf16[4,256,2048]{2,1,0:T(8,128)(2,1)} %bitcast.129, bf16[4,4,576,256]{3,2,1,0:T(8,128)(2,1)} %get-tuple-element.121.p_ref, bf16[4,144,1024]{2,1,0:T(8,128)(2,1)} %bitcast.136, ...), custom_call_target="tpu_custom_call" | custom-call | flops 7762500096 | bytes 24300000 | tf_op jit(solution)/shard_map/pallas_call | solution.py:231
  372.3 4.6 shard_map.341
  376.9 9.8 %shard_map.342.refs_6_ = bf16[512,4096]{1,0:T(8,128)(2,1)} custom-call(s32[3]{0:T(128)} %add_add_fusion.flags, bf16[1024,1024]{1,0:T(8,128)(2,1)} %bitcast.54, bf16[1024,1024]{1,0:T(8,128)(2,1)} %bitcast.55, bf16[1024,1024]{1,0:T(8,128)(2,1)} %bitcast.56, bf16[1024,1024]{1,0:T(8,128)(2,1)} %bitcast.57, bf16[1024,2048]{1,0:T(8,128)(2,1)} %bitcast.98, ...), custom_call_target="tpu_custom_call" | custom-call | flops 4136724736 | bytes 12949747 | tf_op jit(solution)/shard_map/pallas_call | solution.py:366
  388.8 10.7 %shard_map.343 = (f32[576,1024]{1,0:T(8,128)}, f32[1,1024]{1,0:T(1,128)}, bf16[576,1024]{1,0:T(8,128)(2,1)}, bf16[576,1024]{1,0:T(8,128)(2,1)}) custom-call(bf16[576,1024]{1,0:T(8,128)(2,1)} %bitcast.105, bf16[1024,4096]{1,0:T(8,128)(2,1)} %bitcast.94, f32[576,1024]{1,0:T(8,128)} %copy-done.16, f32[576,1024]{1,0:T(8,128)} %get-tuple-element.130.refs_3_, ...), custom_call_target="tpu_custom_call" | custom-call | flops 4210724608 | bytes 13181398 | tf_op jit(solution)/shard_map/pallas_call | solution.py:603
  399.5 5.8 collective-permute-done.25.refs_1_
  412.1 31.4 %collective-permute-done.28.refs_1_ = bf16[2816,256]{1,0:T(8,128)(2,1)S(1)} collective-permute-done((bf16[2816,256]{1,0:T(8,128)(2,1)S(1)}, bf16[2816,256]{1,0:T(8,128)(2,1)S(1)}, u32[]{:S(2)}, u32[]{:S(2)}) %collective-permute-start.28) | collective-permute-done | bytes 1441824 | tf_op jit(solution)/shard_map/ppermute | solution.py:269
  448.2 11.1 %shard_map.346 = (bf16[4,64,2048]{2,1,0:T(8,128)(2,1)}, bf16[4,64,2048]{2,1,0:T(8,128)(2,1)}, bf16[4,64,2048]{2,1,0:T(8,128)(2,1)}, bf16[4,64,2048]{2,1,0:T(8,128)(2,1)}) custom-call(s32[3]{0:T(128)} %add_add_fusion.1.flags, bf16[1024,1024]{1,0:T(8,128)(2,1)} %bitcast.58, bf16[1024,1024]{1,0:T(8,128)(2,1)} %bitcast.59, bf16[1024,1024]{1,0:T(8,128)(2,1)} %bitcast.60, ...), custom_call_target="tpu_custom_call" | custom-call | flops 4136724736 | bytes 12949747 | tf_op jit(solution)/shard_map/pallas_call | solution.py:366
  459.3 11.5 %shard_map.347.refs_2_ = bf16[4,144,3072]{2,1,0:T(8,128)(2,1)} custom-call(bf16[4,144,3072]{2,1,0:T(8,128)(2,1)} %bitcast.131, bf16[4,4,576,144]{3,2,1,0:T(8,128)(2,1)} %get-tuple-element.140.p_ref, bf16[4,144,1024]{2,1,0:T(8,128)(2,1)} %bitcast.125, bf16[4,64,2048]{2,1,0:T(8,128)(2,1)} %get-tuple-element.137.refs_0_), custom_call_target="tpu_custom_call" | custom-call | flops 6612499968 | bytes 20700000 | tf_op jit(solution)/shard_map/pallas_call | solution.py:146
  476.1 8.6 %shard_map.349.refs_4_ = bf16[512,4096]{1,0:T(8,128)(2,1)} custom-call(s32[3]{0:T(128)} %add_add_fusion.flags, bf16[576,1024]{1,0:T(8,128)(2,1)} %copy-done.11, bf16[576,1024]{1,0:T(8,128)(2,1)} %copy-done.11, bf16[576,1024]{1,0:T(8,128)(2,1)} %copy-done.11, bf16[576,1024]{1,0:T(8,128)(2,1)} %copy-done.11, bf16[576,3072]{1,0:T(8,128)(2,1)} %bitcast.81, ...), custom_call_target="tpu_custom_call" | custom-call | flops 4136724736 | bytes 12949747 | tf_op jit(solution)/shard_map/pallas_call | solution.py:366
  484.8 12.4 %collective-permute-done.29.refs_1_ = bf16[4,64,2048]{2,1,0:T(8,128)(2,1)S(1)} collective-permute-done((bf16[4,64,2048]{2,1,0:T(8,128)(2,1)S(1)}, bf16[4,64,2048]{2,1,0:T(8,128)(2,1)S(1)}, u32[]{:S(2)}, u32[]{:S(2)}) %collective-permute-start.29) | collective-permute-done | bytes 1048608 | tf_op jit(solution)/shard_map/ppermute | solution.py:269
  504.3 10.3 %shard_map.352 = (bf16[4,64,2048]{2,1,0:T(8,128)(2,1)}, bf16[4,64,2048]{2,1,0:T(8,128)(2,1)}, bf16[4,64,2048]{2,1,0:T(8,128)(2,1)}, bf16[4,64,2048]{2,1,0:T(8,128)(2,1)}) custom-call(s32[3]{0:T(128)} %add_add_fusion.1.flags, bf16[576,1024]{1,0:T(8,128)(2,1)} %copy-done.11, bf16[576,1024]{1,0:T(8,128)(2,1)} %copy-done.11, bf16[576,1024]{1,0:T(8,128)(2,1)} %copy-done.11, ...), custom_call_target="tpu_custom_call" | custom-call | flops 4136724736 | bytes 12949747 | tf_op jit(solution)/shard_map/pallas_call | solution.py:366
  514.7 11.2 %shard_map.353 = (f32[576,1024]{1,0:T(8,128)}, f32[1,1024]{1,0:T(1,128)}) custom-call(bf16[576,3072]{1,0:T(8,128)(2,1)} %bitcast.85, bf16[1024,4096]{1,0:T(8,128)(2,1)} %bitcast.89, f32[576,1024]{1,0:T(8,128)} %bitcast.107, f32[576,1024]{1,0:T(8,128)} %get-tuple-element.152.refs_3_, f32[1,1024]{1,0:T(1,128)} %copy-done.41, ...), custom_call_target="tpu_custom_call" | custom-call | flops 6882173440 | bytes 21544196 | tf_op jit(solution)/shard_map/pallas_call | solution.py:603
  533.2 40.0 %collective-permute-done.35.refs_1_ = bf16[4,32,2048]{2,1,0:T(8,128)(2,1)S(1)} collective-permute-done((bf16[4,32,2048]{2,1,0:T(8,128)(2,1)S(1)}, bf16[4,32,2048]{2,1,0:T(8,128)(2,1)S(1)}, u32[]{:S(2)}, u32[]{:S(2)}) %collective-permute-start.35) | collective-permute-done | bytes 524320 | tf_op jit(solution)/shard_map/ppermute | solution.py:269
  581.3 9.3 %shard_map.357.refs_0_ = f32[1024,1024]{1,0:T(8,128)} custom-call(bf16[1024,2048]{1,0:T(8,128)(2,1)} %bitcast.100, bf16[1024,4096]{1,0:T(8,128)(2,1)} %bitcast.95, bf16[4,32,2048]{2,1,0:T(8,128)(2,1)} %get-tuple-element.154.refs_0_), custom_call_target="tpu_custom_call" | custom-call | flops 5175000064 | bytes 16200000 | tf_op jit(solution)/shard_map/pallas_call | solution.py:712
  592.5 6.4 shard_map.358
  598.9 8.7 %shard_map.359.refs_0_ = bf16[576,1024]{1,0:T(8,128)(2,1)} custom-call(bf16[576,2816]{1,0:T(8,128)(2,1)} %get-tuple-element.115.refs_0_.x_ref, bf16[2816,1024]{1,0:T(8,128)(2,1)} %bitcast.97, f32[576,1024]{1,0:T(8,128)} %copy-done.22, f32[256,2816]{1,0:T(8,128)} %get-tuple-element.94.refs_0_), custom_call_target="tpu_custom_call" | custom-call | flops 4600000000 | bytes 14400000 | tf_op jit(solution)/shard_map/pallas_call | solution.py:685
  608.5 5.8 shard_map.360.refs_4_
  646.2 4.5 shard_map.365
  664.8 5.3 collective-permute-done.47.refs_1_
  (365 shorter events, 194.9 us)
Async XLA Ops:
  7.2 47.3 %all-gather.12.cloned.1.call-start = ((), (), s32[]{:S(2)}) async-start(), calls=%async_computation.8 | async-start | bytes 1310720 | tf_op jit(solution)/shard_map/all_gather | solution.py:859
  9.1 93.6 %all-gather.14.cloned.1.call-start = ((), (), s32[]{:S(2)}) async-start(), calls=%async_computation.9 | async-start | bytes 1310720 | tf_op jit(solution)/shard_map/all_gather | solution.py:859
  37.9 7.6 %collective-permute-start = (bf16[4,352,128]{2,1,0:T(8,128)(2,1)}, bf16[4,352,128]{2,1,0:T(8,128)(2,1)S(1)}, u32[]{:S(2)}, u32[]{:S(2)}) collective-permute-start(bf16[4,352,128]{2,1,0:T(8,128)(2,1)} %get-tuple-element.97.refs_0_.refs_4_), channel_id=1, source_target_pairs={{0,8},{8,0},{1,9},{9,1},{2,10},{10,2},{3,11},{11,3},{4,12},{12,4},... | collective-permute-start | bytes 1081352 | tf_op jit(solution)/shard_map/ppermute | solution.py:269
  39.4 7.6 %collective-permute-start.1 = (bf16[4,352,128]{2,1,0:T(8,128)(2,1)}, bf16[4,352,128]{2,1,0:T(8,128)(2,1)S(1)}, u32[]{:S(2)}, u32[]{:S(2)}) collective-permute-start(bf16[4,352,128]{2,1,0:T(8,128)(2,1)} %get-tuple-element.98.refs_2_), channel_id=1, source_target_pairs={{0,16},{16,0},{1,17},{17,1},{2,18},{18,2},{3,19},{19,3},{4,20},{20... | collective-permute-start | bytes 1081352 | tf_op jit(solution)/shard_map/ppermute | solution.py:269
  52.2 12.7 %collective-permute-start.4 = (bf16[4,352,256]{2,1,0:T(8,128)(2,1)}, bf16[4,352,256]{2,1,0:T(8,128)(2,1)S(1)}, u32[]{:S(2)}, u32[]{:S(2)}) collective-permute-start(bf16[4,352,256]{2,1,0:T(8,128)(2,1)} %get-tuple-element.99.refs_0_), channel_id=1, source_target_pairs={{0,16},{16,0},{1,17},{17,1},{2,18},{18,2},{3,19},{19,3},{4,20},{20... | collective-permute-start | bytes 2162696 | tf_op jit(solution)/shard_map/ppermute | solution.py:269
  53.7 12.4 %collective-permute-start.5 = (bf16[4,352,256]{2,1,0:T(8,128)(2,1)}, bf16[4,352,256]{2,1,0:T(8,128)(2,1)S(1)}, u32[]{:S(2)}, u32[]{:S(2)}) collective-permute-start(bf16[4,352,256]{2,1,0:T(8,128)(2,1)} %get-tuple-element.102.refs_2_), channel_id=1, source_target_pairs={{0,8},{8,0},{1,9},{9,1},{2,10},{10,2},{3,11},{11,3},{4,12},{12,4},... | collective-permute-start | bytes 2162696 | tf_op jit(solution)/shard_map/ppermute | solution.py:269
  72.1 22.1 %collective-permute-start.8 = (bf16[4,704,512]{2,1,0:T(8,128)(2,1)}, bf16[4,704,512]{2,1,0:T(8,128)(2,1)}, u32[]{:S(2)}, u32[]{:S(2)}) collective-permute-start(bf16[4,704,512]{2,1,0:T(8,128)(2,1)} %shard_map.317.refs_4_.own_ref), channel_id=1, source_target_pairs={{0,4},{4,0},{1,5},{5,1},{2,6},{6,2},{3,7},{7,3},{8,12},{12,8},{9,1... | collective-permute-start | bytes 8650760 | tf_op jit(solution)/shard_map/ppermute | solution.py:269
  72.1 14.3 %collective-permute-start.2 = (bf16[4,32,2048]{2,1,0:T(8,128)(2,1)S(1)}, bf16[4,32,2048]{2,1,0:T(8,128)(2,1)S(1)}, u32[]{:S(2)}, u32[]{:S(2)}) collective-permute-start(bf16[4,32,2048]{2,1,0:T(8,128)(2,1)S(1)} %copy-done.66), channel_id=1, source_target_pairs={{0,8},{8,0},{1,9},{9,1},{2,10},{10,2},{3,11},{11,3},{4,12},{12,4},... | collective-permute-start | bytes 1572872 | tf_op jit(solution)/shard_map/ppermute | solution.py:269
  73.2 14.2 %collective-permute-start.3 = (bf16[4,32,2048]{2,1,0:T(8,128)(2,1)}, bf16[4,32,2048]{2,1,0:T(8,128)(2,1)S(1)}, u32[]{:S(2)}, u32[]{:S(2)}) collective-permute-start(bf16[4,32,2048]{2,1,0:T(8,128)(2,1)} %get-tuple-element.101.refs_2_), channel_id=1, source_target_pairs={{0,16},{16,0},{1,17},{17,1},{2,18},{18,2},{3,19},{19,3},{4,20},{20... | collective-permute-start | bytes 1572872 | tf_op jit(solution)/shard_map/ppermute | solution.py:269
  74.4 100.0 %all-gather.16.cloned.1.call-start = ((), (), s32[]{:S(2)}) async-start(), calls=%async_computation.10 | async-start | bytes 1802240 | tf_op jit(solution)/shard_map/all_gather | solution.py:859
  92.7 24.9 %collective-permute-start.6 = (bf16[4,64,2048]{2,1,0:T(8,128)(2,1)}, bf16[4,64,2048]{2,1,0:T(8,128)(2,1)S(1)}, u32[]{:S(2)}, u32[]{:S(2)}) collective-permute-start(bf16[4,64,2048]{2,1,0:T(8,128)(2,1)} %get-tuple-element.103.refs_0_), channel_id=1, source_target_pairs={{0,16},{16,0},{1,17},{17,1},{2,18},{18,2},{3,19},{19,3},{4,20},{20... | collective-permute-start | bytes 3145736 | tf_op jit(solution)/shard_map/ppermute | solution.py:269
  93.2 24.5 %collective-permute-start.7 = (bf16[4,64,2048]{2,1,0:T(8,128)(2,1)}, bf16[4,64,2048]{2,1,0:T(8,128)(2,1)S(1)}, u32[]{:S(2)}, u32[]{:S(2)}) collective-permute-start(bf16[4,64,2048]{2,1,0:T(8,128)(2,1)} %get-tuple-element.104.refs_2_), channel_id=1, source_target_pairs={{0,8},{8,0},{1,9},{9,1},{2,10},{10,2},{3,11},{11,3},{4,12},{12,4},... | collective-permute-start | bytes 3145736 | tf_op jit(solution)/shard_map/ppermute | solution.py:269
  124.4 24.7 %collective-permute-start.9 = (bf16[4,128,4096]{2,1,0:T(8,128)(2,1)}, bf16[4,128,4096]{2,1,0:T(8,128)(2,1)}, u32[]{:S(2)}, u32[]{:S(2)}) collective-permute-start(bf16[4,128,4096]{2,1,0:T(8,128)(2,1)} %shard_map.321.refs_4_.own_ref), channel_id=1, source_target_pairs={{0,4},{4,0},{1,5},{5,1},{2,6},{6,2},{3,7},{7,3},{8,12},{12,8},{9,1... | collective-permute-start | bytes 12582920 | tf_op jit(solution)/shard_map/ppermute | solution.py:269
  125.3 377.8 %reduce-scatter.5.cloned.1.call-start = ((), (), s32[]{:S(2)}) async-start(), calls=%async_computation.4 | async-start | bytes 1802240 | tf_op jit(solution)/shard_map/reduce_scatter | solution.py:986
  126.2 16.9 %collective-permute-start.10 = (bf16[4,32,2048]{2,1,0:T(8,128)(2,1)S(1)}, bf16[4,32,2048]{2,1,0:T(8,128)(2,1)}, u32[]{:S(2)}, u32[]{:S(2)}) collective-permute-start(bf16[4,32,2048]{2,1,0:T(8,128)(2,1)S(1)} %copy-done.64), channel_id=1, source_target_pairs={{0,8},{8,0},{1,9},{9,1},{2,10},{10,2},{3,11},{11,3},{4,12},{12,4},... | collective-permute-start | bytes 1572872 | tf_op jit(solution)/shard_map/ppermute | solution.py:269
  127.2 15.9 %collective-permute-start.11 = (bf16[4,32,2048]{2,1,0:T(8,128)(2,1)}, bf16[4,32,2048]{2,1,0:T(8,128)(2,1)}, u32[]{:S(2)}, u32[]{:S(2)}) collective-permute-start(bf16[4,32,2048]{2,1,0:T(8,128)(2,1)} %get-tuple-element.106.refs_2_), channel_id=1, source_target_pairs={{0,16},{16,0},{1,17},{17,1},{2,18},{18,2},{3,19},{19,3},{4,20},{20... | collective-permute-start | bytes 1572872 | tf_op jit(solution)/shard_map/ppermute | solution.py:269
  147.6 30.3 %collective-permute-start.12 = (bf16[4,64,2048]{2,1,0:T(8,128)(2,1)}, bf16[4,64,2048]{2,1,0:T(8,128)(2,1)S(1)}, u32[]{:S(2)}, u32[]{:S(2)}) collective-permute-start(bf16[4,64,2048]{2,1,0:T(8,128)(2,1)} %get-tuple-element.107.refs_0_), channel_id=1, source_target_pairs={{0,16},{16,0},{1,17},{17,1},{2,18},{18,2},{3,19},{19,3},{4,20},{20... | collective-permute-start | bytes 3145736 | tf_op jit(solution)/shard_map/ppermute | solution.py:269
  148.2 29.7 %collective-permute-start.13 = (bf16[4,64,2048]{2,1,0:T(8,128)(2,1)}, bf16[4,64,2048]{2,1,0:T(8,128)(2,1)S(1)}, u32[]{:S(2)}, u32[]{:S(2)}) collective-permute-start(bf16[4,64,2048]{2,1,0:T(8,128)(2,1)} %get-tuple-element.109.refs_2_), channel_id=1, source_target_pairs={{0,8},{8,0},{1,9},{9,1},{2,10},{10,2},{3,11},{11,3},{4,12},{12,4},... | collective-permute-start | bytes 3145736 | tf_op jit(solution)/shard_map/ppermute | solution.py:269
  185.6 27.4 %collective-permute-start.14 = (bf16[4,128,4096]{2,1,0:T(8,128)(2,1)}, bf16[4,128,4096]{2,1,0:T(8,128)(2,1)S(1)}, u32[]{:S(2)}, u32[]{:S(2)}) collective-permute-start(bf16[4,128,4096]{2,1,0:T(8,128)(2,1)} %shard_map.326.refs_4_.own_ref), channel_id=1, source_target_pairs={{0,4},{4,0},{1,5},{5,1},{2,6},{6,2},{3,7},{7,3},{8,12},{12,8},{9,1... | collective-permute-start | bytes 12582920 | tf_op jit(solution)/shard_map/ppermute | solution.py:269
  186.2 18.9 %collective-permute-start.15 = (bf16[4,32,2816]{2,1,0:T(8,128)(2,1)}, bf16[4,32,2816]{2,1,0:T(8,128)(2,1)}, u32[]{:S(2)}, u32[]{:S(2)}) collective-permute-start(bf16[4,32,2816]{2,1,0:T(8,128)(2,1)} %get-tuple-element.110.refs_4_.refs_0_), channel_id=1, source_target_pairs={{0,8},{8,0},{1,9},{9,1},{2,10},{10,2},{3,11},{11,3},{4,12},{12,4},... | collective-permute-start | bytes 2162696 | tf_op jit(solution)/shard_map/ppermute | solution.py:269
  187.3 18.6 %collective-permute-start.16 = (bf16[4,32,2816]{2,1,0:T(8,128)(2,1)}, bf16[4,32,2816]{2,1,0:T(8,128)(2,1)}, u32[]{:S(2)}, u32[]{:S(2)}) collective-permute-start(bf16[4,32,2816]{2,1,0:T(8,128)(2,1)} %get-tuple-element.111.refs_2_), channel_id=1, source_target_pairs={{0,16},{16,0},{1,17},{17,1},{2,18},{18,2},{3,19},{19,3},{4,20},{20... | collective-permute-start | bytes 2162696 | tf_op jit(solution)/shard_map/ppermute | solution.py:269
  210.7 33.4 %collective-permute-start.17 = (bf16[4,64,2816]{2,1,0:T(8,128)(2,1)}, bf16[4,64,2816]{2,1,0:T(8,128)(2,1)S(1)}, u32[]{:S(2)}, u32[]{:S(2)}) collective-permute-start(bf16[4,64,2816]{2,1,0:T(8,128)(2,1)} %get-tuple-element.112.refs_0_), channel_id=1, source_target_pairs={{0,16},{16,0},{1,17},{17,1},{2,18},{18,2},{3,19},{19,3},{4,20},{20... | collective-permute-start | bytes 4325384 | tf_op jit(solution)/shard_map/ppermute | solution.py:269
  212.2 32.9 %collective-permute-start.18 = (bf16[4,64,2816]{2,1,0:T(8,128)(2,1)}, bf16[4,64,2816]{2,1,0:T(8,128)(2,1)}, u32[]{:S(2)}, u32[]{:S(2)}) collective-permute-start(bf16[4,64,2816]{2,1,0:T(8,128)(2,1)} %get-tuple-element.114.refs_2_), channel_id=1, source_target_pairs={{0,8},{8,0},{1,9},{9,1},{2,10},{10,2},{3,11},{11,3},{4,12},{12,4},... | collective-permute-start | bytes 4325384 | tf_op jit(solution)/shard_map/ppermute | solution.py:269
  251.7 9.8 %collective-permute-start.19 = (bf16[4,128,5632]{2,1,0:T(8,128)(2,1)}, bf16[4,128,5632]{2,1,0:T(8,128)(2,1)}, u32[]{:S(2)}, u32[]{:S(2)}) collective-permute-start(bf16[4,128,5632]{2,1,0:T(8,128)(2,1)} %shard_map.330.own_ref.refs_0_), channel_id=1, source_target_pairs={{0,4},{4,0},{1,5},{5,1},{2,6},{6,2},{3,7},{7,3},{8,12},{12,8},{9,1... | collective-permute-start | bytes 17301512 | tf_op jit(solution)/shard_map/ppermute | solution.py:269
  297.1 15.8 %collective-permute-start.20 = (bf16[512,2816]{1,0:T(8,128)(2,1)}, bf16[512,2816]{1,0:T(8,128)(2,1)S(1)}, u32[]{:S(2)}, u32[]{:S(2)}) collective-permute-start(bf16[512,2816]{1,0:T(8,128)(2,1)} %shard_map.333.refs_5_), channel_id=1, source_target_pairs={{0,4},{4,0},{1,5},{5,1},{2,6},{6,2},{3,7},{7,3},{8,12},{12,8},{9,1... | collective-permute-start | bytes 8650760 | tf_op jit(solution)/shard_map/ppermute | solution.py:269
  304.1 18.7 %collective-permute-start.22 = (bf16[512,2816]{1,0:T(8,128)(2,1)}, bf16[512,2816]{1,0:T(8,128)(2,1)S(1)}, u32[]{:S(2)}, u32[]{:S(2)}) collective-permute-start(bf16[512,2816]{1,0:T(8,128)(2,1)} %shard_map.334.refs_2_), channel_id=1, source_target_pairs={{0,4},{4,0},{1,5},{5,1},{2,6},{6,2},{3,7},{7,3},{8,12},{12,8},{9,1... | collective-permute-start | bytes 8650760 | tf_op jit(solution)/shard_map/ppermute | solution.py:269
  310.4 40.0 %collective-permute-start.24 = (bf16[2816,512]{1,0:T(8,128)(2,1)}, bf16[2816,512]{1,0:T(8,128)(2,1)}, u32[]{:S(2)}, u32[]{:S(2)}) collective-permute-start(bf16[2816,512]{1,0:T(8,128)(2,1)} %shard_map.335.refs_6_), channel_id=1, source_target_pairs={{0,4},{4,0},{1,5},{5,1},{2,6},{6,2},{3,7},{7,3},{8,12},{12,8},{9,1... | collective-permute-start | bytes 8650760 | tf_op jit(solution)/shard_map/ppermute | solution.py:269
  321.6 49.1 %collective-permute-start.21 = (bf16[4,64,2816]{2,1,0:T(8,128)(2,1)}, bf16[4,64,2816]{2,1,0:T(8,128)(2,1)S(1)}, u32[]{:S(2)}, u32[]{:S(2)}) collective-permute-start(bf16[4,64,2816]{2,1,0:T(8,128)(2,1)} %get-tuple-element.118.refs_6_), channel_id=1, source_target_pairs={{0,8},{8,0},{1,9},{9,1},{2,10},{10,2},{3,11},{11,3},{4,12},{12,4},... | collective-permute-start | bytes 4325384 | tf_op jit(solution)/shard_map/ppermute | solution.py:269
  331.4 39.3 %collective-permute-start.23 = (bf16[4,64,2816]{2,1,0:T(8,128)(2,1)}, bf16[4,64,2816]{2,1,0:T(8,128)(2,1)S(1)}, u32[]{:S(2)}, u32[]{:S(2)}) collective-permute-start(bf16[4,64,2816]{2,1,0:T(8,128)(2,1)} %get-tuple-element.120.refs_6_), channel_id=1, source_target_pairs={{0,16},{16,0},{1,17},{17,1},{2,18},{18,2},{3,19},{19,3},{4,20},{20... | collective-permute-start | bytes 4325384 | tf_op jit(solution)/shard_map/ppermute | solution.py:269
  386.7 61.5 %collective-permute-start.27 = (bf16[512,4096]{1,0:T(8,128)(2,1)}, bf16[512,4096]{1,0:T(8,128)(2,1)}, u32[]{:S(2)}, u32[]{:S(2)}) collective-permute-start(bf16[512,4096]{1,0:T(8,128)(2,1)} %shard_map.342.refs_6_), channel_id=1, source_target_pairs={{0,4},{4,0},{1,5},{5,1},{2,6},{6,2},{3,7},{7,3},{8,12},{12,8},{9,1... | collective-permute-start | bytes 12582920 | tf_op jit(solution)/shard_map/ppermute | solution.py:269
  386.7 18.5 %collective-permute-start.25 = (bf16[4,32,2816]{2,1,0:T(8,128)(2,1)S(1)}, bf16[4,32,2816]{2,1,0:T(8,128)(2,1)S(1)}, u32[]{:S(2)}, u32[]{:S(2)}) collective-permute-start(bf16[4,32,2816]{2,1,0:T(8,128)(2,1)S(1)} %copy-done.29), channel_id=1, source_target_pairs={{0,16},{16,0},{1,17},{17,1},{2,18},{18,2},{3,19},{19,3},{4,20},{20... | collective-permute-start | bytes 2162696 | tf_op jit(solution)/shard_map/ppermute | solution.py:269
  387.9 18.2 %collective-permute-start.26 = (bf16[4,32,2816]{2,1,0:T(8,128)(2,1)S(1)}, bf16[4,32,2816]{2,1,0:T(8,128)(2,1)S(1)}, u32[]{:S(2)}, u32[]{:S(2)}) collective-permute-start(bf16[4,32,2816]{2,1,0:T(8,128)(2,1)S(1)} %copy-done.58), channel_id=1, source_target_pairs={{0,8},{8,0},{1,9},{9,1},{2,10},{10,2},{3,11},{11,3},{4,12},{12,4},... | collective-permute-start | bytes 2162696 | tf_op jit(solution)/shard_map/ppermute | solution.py:269
  410.5 116.2 %reduce-scatter.7.cloned.1.call-start = ((), (), s32[]{:S(2)}) async-start(), calls=%async_computation.5 | async-start | bytes 901120 | tf_op jit(solution)/shard_map/reduce_scatter | solution.py:986
  410.6 32.9 %collective-permute-start.28 = (bf16[2816,256]{1,0:T(8,128)(2,1)S(1)}, bf16[2816,256]{1,0:T(8,128)(2,1)S(1)}, u32[]{:S(2)}, u32[]{:S(2)}) collective-permute-start(bf16[2816,256]{1,0:T(8,128)(2,1)S(1)} %copy-done.46), channel_id=1, source_target_pairs={{0,8},{8,0},{1,9},{9,1},{2,10},{10,2},{3,11},{11,3},{4,12},{12,4},... | collective-permute-start | bytes 4325384 | tf_op jit(solution)/shard_map/ppermute | solution.py:269
  447.3 23.5 %collective-permute-start.31 = (bf16[2816,128]{1,0:T(8,128)(2,1)}, bf16[2816,128]{1,0:T(8,128)(2,1)S(1)}, u32[]{:S(2)}, u32[]{:S(2)}) collective-permute-start(bf16[2816,128]{1,0:T(8,128)(2,1)} %get-tuple-element.135.refs_16_), channel_id=1, source_target_pairs={{0,16},{16,0},{1,17},{17,1},{2,18},{18,2},{3,19},{19,3},{4,20},{20... | collective-permute-start | bytes 2162696 | tf_op jit(solution)/shard_map/ppermute | solution.py:269
  474.0 118.5 %all-gather.18.cloned.1.call-start = ((), (), s32[]{:S(2)}) async-start(), calls=%async_computation.11 | async-start | bytes 3244032 | tf_op jit(solution)/shard_map/all_gather | solution.py:982
  474.0 23.2 %collective-permute-start.29 = (bf16[4,64,2048]{2,1,0:T(8,128)(2,1)S(1)}, bf16[4,64,2048]{2,1,0:T(8,128)(2,1)S(1)}, u32[]{:S(2)}, u32[]{:S(2)}) collective-permute-start(bf16[4,64,2048]{2,1,0:T(8,128)(2,1)S(1)} %copy-done.53), channel_id=1, source_target_pairs={{0,8},{8,0},{1,9},{9,1},{2,10},{10,2},{3,11},{11,3},{4,12},{12,4},... | collective-permute-start | bytes 3145736 | tf_op jit(solution)/shard_map/ppermute | solution.py:269
  475.2 22.8 %collective-permute-start.30 = (bf16[4,64,2048]{2,1,0:T(8,128)(2,1)S(1)}, bf16[4,64,2048]{2,1,0:T(8,128)(2,1)S(1)}, u32[]{:S(2)}, u32[]{:S(2)}) collective-permute-start(bf16[4,64,2048]{2,1,0:T(8,128)(2,1)S(1)} %copy-done.52), channel_id=1, source_target_pairs={{0,16},{16,0},{1,17},{17,1},{2,18},{18,2},{3,19},{19,3},{4,20},{20... | collective-permute-start | bytes 3145736 | tf_op jit(solution)/shard_map/ppermute | solution.py:269
  484.7 19.6 %collective-permute-start.32 = (bf16[512,4096]{1,0:T(8,128)(2,1)}, bf16[512,4096]{1,0:T(8,128)(2,1)}, u32[]{:S(2)}, u32[]{:S(2)}) collective-permute-start(bf16[512,4096]{1,0:T(8,128)(2,1)} %shard_map.349.refs_4_), channel_id=1, source_target_pairs={{0,4},{4,0},{1,5},{5,1},{2,6},{6,2},{3,7},{7,3},{8,12},{12,8},{9,1... | collective-permute-start | bytes 12582920 | tf_op jit(solution)/shard_map/ppermute | solution.py:269
  504.2 103.4 %all-gather.20.cloned.1.call-start = ((), (), s32[]{:S(2)}) async-start(), calls=%async_computation.12 | async-start | bytes 1695744 | tf_op jit(solution)/shard_map/all_gather | solution.py:982
  529.1 91.6 %reduce-scatter.11.cloned.1.call-start = ((), (), s32[]{:S(2)}) async-start(), calls=%async_computation.7 | async-start | bytes 1310720 | tf_op jit(solution)/shard_map/reduce_scatter | solution.py:986
  529.1 48.2 %collective-permute-start.33 = (bf16[4,64,2048]{2,1,0:T(8,128)(2,1)S(1)}, bf16[4,64,2048]{2,1,0:T(8,128)(2,1)}, u32[]{:S(2)}, u32[]{:S(2)}) collective-permute-start(bf16[4,64,2048]{2,1,0:T(8,128)(2,1)S(1)} %copy-done.51), channel_id=1, source_target_pairs={{0,8},{8,0},{1,9},{9,1},{2,10},{10,2},{3,11},{11,3},{4,12},{12,4},... | collective-permute-start | bytes 3145736 | tf_op jit(solution)/shard_map/ppermute | solution.py:269
  530.0 47.3 %collective-permute-start.34 = (bf16[4,64,2048]{2,1,0:T(8,128)(2,1)S(1)}, bf16[4,64,2048]{2,1,0:T(8,128)(2,1)}, u32[]{:S(2)}, u32[]{:S(2)}) collective-permute-start(bf16[4,64,2048]{2,1,0:T(8,128)(2,1)S(1)} %copy-done.50), channel_id=1, source_target_pairs={{0,16},{16,0},{1,17},{17,1},{2,18},{18,2},{3,19},{19,3},{4,20},{20... | collective-permute-start | bytes 3145736 | tf_op jit(solution)/shard_map/ppermute | solution.py:269
  531.3 42.0 %collective-permute-start.35 = (bf16[4,32,2048]{2,1,0:T(8,128)(2,1)S(1)}, bf16[4,32,2048]{2,1,0:T(8,128)(2,1)S(1)}, u32[]{:S(2)}, u32[]{:S(2)}) collective-permute-start(bf16[4,32,2048]{2,1,0:T(8,128)(2,1)S(1)} %copy-done.9), channel_id=1, source_target_pairs={{0,16},{16,0},{1,17},{17,1},{2,18},{18,2},{3,19},{19,3},{4,20},{20... | collective-permute-start | bytes 1572872 | tf_op jit(solution)/shard_map/ppermute | solution.py:269
  532.0 41.2 %collective-permute-start.36 = (bf16[4,32,2048]{2,1,0:T(8,128)(2,1)S(1)}, bf16[4,32,2048]{2,1,0:T(8,128)(2,1)S(1)}, u32[]{:S(2)}, u32[]{:S(2)}) collective-permute-start(bf16[4,32,2048]{2,1,0:T(8,128)(2,1)S(1)} %copy-done.63), channel_id=1, source_target_pairs={{0,8},{8,0},{1,9},{9,1},{2,10},{10,2},{3,11},{11,3},{4,12},{12,4},... | collective-permute-start | bytes 1572872 | tf_op jit(solution)/shard_map/ppermute | solution.py:269
  577.3 73.4 %reduce-scatter.9.cloned.1.call-start = ((), (), s32[]{:S(2)}) async-start(), calls=%async_computation.6 | async-start | bytes 1351680 | tf_op jit(solution)/shard_map/reduce_scatter | solution.py:986
  590.6 23.6 %collective-permute-start.37 = (bf16[4,32,2048]{2,1,0:T(8,128)(2,1)S(1)}, bf16[4,32,2048]{2,1,0:T(8,128)(2,1)S(1)}, u32[]{:S(2)}, u32[]{:S(2)}) collective-permute-start(bf16[4,32,2048]{2,1,0:T(8,128)(2,1)S(1)} %copy-done.67), channel_id=1, source_target_pairs={{0,16},{16,0},{1,17},{17,1},{2,18},{18,2},{3,19},{19,3},{4,20},{20... | collective-permute-start | bytes 1572872 | tf_op jit(solution)/shard_map/ppermute | solution.py:269
  591.8 22.5 %collective-permute-start.38 = (bf16[4,32,2048]{2,1,0:T(8,128)(2,1)S(1)}, bf16[4,32,2048]{2,1,0:T(8,128)(2,1)S(1)}, u32[]{:S(2)}, u32[]{:S(2)}) collective-permute-start(bf16[4,32,2048]{2,1,0:T(8,128)(2,1)S(1)} %copy-done.65), channel_id=1, source_target_pairs={{0,8},{8,0},{1,9},{9,1},{2,10},{10,2},{3,11},{11,3},{4,12},{12,4},... | collective-permute-start | bytes 1572872 | tf_op jit(solution)/shard_map/ppermute | solution.py:269
  (101 other events, 555.6 us)
Sparse Core Ops, SparseCore 0:
  10.2 35.0 all-gather.11
  74.5 28.1 all-gather.13
  125.4 35.1 all-gather.15
  410.6 32.7 reduce-scatter.4
  474.1 22.2 reduce-scatter.6
  504.3 34.2 all-gather.17
  540.5 32.8 all-gather.19
  577.4 27.1 reduce-scatter.10
  620.8 27.7 reduce-scatter.8

commit v3 on v2

--- a/solution.py
+++ b/solution.py
@@ -14,6 +14,9 @@
 MASKED = -1e30
 SCALE = 0.125
 VMEM_LIMIT = 56 * 1024 * 1024
+
+C_LONG = 100
+C_SEG1 = 20
 
 BF16 = jnp.bfloat16
 F32 = jnp.float32
@@ -112,11 +115,7 @@
             jax.ShapeDtypeStruct((items, quads, QUAD * rows, rows), BF16),
         ],
         compiler_params=params(),
-        cost_estimate=pl.CostEstimate(
-            flops=8 * items * quads * QUAD * rows * 256 * 256,
-            bytes_accessed=2 * items * rows * (4 * width + 16 * rows),
-            transcendentals=0,
-        ),
+        cost_estimate=cost(0.1),
     )(lengths, qkv)
 
 
@@ -155,7 +154,7 @@
         out_specs=pl.BlockSpec((1, rows, width3), lambda i: (i, 0, 0)),
         out_shape=jax.ShapeDtypeStruct((items, rows, width3), BF16),
         compiler_params=params(),
-        cost_estimate=cost(11.5),
+        cost_estimate=cost(order.long()),
     )(qkv, probs, grad, *waits)
     return order.after(out)
 
@@ -196,11 +195,7 @@
             jax.ShapeDtypeStruct((items, quads, QUAD * rows, keys), BF16),
         ],
         compiler_params=params(),
-        cost_estimate=pl.CostEstimate(
-            flops=8 * items * quads * QUAD * rows * 256 * 256,
-            bytes_accessed=2 * items * rows * (6 * width + 16 * keys),
-            transcendentals=0,
-        ),
+        cost_estimate=cost(0.1),
     )(q, kv, mask)
 
 
@@ -248,7 +243,7 @@
             jax.ShapeDtypeStruct((items, keys, 2 * width), BF16),
         ],
         compiler_params=params(),
-        cost_estimate=cost(13.5),
+        cost_estimate=cost(order.long()),
     )(q, kv, probs, grad, mask, *waits)
     order.after(out[0])
     return out
@@ -271,7 +266,11 @@
 
 class Order:
     def __init__(self):
-        self.waits = []
+        self.waits, self.micros = [], 0.1
+
+    def long(self):
+        micros, self.micros = self.micros, 0.1
+        return micros
 
     def take(self):
         waits, self.waits = self.waits, []
@@ -296,19 +295,14 @@
         out_shape=jax.ShapeDtypeStruct(array.shape, array.dtype),
         input_output_aliases={0: 0},
         compiler_params=pltpu.CompilerParams(vmem_limit_bytes=1024 * 1024),
-        cost_estimate=cost(0.5),
+        cost_estimate=cost(order.long()),
     )(array, *waits)
     return order.after(out)
 
 
-SHARE = 0.5
-
-
 def cost(micros):
     return pl.CostEstimate(
-        flops=int(SHARE * micros * 1.15e9),
-        bytes_accessed=int(SHARE * micros * 3.6e6),
-        transcendentals=0,
+        flops=int(micros * 1.15e9), bytes_accessed=int(micros * 3.6e6), transcendentals=0
     )
 
 
@@ -373,7 +367,7 @@
         ),
         out_shape=out_shapes,
         compiler_params=params(),
-        cost_estimate=cost(3 + 2e-6 * sum(v.size for v in out_shapes)),
+        cost_estimate=cost(order.long()),
     )(flags, *operands, *waits)
     order.after(out[0])
     return out
@@ -484,49 +478,52 @@
         ),
         out_shape=[jax.ShapeDtypeStruct(shape, BF16) for shape in shapes],
         compiler_params=params(),
-        cost_estimate=cost(1.5 + 1.7e-6 * sum(k.size for k, _ in pairs)),
+        cost_estimate=cost(order.long()),
     )(jnp.stack(flags), *operands, *waits)
     order.after(out[0])
     return out
 
 
-def join_kernel(count, pieces, flags, *refs):
-    outs = refs[len(refs) - count * pieces :]
-    for i in range(count):
-        own, got = refs[2 * i], refs[2 * i + 1]
-        half, columns = own.shape[0], own.shape[1] // pieces
-        for k in range(pieces):
-            out = outs[i * pieces + k]
-            at = slice(k * columns, (k + 1) * columns)
-
-            def put(low, high, out=out, at=at, half=half):
-                out[:half] = low[:, at].astype(out.dtype)
-                out[half:] = high[:, at].astype(out.dtype)
-
-            pl.when(flags[i] == 0)(functools.partial(put, own, got))
-            pl.when(flags[i] > 0)(functools.partial(put, got, own))
-
-
-def land_joins(order, pairs, flags, pieces, kind):
+def join_kernel(axis, parts, turned, flag, own_ref, got_ref, *refs):
+    outs = refs[len(refs) - len(parts) :]
+    half = own_ref.shape[axis]
+
+    def put(low, high):
+        column = 0
+        for out, columns, turn in zip(outs, parts, turned):
+            at = slice(column, column + columns)
+            column += columns
+            for start, ref in ((0, low), (half, high)):
+                value = ref[:, at].astype(out.dtype)
+                if axis == 1:
+                    out[:, start : start + half] = value
+                elif turn:
+                    n = half // 4
+                    for i, j in enumerate((0, 2, 1, 3)):
+                        out[start + j * n : start + (j + 1) * n] = value[i * n : (i + 1) * n]
+                else:
+                    out[start : start + half] = value
+
+    either(flag[0], put, own_ref, got_ref)
+
+
+def land_join(order, own, got, flag, axis, parts, turned, kind):
     waits = order.take()
     whole = lambda shape: pl.BlockSpec(shape, lambda j, f: (0, 0))
-    specs, operands, shapes = [], [], []
-    for own, got in pairs:
-        specs += [whole(own.shape)] * 2
-        operands += [own, got]
-        shapes += [(2 * own.shape[0], own.shape[1] // pieces)] * pieces
+    n, c = own.shape
+    shapes = [(2 * n, columns) for columns in parts] if axis == 0 else [(n, 2 * c)]
     out = pl.pallas_call(
-        functools.partial(join_kernel, len(pairs), pieces),
+        functools.partial(join_kernel, axis, parts, turned),
         grid_spec=pltpu.PrefetchScalarGridSpec(
             num_scalar_prefetch=1,
             grid=(1,),
-            in_specs=specs + [pl.BlockSpec(memory_space=pl.ANY)] * len(waits),
+            in_specs=[whole(own.shape)] * 2 + [pl.BlockSpec(memory_space=pl.ANY)] * len(waits),
             out_specs=[whole(shape) for shape in shapes],
         ),
         out_shape=[jax.ShapeDtypeStruct(shape, kind) for shape in shapes],
         compiler_params=params(),
-        cost_estimate=cost(2 + 1.5e-6 * sum(v.size for v, _ in pairs)),
-    )(jnp.stack(flags), *operands, *waits)
+        cost_estimate=cost(order.long()),
+    )(flag.reshape(1), own, got, *waits)
     order.after(out[0])
     return out
 
@@ -608,7 +605,7 @@
         out_shape=shapes,
         scratch_shapes=[pltpu.VMEM((rows, width), F32)],
         compiler_params=params(),
-        cost_estimate=cost(5 + x.size * width / 2.6e8),
+        cost_estimate=cost(order.long()),
     )(*operands, *waits)
     order.after(out[1])
     return out
@@ -629,7 +626,7 @@
     d_ref[1] = (grad * act).astype(BF16)
 
 
-def mlp(a3, e3, w_wide, w_down):
+def mlp(order, a3, e3, w_wide, w_down):
     rows, width = a3.shape
     hidden = w_down.shape[0]
     tile = 256
@@ -654,7 +651,7 @@
             jax.ShapeDtypeStruct((2, rows, hidden), BF16),
         ],
         compiler_params=params(),
-        cost_estimate=cost(20),
+        cost_estimate=cost(order.long()),
     )(a3, e3, w_wide, w_wide, w_down)
 
 
@@ -695,7 +692,7 @@
         out_shape=jax.ShapeDtypeStruct((rows, width), BF16),
         scratch_shapes=[pltpu.VMEM((rows, width), F32)],
         compiler_params=params(),
-        cost_estimate=cost(8),
+        cost_estimate=cost(order.long()),
     )(x, w, base, *waits)
     return order.after(out)
 
@@ -720,7 +717,7 @@
         out_specs=pl.BlockSpec((rows, tile), lambda j: (0, j)),
         out_shape=jax.ShapeDtypeStruct((rows, width), F32),
         compiler_params=params(),
-        cost_estimate=cost(9),
+        cost_estimate=cost(order.long()),
     )(x, w, *waits)
     return order.after(out)
 
@@ -782,6 +779,30 @@
     half = z_ref.shape[2 - axis] // 2
     a_ref[0] = z_ref.at[0][region(axis, slice(None), slice(0, half))]
     b_ref[0] = z_ref.at[0][region(axis, slice(None), slice(half, None))]
+
+
+def cut(order, value, axis, column, columns):
+    waits = order.take()
+    z, n, _ = value.shape
+    shape = (z, n, columns // 2) if axis == 0 else (z, n // 2, columns)
+    out = pl.pallas_call(
+        functools.partial(cut_kernel, axis),
+        grid=(z,),
+        in_specs=[pl.BlockSpec((1, n, columns), lambda j: (j, 0, column))]
+        + [pl.BlockSpec(memory_space=pl.ANY)] * len(waits),
+        out_specs=[pl.BlockSpec((1, *shape[1:]), lambda j: (j, 0, 0))] * 2,
+        out_shape=[jax.ShapeDtypeStruct(shape, BF16)] * 2,
+        compiler_params=params(),
+        cost_estimate=cost(order.long()),
+    )(value, *waits)
+    order.after(out[0])
+    return out
+
+
+def eighth(spot, shard, axis):
+    size = shard.shape[axis] // 8
+    seat = 4 * bit_of(spot, 1) + 2 * bit_of(spot, 4) + bit_of(spot, 2)
+    return lax.dynamic_slice_in_dim(shard, seat * size, size, axis)
 
 
 def pairs_kernel(axis, flags, *refs):
@@ -843,20 +864,17 @@
         ),
         out_shape=[jax.ShapeDtypeStruct(shape, BF16) for shape in shapes],
         compiler_params=params(),
-        cost_estimate=cost(2.5 + 1.1e-6 * sum(v.size for v in operands)),
+        cost_estimate=cost(order.long()),
     )(*flags, *operands, *waits)
     order.after(out[0])
     return out
 
 
 class Gather:
-    def __init__(self, order, spot, shard, axis):
+    def __init__(self, order, spot, value, axis, column=0, columns=None):
         self.order, self.axis = order, axis
         self.flags = [jnp.stack([bit_of(spot, b) for b in (2, 4, 1)])]
-        size = shard.shape[axis] // 8
-        seat = 4 * bit_of(spot, 1) + 2 * bit_of(spot, 4) + bit_of(spot, 2)
-        piece = lax.dynamic_slice_in_dim(shard, seat * size, size, axis)
-        self.value = lax.all_gather(piece, "fsdp", axis=0)
+        self.value, self.place = value, (column, columns or value.shape[2])
 
     def scaled(self, shape, along, across):
         shape = list(shape)
@@ -868,8 +886,7 @@
         return by_shard(self.order, kernel, self.axis, flags, operands, shapes)
 
     def one(self):
-        shape = self.scaled(self.value.shape, 1, 1)
-        self.a, self.b = self.run(cut_kernel, [], [self.value], [shape] * 2)
+        self.a, self.b = cut(self.order, self.value, self.axis, *self.place)
         self.got = swap(self.a, 2), swap(self.b, 4)
 
     def two(self):
@@ -908,82 +925,12 @@
     return out.reshape(-1, out.shape[-1])
 
 
-class Spread:
-    def __init__(self, order, spot, values):
-        self.order, self.spot = order, spot
-        self.values = values
-        self.bits = [(4, 2), (2, 4), (1, 1)]
-        self.send()
-
-    def send(self):
-        self.flights = [swap(v, b) for v, b in zip(self.values, self.bits[0])]
-
-    def land(self):
-        flags = [bit_of(self.spot, b) for b in self.bits.pop(0)]
-        pairs = list(zip(self.values, self.flights))
-        last = not self.bits
-        self.values = land_joins(
-            self.order, pairs, flags, 2 if last else 1, F32 if last else BF16
-        )
-        if not last:
-            self.send()
-
-
-def unpack_rows_kernel(v_ref, *refs):
-    gate_ref, up_ref = refs[-2:]
-    columns = gate_ref.shape[1]
-    gate_ref[...] = v_ref[0, :, :columns].astype(F32)
-    up_ref[...] = v_ref[0, :, columns:].astype(F32)
-
-
-def unpack_rows(order, value):
-    count, n, both = value.shape
-    c = both // 2
-    waits = order.take()
-    out = pl.pallas_call(
-        unpack_rows_kernel,
-        grid=(count,),
-        in_specs=[pl.BlockSpec((1, n, both), lambda j: (j, 0, 0))]
-        + [pl.BlockSpec(memory_space=pl.ANY)] * len(waits),
-        out_specs=[
-            pl.BlockSpec((n, c), lambda j: (4 * (j % 2) + 2 * (j // 2 % 2) + j // 4, 0)),
-            pl.BlockSpec((n, c), lambda j: (4 * (j % 2) + j // 2, 0)),
-        ],
-        out_shape=[jax.ShapeDtypeStruct((count * n, c), F32)] * 2,
-        compiler_params=params(),
-        cost_estimate=cost(6),
-    )(value, *waits)
-    order.after(out[0])
-    return out
-
-
-def unpack_columns_kernel(v_ref, *refs):
-    out_ref = refs[-1]
-    out_ref[...] = v_ref[0, : out_ref.shape[0], :].astype(F32)
-
-
-def unpack_columns(order, value, n):
-    count, held, c = value.shape
-    waits = order.take()
-    out = pl.pallas_call(
-        unpack_columns_kernel,
-        grid=(count,),
-        in_specs=[pl.BlockSpec((1, held, c), lambda j: (j, 0, 0))]
-        + [pl.BlockSpec(memory_space=pl.ANY)] * len(waits),
-        out_specs=pl.BlockSpec((n, c), lambda j: (0, 4 * (j % 2) + 2 * (j // 2 % 2) + j // 4)),
-        out_shape=jax.ShapeDtypeStruct((n, count * c), F32),
-        compiler_params=params(),
-        cost_estimate=cost(6),
-    )(value, *waits)
-    return order.after(out)
-
-
-def from_group(value):
-    return lax.all_gather(value, ("y", "x", "core"), axis=0)
-
-
-def over_groups(value):
+def over_shards(value):
     value = lax.psum_scatter(value, "fsdp", scatter_dimension=0, tiled=True)
+    return across_groups(value)
+
+
+def across_groups(value):
     size = lax.axis_size("group")
     ring = [(i, (i + 1) % size) for i in range(size)]
     total = step = value
@@ -991,6 +938,36 @@
         step = lax.ppermute(step, "group", ring)
         total = total + step
     return total
+
+
+class Spread:
+    def __init__(self, order, spot, value, parts, turned, axis=0):
+        self.order, self.spot, self.axis = order, spot, axis
+        self.value, self.parts, self.turned = value, parts, turned
+        self.bits = [4, 2, 1]
+        self.send()
+
+    def send(self):
+        self.flight = swap(self.value, self.bits[0])
+
+    def land(self):
+        bit = self.bits.pop(0)
+        last = not self.bits
+        out = land_join(
+            self.order,
+            self.value,
+            self.flight,
+            bit_of(self.spot, bit),
+            self.axis,
+            self.parts if last else [self.value.shape[1]],
+            self.turned if last else [False],
+            F32 if last else BF16,
+        )
+        if last:
+            self.values = out
+        else:
+            self.value = out[0]
+            self.send()
 
 
 def on_device(
@@ -1018,15 +995,32 @@
     keys = memory.shape[1]
     spot = 4 * lax.axis_index("y") + 2 * lax.axis_index("x") + lax.axis_index("core")
 
-    gains = lax.all_gather(jnp.stack([self_gain, cross_gain, mlp_gain]), "fsdp", axis=1, tiled=True)
-    gains = gains.astype(F32)
     order = Order()
-    gather = lambda shard, axis=0: Gather(order, spot, shard, axis)
     join = lambda *parts: jnp.concatenate(parts, axis=1)
-    g_down = gather(mlp_down, 1)
-    g_self = gather(join(self_query, self_key, self_value, self_output))
-    g_cross = gather(join(cross_key, cross_value, cross_query, cross_output))
-    g_wide = gather(join(mlp_gate, mlp_up))
+    gather = lambda value: lax.all_gather(value, "fsdp", axis=0)
+    g_down = Gather(order, spot, gather(eighth(spot, mlp_down, 1)), 1)
+    own = self_gain.shape[0]
+    lines = jnp.stack([self_gain, cross_gain, mlp_gain]).reshape(-1, 128)
+    squares = [
+        self_query,
+        self_key,
+        self_value,
+        self_output,
+        cross_key,
+        cross_value,
+        cross_query,
+        cross_output,
+    ]
+    lines = jnp.pad(lines, ((0, width // 32 - lines.shape[0]), (0, 0)))
+    both = gather(join(*[eighth(spot, w, 0) for w in squares], lines))
+    g_self = Gather(order, spot, both, 0, 0, 4 * width)
+    g_cross = Gather(order, spot, both, 0, 1, 4 * width)
+    shards = both.shape[0]
+    gains = both[:, : 3 * own // 128, 8 * width :].reshape(shards, 3, own)
+    gains = gains.transpose(1, 0, 2).reshape(3, width).astype(F32)
+    g_wide = Gather(
+        order, spot, gather(join(eighth(spot, mlp_gate, 0), eighth(spot, mlp_up, 0))), 0
+    )
     hidden = mlp_gate.shape[1]
 
     x = text.reshape(-1, width).astype(F32)
@@ -1037,12 +1031,15 @@
     g_down.one()
     g_down.two()
     g_self.one()
+    g_cross.one()
+    order.micros = C_LONG
     g_down.three()
     g_self.two()
+    g_cross.two()
+    order.micros = C_LONG
     w_down = g_down.four()
-    g_cross.one()
+    g_wide.one()
     g_self.three()
-    g_cross.two()
     w_self = g_self.four()
     w_qkv, w_so = w_self[:, : 3 * width], w_self[:, 3 * width :]
     c1 = factor_of(x)
@@ -1050,13 +1047,13 @@
     qkv = matmul(a1, w_qkv).astype(BF16).reshape(items, rows, 3 * width)
     o1, p1 = self_forward(qkv, text_lengths)
     o1 = order.after(o1).reshape(-1, width)
-    g_wide.one()
+    g_wide.two()
     g_cross.three()
-    g_wide.two()
     h1 = x + matmul(o1, w_so)
     c2 = factor_of(h1)
     a2 = (h1 * c2 * gains[1]).astype(BF16)
     order.after(a2)
+    order.micros = C_LONG
     w_cross = g_cross.four()
     w_kv = w_cross[:, : 2 * width]
     w_cq, w_co = w_cross[:, 2 * width : 3 * width], w_cross[:, 3 * width :]
@@ -1070,7 +1067,7 @@
     a3 = (h2 * c3 * gains[2]).astype(BF16)
     order.after(a3)
     w_wide = g_wide.four()
-    inner, d_wide = mlp(a3, e3, w_wide, w_down)
+    inner, d_wide = mlp(order, a3, e3, w_wide, w_down)
     order.take()
 
     sum_of = lambda first, second, pairs: Sum(
@@ -1081,14 +1078,13 @@
     s_down = Sum(order, spot, 1, functools.partial(grad_columns, order, inner, e3), 2, 4)
     s_gate.core()
     s_up.core()
+    order.micros = C_LONG
     d_h2, gg3, e2, d_o2 = segment(
         order, d_wide, w_wide, 0, hidden // 2, h2, e3, gains[2], (w_cross, 3)
     )
-    s_down.core()
     d_q2, d_kv = cross_backward(order, q2, kv, p2, d_o2.reshape(text.shape), mask)
     d_q2 = d_q2.reshape(-1, width)
     d_kv = d_kv.reshape(-1, 2 * width)
-    land_first(order, s_gate, s_up)
     s_cross = Pair(
         order,
         spot,
@@ -1098,14 +1094,13 @@
             (o2, e2, 0, width),
         ],
     )
+    s_down.core()
+    land_first(order, s_gate, s_up)
+    order.micros = C_LONG
     d_h1, gg2, e1, d_o1 = segment(
         order, d_q2, w_cross, 4, width // 2, h1, d_h2, gains[1], (w_self, 3)
     )
-    z_wide = over_groups(land_second(order, s_gate, s_up))
-    land_first(order, s_down)
-    cross = s_cross.core()
     d_qkv = self_backward(order, qkv, p1, d_o1.reshape(text.shape)).reshape(-1, 3 * width)
-    z_down = over_groups(land_second(order, s_down))
     s_self = Pair(
         order,
         spot,
@@ -1115,38 +1110,56 @@
             (o1, e1, 0, width),
         ],
     )
+    cross = s_cross.core()
+    land_first(order, s_down)
+    z_wide = over_shards(land_second(order, s_gate, s_up))
+    order.micros = C_LONG
+    grad_memory = back_product(order, d_kv, w_cross)
+    both = s_self.core()
     land_first(order, *cross)
+    z_down = over_shards(land_second(order, s_down))
+    order.micros = C_SEG1
+    grad_text, gg1 = segment(order, d_qkv, w_self, 0, width, x, d_h1, gains[0])
     z_wide = hold(order, z_wide)
-    all_wide = from_group(z_wide)
-    both = s_self.core()
-    grad_text, gg1 = segment(order, d_qkv, w_self, 0, width, x, d_h1, gains[0])
-    lines = jnp.concatenate([gg1, gg2, gg3]).astype(BF16).reshape(-1, width // 8)
-    z_down = hold(order, jnp.concatenate([z_down, jnp.pad(lines, ((0, 8), (0, 0)))]))
-    all_down = from_group(z_down)
-    z_cross = over_groups(land_second(order, *cross))
+    t_wide = Spread(order, spot, z_wide, [hidden, hidden], [False, True])
+    z_down = hold(order, z_down)
+    z_cross = over_shards(land_second(order, *cross))
     land_first(order, *both)
-    grad_memory = back_product(order, d_kv, w_cross)
-    g_gate, g_up = unpack_rows(order, all_wide)
+    lines = jnp.concatenate([gg1, gg2, gg3]).reshape(3, shards, own).transpose(1, 0, 2)
+    lines = lines.reshape(shards, -1, 128)
+    lines = jnp.pad(lines, ((0, 0), (0, width // 32 - lines.shape[1]), (0, 0)))
+    lines = order.after(lines.astype(BF16).reshape(-1, 128))
+    order.micros = C_LONG
+    t_wide.land()
+    z_self = land_second(order, *both)
+    z_self = over_shards(jnp.concatenate([z_self, lines], axis=1))
+    z_cross = hold(order, z_cross)
+    order.micros = C_LONG
     block_out = forward_out(order, inner, w_down, h2)
-    g_down = unpack_columns(order, all_down, mlp_down.shape[0])
-    lines = jnp.sum(all_down[:, mlp_down.shape[0] : -8].astype(F32), axis=0)
-    shards, own = lax.axis_size("fsdp"), self_gain.shape[0]
-    lines = lines.reshape(3, shards, own).transpose(1, 0, 2).reshape(shards, -1)
-    lines = jnp.pad(lines, ((0, 0), (0, 32 * 128 - 3 * own))).astype(BF16).reshape(-1, 128)
-    z_self = over_groups(jnp.concatenate([land_second(order, *both), lines], axis=1))
-    z_cross = hold(order, z_cross)
-    t_cross = Spread(order, spot, [z_cross[:, : 2 * width], z_cross[:, 2 * width :]])
+    squares = [width] * 4
+    t_cross = Spread(order, spot, z_cross, squares, [False, False, True, True])
+    t_down = Spread(order, spot, z_down, [width], [False], 1)
+    t_wide.land()
     t_cross.land()
+    t_down.land()
+    t_wide.land()
     t_cross.land()
+    z_self = hold(order, z_self)
+    t_self = Spread(
+        order, spot, z_self, [*squares, 128], [False, False, True, True, False]
+    )
+    t_down.land()
     t_cross.land()
-    g_ck, g_cv, g_cq, g_co = t_cross.values
-    z_self = hold(order, z_self)
-    t_self = Spread(order, spot, [z_self[:, : 2 * width], z_self[:, 2 * width : 4 * width]])
-    gg = z_self[:, 4 * width :].reshape(-1)[: 3 * own].reshape(3, own).astype(F32)
+    t_self.land()
+    t_down.land()
     t_self.land()
     t_self.land()
-    t_self.land()
-    g_sq, g_sk, g_sv, g_so = t_self.values
+    g_gate, g_up = t_wide.values
+    (g_down,) = t_down.values
+    g_ck, g_cv, g_cq, g_co = t_cross.values
+    g_sq, g_sk, g_sv, g_so, lines = t_self.values
+    lines = jnp.sum(lines.reshape(8, -1, 128), axis=0)
+    gg = lines[: 3 * own // 128].reshape(3, own)
 
     return (
         block_out.reshape(text.shape),

time: 695 us -> 649 us (0.934); the launches traced: 690 us -> 636 us
  waiting for transfers between devices: 170 us -> 114 us
  local copies, waits for them, and re-layouts: 32.2 us -> 52.7 us
  blocking collectives: 38.1 us -> 26.3 us
  other arithmetic: 20.1 us -> 11.6 us
    ppermute x51, waiting for transfers between devices: 167 us -> 90.1 us  [swap(): return lax.ppermute(value, AXES[bit], [(0, 1), (1, 0)])]
    unnamed x178 -> x164, local copies, waits for them, and re-layouts: 30.8 us -> 47 us
    reduce_scatter x4, waiting for transfers between devices: 0.04 us -> 15.6 us  [over_shards(): value = lax.psum_scatter(value, 'fsdp', scatter_dimension=0, tiled=True)]
    pallas_call x8 -> x16, Pallas kernels: 32.2 us -> 45.7 us  [the longest x12 32.2 us: land_join(): pl.pallas_call(functools.partial(join_kernel, axis, parts, turned), grid_...]
    pallas_call x16 -> x12, Pallas kernels: 85.6 us -> 72.2 us  [by_shard(): pl.pallas_call(functools.partial(kernel, axis), grid_spec=pltpu.PrefetchS...]
    all_gather x2 -> x1, blocking collectives: 38.1 us -> 26.3 us  [on_device(): gather = lambda value: lax.all_gather(value, 'fsdp', axis=0)]
  transfers between devices with their start and end apart: 60 -> 57, of which waited for: 31 -> 23; matrix products, arithmetic and copies ran while one was open for 7% -> 6% of each run, Pallas kernels for 38% -> 44%
where the time goes in v3:
time: 649 us; the launch traced here: 636 us
  Pallas kernels  345 us (53%)
  waiting for transfers between devices  114 us (18%)
  local copies, waits for them, and re-layouts  52.7 us (8%)
  starting transfers between devices  43.7 us (7%)
  matrix products  27.2 us (4%)
  blocking collectives  26.3 us (4%)
  between operations  15.1 us (2%)
  other arithmetic  11.6 us (2%)
    ppermute x51, waiting for transfers between devices, swap(): return lax.ppermute(value, AXES[bit], [(0, 1), (1, 0)])  90.1 us
    pallas_call x10, Pallas kernels, call_product(): pl.pallas_call(functools.partial(product_kernel, jobs, has_add, axis, len...  79.2 us
    pallas_call x12, Pallas kernels, by_shard(): pl.pallas_call(functools.partial(kernel, axis), grid_spec=pltpu.PrefetchS...  72.2 us
    unnamed x164, local copies, waits for them, and re-layouts  47 us
    ppermute x51, starting transfers between devices, swap(): return lax.ppermute(value, AXES[bit], [(0, 1), (1, 0)])  43.5 us
    pallas_call x3, Pallas kernels, segment(): pl.pallas_call(functools.partial(segment_kernel, steps, after is not None...  39.5 us
    pallas_call x12, Pallas kernels, land_join(): pl.pallas_call(functools.partial(join_kernel, axis, parts, turned), grid_...  32.2 us
    dot_general x5, matrix products, matmul(): return jnp.dot(left, right, preferred_element_type=F32)  27.2 us
  transfers between devices with their start and end apart: 57, of which 23 were waited for; matrix products, arithmetic and copies ran while one was open for 6% of the time, Pallas kernels for 44%

profile of v3, /device:TPU:0, one launch (start us, length us, event | category | flops | bytes accessed | tf_op | source)
XLA Modules:
  0.0 636.2 jit_solution(14178257308390633674)
XLA Ops:
  17.1 26.3 %all-gather.1 = bf16[2816,128]{1,0:T(8,128)(2,1)} all-gather(bf16[704,128]{1,0:T(8,128)(2,1)S(1)} %constant_dynamic-slice_fusion.2), channel_id=3, replica_groups=mesh['group'=1,'y'=2,'x'=2,'core'=2,'fsdp'=4] {'fsdp'}, dimensions={0}, use_global_device_ids=true | all-gather | bytes 901120 | tf_op jit(solution)/shard_map/all_gather | solution.py:1000
  56.5 4.3 shard_map.315
  63.1 7.2 %all-gather.6.cloned.1.call-done = bf16[128,8320]{1,0:T(8,128)(2,1)} async-done(((bf16[32,8320]{1,0:T(8,128)(2,1)}), bf16[128,8320]{1,0:T(8,128)(2,1)}) %all-gather.6.cloned.1.call-update) | async-done | bytes 2129936 | tf_op jit(solution)/shard_map/all_gather | solution.py:1000
  78.2 5.1 shard_map.318.refs_4_.own_ref
  89.3 9.8 %collective-permute-done.2.refs_1_ = bf16[4,32,2048]{2,1,0:T(8,128)(2,1)S(1)} collective-permute-done((bf16[4,32,2048]{2,1,0:T(8,128)(2,1)S(1)}, bf16[4,32,2048]{2,1,0:T(8,128)(2,1)S(1)}, u32[]{:S(2)}, u32[]{:S(2)}) %collective-permute-start.2) | collective-permute-done | bytes 524320 | tf_op jit(solution)/shard_map/ppermute | solution.py:264
  102.0 4.5 shard_map.319
  112.5 4.5 shard_map.320
  117.0 6.3 shard_map.321.refs_0_
  128.2 5.7 collective-permute-done.6.refs_1_
  135.2 5.5 shard_map.323.own_ref.refs_0_
  148.2 7.7 %shard_map.324.refs_4_ = bf16[4,256,4096]{2,1,0:T(8,128)(2,1)} custom-call(s32[3]{0:T(128)} %pad_add_fusion.flags, bf16[4,128,4096]{2,1,0:T(8,128)(2,1)} %shard_map.323.own_ref.refs_0_, bf16[4,128,4096]{2,1,0:T(8,128)(2,1)} %collective-permute-done.11.got_ref, bf16[4,128,4096]{2,1,0:T(8,128)(2,1)} %shard_map.323.own_ref.refs_0_), custom_call_target="tpu_custom_call" | custom-call | flops 115000000 | bytes 360000 | tf_op jit(solution)/shard_map/pallas_call | solution.py:856
  155.9 8.0 %fusion.2 = bf16[576,3072]{1,0:T(8,128)(2,1)} fusion(bf16[576,1024]{1,0:T(8,128)(2,1)S(1)} %get-tuple-element.163.refs_0_.refs_1_.refs_2_.refs_3_.refs_5_.refs_6_.refs_7_.refs_8_, bf16[1024,4096]{1,0:T(8,128)(2,1)} %bitcast.92), kind=kOutput, calls=%fused_computation.2 | convolution fusion | flops 3625648128 | bytes 11010048 | tf_op jit(solution)/shard_map/dot_general | solution.py:257
  163.9 9.6 %shard_map.325 = (bf16[4,144,1024]{2,1,0:T(8,128)(2,1)}, bf16[4,4,576,144]{3,2,1,0:T(8,128)(2,1)}) custom-call(s32[4]{0:T(128)} %lengths.1, bf16[4,144,3072]{2,1,0:T(8,128)(2,1)} %bitcast.103), custom_call_target="tpu_custom_call" | custom-call | flops 115000000 | bytes 360000 | tf_op jit(solution)/shard_map/pallas_call | solution.py:102
  173.5 11.4 %collective-permute-done.14.refs_1_ = bf16[4,32,2816]{2,1,0:T(8,128)(2,1)S(1)} collective-permute-done((bf16[4,32,2816]{2,1,0:T(8,128)(2,1)S(1)}, bf16[4,32,2816]{2,1,0:T(8,128)(2,1)S(1)}, u32[]{:S(2)}, u32[]{:S(2)}) %collective-permute-start.14) | collective-permute-done | bytes 720928 | tf_op jit(solution)/shard_map/ppermute | solution.py:264
  186.0 4.8 shard_map.326
  190.8 5.9 shard_map.327.own_ref.refs_0_
  205.1 7.9 %shard_map.328.refs_4_ = bf16[4,256,4096]{2,1,0:T(8,128)(2,1)} custom-call(s32[3]{0:T(128)} %pad_add_fusion.flags, bf16[4,128,4096]{2,1,0:T(8,128)(2,1)} %shard_map.327.own_ref.refs_0_, bf16[4,128,4096]{2,1,0:T(8,128)(2,1)} %collective-permute-done.16.got_ref, bf16[4,128,4096]{2,1,0:T(8,128)(2,1)} %shard_map.327.own_ref.refs_0_, ...), custom_call_target="tpu_custom_call" | custom-call | flops 115000000512 | bytes 360000000 | tf_op jit(solution)/shard_map/pallas_call | solution.py:856
  217.2 8.2 %fusion.7 = bf16[2048,1024]{0,1:T(8,128)(2,1)} fusion(bf16[1024,1024]{1,0:T(8,128)(2,1)S(1)} %bitcast.65, bf16[1024,4096]{1,0:T(8,128)(2,1)} %bitcast.117), kind=kOutput, calls=%fused_computation.5 | convolution fusion | flops 4297064448 | bytes 10485760 | tf_op jit(solution)/shard_map/dot_general | solution.py:257
  225.4 9.0 %shard_map.329 = (bf16[4,144,1024]{2,1,0:T(8,128)(2,1)}, bf16[4,4,576,256]{3,2,1,0:T(8,128)(2,1)}) custom-call(bf16[4,144,1024]{2,1,0:T(8,128)(2,1)} %bitcast.123, bf16[4,256,2048]{2,1,0:T(8,128)(2,1)} %bitcast.101, s32[4,1,256]{2,1,0:T(1,128)} %broadcast_in_dim.2.m_ref), custom_call_target="tpu_custom_call" | custom-call | flops 115000000 | bytes 360000 | tf_op jit(solution)/shard_map/pallas_call | solution.py:181
  235.5 6.3 shard_map.330.own_ref.refs_0_
  251.6 9.5 %shard_map.331 = bf16[4,256,5632]{2,1,0:T(8,128)(2,1)} custom-call(s32[3]{0:T(128)} %pad_add_fusion.flags, bf16[4,128,5632]{2,1,0:T(8,128)(2,1)} %shard_map.330.own_ref.refs_0_, bf16[4,128,5632]{2,1,0:T(8,128)(2,1)} %collective-permute-done.19.got_ref, bf16[4,128,5632]{2,1,0:T(8,128)(2,1)} %shard_map.330.own_ref.refs_0_, ...), custom_call_target="tpu_custom_call" | custom-call | flops 115000000 | bytes 360000 | tf_op jit(solution)/shard_map/pallas_call | solution.py:856
  261.1 19.9 %shard_map.332 = (bf16[576,2816]{1,0:T(8,128)(2,1)}, bf16[2,576,2816]{2,1,0:T(8,128)(2,1)}) custom-call(bf16[576,1024]{1,0:T(8,128)(2,1)} %multiply_convert_fusion.refs_1_.a_ref.refs_0_.refs_2_.refs_3_, bf16[576,1024]{1,0:T(8,128)(2,1)} %bitcast.108, bf16[1024,5632]{1,0:T(8,128)(2,1)} %bitcast.71, bf16[1024,5632]{1,0:T(8,128)(2,1)} %bitcast.72, ...), custom_call_target="tpu_custom_call" | custom-call | flops 115000000 | bytes 360000 | tf_op jit(solution)/shard_map/pallas_call | solution.py:635
  281.0 6.2 shard_map.333.refs_5_
  287.9 6.2 shard_map.334.refs_2_
  297.5 6.1 shard_map.335.refs_6_
  305.2 7.0 %shard_map.336 = (bf16[4,64,2816]{2,1,0:T(8,128)(2,1)}, bf16[4,64,2816]{2,1,0:T(8,128)(2,1)}) custom-call(s32[2]{0:T(128)} %pad_add_fusion.4.flags, bf16[576,1024]{1,0:T(8,128)(2,1)} %multiply_convert_fusion.refs_1_.a_ref.refs_0_.refs_2_.refs_3_, bf16[576,1024]{1,0:T(8,128)(2,1)} %multiply_convert_fusion.refs_1_.a_ref.refs_0_.refs_2_.refs_3_, ...), custom_call_target="tpu_custom_call" | custom-call | flops 115000000 | bytes 360000 | tf_op jit(solution)/shard_map/pallas_call | solution.py:360
  314.4 7.5 %shard_map.337 = (bf16[4,64,2816]{2,1,0:T(8,128)(2,1)}, bf16[4,64,2816]{2,1,0:T(8,128)(2,1)}) custom-call(s32[2]{0:T(128)} %pad_add_fusion.3.flags, bf16[576,1024]{1,0:T(8,128)(2,1)} %multiply_convert_fusion.refs_1_.a_ref.refs_0_.refs_2_.refs_3_, bf16[576,1024]{1,0:T(8,128)(2,1)} %multiply_convert_fusion.refs_1_.a_ref.refs_0_.refs_2_.refs_3_, ...), custom_call_target="tpu_custom_call" | custom-call | flops 115000000 | bytes 360000 | tf_op jit(solution)/shard_map/pallas_call | solution.py:360
  323.4 17.9 %shard_map.338 = (f32[576,1024]{1,0:T(8,128)}, f32[1,1024]{1,0:T(1,128)}, bf16[576,1024]{1,0:T(8,128)(2,1)}, bf16[576,1024]{1,0:T(8,128)(2,1)}) custom-call(bf16[2,576,2816]{2,1,0:T(8,128)(2,1)} %get-tuple-element.110.refs_4_.refs_0_, bf16[1024,5632]{1,0:T(8,128)(2,1)} %bitcast.73, f32[576,1024]{1,0:T(8,128)} %copy-done.27, bf16[576,1024]{1,0:T(8,128)(2,1)} %bitcast.110, ...), custom_call_target="tpu_custom_call" | custom-call | flops 115000000512 | bytes 360000000 | tf_op jit(solution)/shard_map/pallas_call | solution.py:600
  341.4 13.5 %shard_map.339 = (bf16[4,144,1024]{2,1,0:T(8,128)(2,1)}, bf16[4,256,2048]{2,1,0:T(8,128)(2,1)}) custom-call(bf16[4,144,1024]{2,1,0:T(8,128)(2,1)} %bitcast.124, bf16[4,256,2048]{2,1,0:T(8,128)(2,1)} %bitcast.102, bf16[4,4,576,256]{3,2,1,0:T(8,128)(2,1)} %get-tuple-element.109.p_ref, bf16[4,144,1024]{2,1,0:T(8,128)(2,1)} %bitcast.130, ...), custom_call_target="tpu_custom_call" | custom-call | flops 115000000 | bytes 360000 | tf_op jit(solution)/shard_map/pallas_call | solution.py:226
  354.9 9.6 %shard_map.340.refs_3_ = bf16[512,4096]{1,0:T(8,128)(2,1)} custom-call(s32[3]{0:T(128)} %add_add_fusion.1.flags, bf16[1024,1024]{1,0:T(8,128)(2,1)} %bitcast.57, bf16[1024,1024]{1,0:T(8,128)(2,1)} %bitcast.58, bf16[1024,1024]{1,0:T(8,128)(2,1)} %bitcast.59, bf16[1024,1024]{1,0:T(8,128)(2,1)} %bitcast.60, bf16[1024,2048]{1,0:T(8,128)(2,1)} %bitcast.98, ...), custom_call_target="tpu_custom_call" | custom-call | flops 115000000 | bytes 360000 | tf_op jit(solution)/shard_map/pallas_call | solution.py:360
  364.5 6.8 %shard_map.341 = (bf16[2816,256]{1,0:T(8,128)(2,1)}, bf16[2816,256]{1,0:T(8,128)(2,1)}) custom-call(s32[2]{0:T(128)} %pad_add_fusion.4.flags, bf16[576,2816]{1,0:T(8,128)(2,1)} %get-tuple-element.108.refs_0_.x_ref, bf16[576,1024]{1,0:T(8,128)(2,1)} %bitcast.111, bf16[2816,512]{1,0:T(8,128)(2,1)} %collective-permute-done.25.refs_2_, ...), custom_call_target="tpu_custom_call" | custom-call | flops 115000000 | bytes 360000 | tf_op jit(solution)/shard_map/pallas_call | solution.py:360
  374.3 4.6 shard_map.342
  380.1 10.4 %shard_map.343 = (f32[576,1024]{1,0:T(8,128)}, f32[1,1024]{1,0:T(1,128)}, bf16[576,1024]{1,0:T(8,128)(2,1)}, bf16[576,1024]{1,0:T(8,128)(2,1)}) custom-call(bf16[576,1024]{1,0:T(8,128)(2,1)} %bitcast.106, bf16[1024,4096]{1,0:T(8,128)(2,1)} %bitcast.120, f32[576,1024]{1,0:T(8,128)} %copy-done.29, f32[576,1024]{1,0:T(8,128)} %get-tuple-element.119.refs_3_, ...), custom_call_target="tpu_custom_call" | custom-call | flops 115000000512 | bytes 360000000 | tf_op jit(solution)/shard_map/pallas_call | solution.py:600
  390.5 11.5 %shard_map.344.refs_15_ = bf16[4,144,3072]{2,1,0:T(8,128)(2,1)} custom-call(bf16[4,144,3072]{2,1,0:T(8,128)(2,1)} %bitcast.104, bf16[4,4,576,144]{3,2,1,0:T(8,128)(2,1)} %get-tuple-element.118.p_ref, bf16[4,144,1024]{2,1,0:T(8,128)(2,1)} %bitcast.131, f32[1,1024]{1,0:T(1,128)} %get-tuple-element.125.refs_0_), custom_call_target="tpu_custom_call" | custom-call | flops 115000000 | bytes 360000 | tf_op jit(solution)/shard_map/pallas_call | solution.py:145
  402.0 8.8 %shard_map.345.refs_16_ = bf16[512,4096]{1,0:T(8,128)(2,1)} custom-call(s32[3]{0:T(128)} %add_add_fusion.1.flags, bf16[576,1024]{1,0:T(8,128)(2,1)} %copy-done.15, bf16[576,1024]{1,0:T(8,128)(2,1)} %copy-done.15, bf16[576,1024]{1,0:T(8,128)(2,1)} %copy-done.15, bf16[576,1024]{1,0:T(8,128)(2,1)} %copy-done.15, bf16[576,3072]{1,0:T(8,128)(2,1)} %bitcast.66, ...), custom_call_target="tpu_custom_call" | custom-call | flops 115000000 | bytes 360000 | tf_op jit(solution)/shard_map/pallas_call | solution.py:360
  412.9 10.9 %shard_map.346 = (bf16[4,64,2048]{2,1,0:T(8,128)(2,1)}, bf16[4,64,2048]{2,1,0:T(8,128)(2,1)}, bf16[4,64,2048]{2,1,0:T(8,128)(2,1)}, bf16[4,64,2048]{2,1,0:T(8,128)(2,1)}) custom-call(s32[3]{0:T(128)} %add_add_fusion.flags, bf16[1024,1024]{1,0:T(8,128)(2,1)} %bitcast.61, bf16[1024,1024]{1,0:T(8,128)(2,1)} %bitcast.62, bf16[1024,1024]{1,0:T(8,128)(2,1)} %bitcast.63, ...), custom_call_target="tpu_custom_call" | custom-call | flops 115000000 | bytes 360000 | tf_op jit(solution)/shard_map/pallas_call | solution.py:360
  434.5 9.3 %shard_map.349.refs_16_ = f32[1024,1024]{1,0:T(8,128)} custom-call(bf16[1024,2048]{1,0:T(8,128)(2,1)} %bitcast.100, bf16[1024,4096]{1,0:T(8,128)(2,1)} %bitcast.121, bf16[4,32,5632]{2,1,0:T(8,128)(2,1)} %shard_map.348.refs_0_), custom_call_target="tpu_custom_call" | custom-call | flops 115000000512 | bytes 360000000 | tf_op jit(solution)/shard_map/pallas_call | solution.py:709
  443.8 10.2 %shard_map.350 = (bf16[4,64,2048]{2,1,0:T(8,128)(2,1)}, bf16[4,64,2048]{2,1,0:T(8,128)(2,1)}, bf16[4,64,2048]{2,1,0:T(8,128)(2,1)}, bf16[4,64,2048]{2,1,0:T(8,128)(2,1)}) custom-call(s32[3]{0:T(128)} %add_add_fusion.flags, bf16[576,1024]{1,0:T(8,128)(2,1)} %copy-done.15, bf16[576,1024]{1,0:T(8,128)(2,1)} %copy-done.15, bf16[576,1024]{1,0:T(8,128)(2,1)} %copy-done.15, ...), custom_call_target="tpu_custom_call" | custom-call | flops 115000000 | bytes 360000 | tf_op jit(solution)/shard_map/pallas_call | solution.py:360
  469.3 11.2 %shard_map.353 = (f32[576,1024]{1,0:T(8,128)}, f32[1,1024]{1,0:T(1,128)}) custom-call(bf16[576,3072]{1,0:T(8,128)(2,1)} %bitcast.70, bf16[1024,4096]{1,0:T(8,128)(2,1)} %bitcast.95, f32[576,1024]{1,0:T(8,128)} %bitcast.128, f32[576,1024]{1,0:T(8,128)} %get-tuple-element.142.refs_3_, f32[1,1024]{1,0:T(1,128)} %bitcast.139, bf16[2816,128]{1,0:T(8,128)(2,1)} %shard_map.352.refs_5_), custom_call_target="tpu_custom_call" | custom-call | flops 23000000512 | bytes 72000000 | tf_op jit(solution)/shard_map/pallas_call | solution.py:600
  484.4 7.2 %reduce-scatter.5.cloned.1.call-done.refs_0_ = bf16[704,128]{1,0:T(8,128)(2,1)} async-done(((bf16[2816,128]{1,0:T(8,128)(2,1)}), bf16[704,128]{1,0:T(8,128)(2,1)}) %reduce-scatter.5.cloned.1.call-update) | async-done | bytes 180240 | tf_op jit(solution)/shard_map/reduce_scatter | solution.py:929
  512.1 6.9 %collective-permute-done.37.refs_1_ = bf16[4,32,2048]{2,1,0:T(8,128)(2,1)S(1)} collective-permute-done((bf16[4,32,2048]{2,1,0:T(8,128)(2,1)}, bf16[4,32,2048]{2,1,0:T(8,128)(2,1)S(1)}, u32[]{:S(2)}, u32[]{:S(2)}) %collective-permute-start.37) | collective-permute-done | bytes 524320 | tf_op jit(solution)/shard_map/ppermute | solution.py:264
  526.1 8.3 %reduce-scatter.9.cloned.1.call-done.refs_0_ = bf16[32,4096]{1,0:T(8,128)(2,1)} async-done(((bf16[128,4096]{1,0:T(8,128)(2,1)}), bf16[32,4096]{1,0:T(8,128)(2,1)}) %reduce-scatter.9.cloned.1.call-update) | async-done | bytes 262160 | tf_op jit(solution)/shard_map/reduce_scatter | solution.py:929
  537.3 8.6 %shard_map.361.refs_0_ = bf16[576,1024]{1,0:T(8,128)(2,1)} custom-call(bf16[576,2816]{1,0:T(8,128)(2,1)} %get-tuple-element.108.refs_0_.x_ref, bf16[2816,1024]{1,0:T(8,128)(2,1)} %bitcast.97, f32[576,1024]{1,0:T(8,128)} %copy-done.27, bf16[32,4096]{1,0:T(8,128)(2,1)} %copy-done.12), custom_call_target="tpu_custom_call" | custom-call | flops 115000000512 | bytes 360000000 | tf_op jit(solution)/shard_map/pallas_call | solution.py:682
  552.0 7.2 %collective-permute-done.40.got_ref = bf16[32,4096]{1,0:T(8,128)(2,1)S(1)} collective-permute-done((bf16[32,4096]{1,0:T(8,128)(2,1)S(1)}, bf16[32,4096]{1,0:T(8,128)(2,1)S(1)}, u32[]{:S(2)}, u32[]{:S(2)}) %collective-permute-start.40) | collective-permute-done | bytes 262176 | tf_op jit(solution)/shard_map/ppermute | solution.py:264
  564.7 4.5 collective-permute-done.44.got_ref
  572.8 4.7 shard_map.365
  584.9 6.6 %collective-permute-done.47.got_ref = bf16[704,256]{1,0:T(8,128)(2,1)S(1)} collective-permute-done((bf16[704,256]{1,0:T(8,128)(2,1)S(1)}, bf16[704,256]{1,0:T(8,128)(2,1)S(1)}, u32[]{:S(2)}, u32[]{:S(2)}) %collective-permute-start.47) | collective-permute-done | bytes 360480 | tf_op jit(solution)/shard_map/ppermute | solution.py:264
  606.1 10.4 %collective-permute-done.48.got_ref = bf16[64,4224]{1,0:T(8,128)(2,1)S(1)} collective-permute-done((bf16[64,4224]{1,0:T(8,128)(2,1)}, bf16[64,4224]{1,0:T(8,128)(2,1)S(1)}, u32[]{:S(2)}, u32[]{:S(2)}) %collective-permute-start.48) | collective-permute-done | bytes 540704 | tf_op jit(solution)/shard_map/ppermute | solution.py:264
  (340 shorter events, 211.5 us)
Async XLA Ops:
  7.2 63.2 %all-gather.6.cloned.1.call-start = ((), (), s32[]{:S(2)}) async-start(), calls=%async_computation.8 | async-start | bytes 2662400 | tf_op jit(solution)/shard_map/all_gather | solution.py:1000
  17.0 107.7 %all-gather.8.cloned.1.call-start = ((), (), s32[]{:S(2)}) async-start(), calls=%async_computation.9 | async-start | bytes 1802240 | tf_op jit(solution)/shard_map/all_gather | solution.py:1000
  60.8 16.2 %collective-permute-start.4 = (bf16[4,352,256]{2,1,0:T(8,128)(2,1)}, bf16[4,352,256]{2,1,0:T(8,128)(2,1)S(1)}, u32[]{:S(2)}, u32[]{:S(2)}) collective-permute-start(bf16[4,352,256]{2,1,0:T(8,128)(2,1)} %get-tuple-element.92.refs_0_), channel_id=1, source_target_pairs={{0,16},{16,0},{1,17},{17,1},{2,18},{18,2},{3,19},{19,3},{4,20},{20... | collective-permute-start | bytes 2162696 | tf_op jit(solution)/shard_map/ppermute | solution.py:264
  62.4 14.7 %collective-permute-start.5 = (bf16[4,352,256]{2,1,0:T(8,128)(2,1)}, bf16[4,352,256]{2,1,0:T(8,128)(2,1)S(1)}, u32[]{:S(2)}, u32[]{:S(2)}) collective-permute-start(bf16[4,352,256]{2,1,0:T(8,128)(2,1)} %get-tuple-element.95.refs_2_), channel_id=1, source_target_pairs={{0,8},{8,0},{1,9},{9,1},{2,10},{10,2},{3,11},{11,3},{4,12},{12,4},... | collective-permute-start | bytes 2162696 | tf_op jit(solution)/shard_map/ppermute | solution.py:264
  83.2 33.8 %collective-permute-start.8 = (bf16[4,704,512]{2,1,0:T(8,128)(2,1)}, bf16[4,704,512]{2,1,0:T(8,128)(2,1)}, u32[]{:S(2)}, u32[]{:S(2)}) collective-permute-start(bf16[4,704,512]{2,1,0:T(8,128)(2,1)} %shard_map.318.refs_4_.own_ref), channel_id=1, source_target_pairs={{0,4},{4,0},{1,5},{5,1},{2,6},{6,2},{3,7},{7,3},{8,12},{12,8},{9,1... | collective-permute-start | bytes 8650760 | tf_op jit(solution)/shard_map/ppermute | solution.py:264
  84.3 14.8 %collective-permute-start.2 = (bf16[4,32,2048]{2,1,0:T(8,128)(2,1)S(1)}, bf16[4,32,2048]{2,1,0:T(8,128)(2,1)S(1)}, u32[]{:S(2)}, u32[]{:S(2)}) collective-permute-start(bf16[4,32,2048]{2,1,0:T(8,128)(2,1)S(1)} %copy-done.30), channel_id=1, source_target_pairs={{0,8},{8,0},{1,9},{9,1},{2,10},{10,2},{3,11},{11,3},{4,12},{12,4},... | collective-permute-start | bytes 1572872 | tf_op jit(solution)/shard_map/ppermute | solution.py:264
  85.9 26.7 %collective-permute-start.9 = (bf16[4,32,2048]{2,1,0:T(8,128)(2,1)S(1)}, bf16[4,32,2048]{2,1,0:T(8,128)(2,1)}, u32[]{:S(2)}, u32[]{:S(2)}) collective-permute-start(bf16[4,32,2048]{2,1,0:T(8,128)(2,1)S(1)} %copy-done.57), channel_id=1, source_target_pairs={{0,8},{8,0},{1,9},{9,1},{2,10},{10,2},{3,11},{11,3},{4,12},{12,4},... | collective-permute-start | bytes 1572872 | tf_op jit(solution)/shard_map/ppermute | solution.py:264
  86.4 14.8 %collective-permute-start.3 = (bf16[4,32,2048]{2,1,0:T(8,128)(2,1)S(1)}, bf16[4,32,2048]{2,1,0:T(8,128)(2,1)S(1)}, u32[]{:S(2)}, u32[]{:S(2)}) collective-permute-start(bf16[4,32,2048]{2,1,0:T(8,128)(2,1)S(1)} %copy-done.53), channel_id=1, source_target_pairs={{0,16},{16,0},{1,17},{17,1},{2,18},{18,2},{3,19},{19,3},{4,20},{20... | collective-permute-start | bytes 1572872 | tf_op jit(solution)/shard_map/ppermute | solution.py:264
  87.9 24.6 %collective-permute-start.10 = (bf16[4,32,2048]{2,1,0:T(8,128)(2,1)S(1)}, bf16[4,32,2048]{2,1,0:T(8,128)(2,1)}, u32[]{:S(2)}, u32[]{:S(2)}) collective-permute-start(bf16[4,32,2048]{2,1,0:T(8,128)(2,1)S(1)} %copy-done.58), channel_id=1, source_target_pairs={{0,16},{16,0},{1,17},{17,1},{2,18},{18,2},{3,19},{19,3},{4,20},{20... | collective-permute-start | bytes 1572872 | tf_op jit(solution)/shard_map/ppermute | solution.py:264
  89.2 391.3 %reduce-scatter.7.cloned.1.call-start = ((), (), s32[]{:S(2)}) async-start(), calls=%async_computation.5 | async-start | bytes 1802240 | tf_op jit(solution)/shard_map/reduce_scatter | solution.py:929
  106.5 27.4 %collective-permute-start.6 = (bf16[4,64,2048]{2,1,0:T(8,128)(2,1)}, bf16[4,64,2048]{2,1,0:T(8,128)(2,1)S(1)}, u32[]{:S(2)}, u32[]{:S(2)}) collective-permute-start(bf16[4,64,2048]{2,1,0:T(8,128)(2,1)} %get-tuple-element.97.refs_4_.refs_0_), channel_id=1, source_target_pairs={{0,16},{16,0},{1,17},{17,1},{2,18},{18,2},{3,19},{19,3},{4,20},{20... | collective-permute-start | bytes 3145736 | tf_op jit(solution)/shard_map/ppermute | solution.py:264
  108.0 25.9 %collective-permute-start.7 = (bf16[4,64,2048]{2,1,0:T(8,128)(2,1)}, bf16[4,64,2048]{2,1,0:T(8,128)(2,1)S(1)}, u32[]{:S(2)}, u32[]{:S(2)}) collective-permute-start(bf16[4,64,2048]{2,1,0:T(8,128)(2,1)} %get-tuple-element.98.refs_2_), channel_id=1, source_target_pairs={{0,8},{8,0},{1,9},{9,1},{2,10},{10,2},{3,11},{11,3},{4,12},{12,4},... | collective-permute-start | bytes 3145736 | tf_op jit(solution)/shard_map/ppermute | solution.py:264
  142.4 48.4 %collective-permute-start.12 = (bf16[4,64,2048]{2,1,0:T(8,128)(2,1)}, bf16[4,64,2048]{2,1,0:T(8,128)(2,1)}, u32[]{:S(2)}, u32[]{:S(2)}) collective-permute-start(bf16[4,64,2048]{2,1,0:T(8,128)(2,1)} %get-tuple-element.100.refs_0_), channel_id=1, source_target_pairs={{0,16},{16,0},{1,17},{17,1},{2,18},{18,2},{3,19},{19,3},{4,20},{20... | collective-permute-start | bytes 3145736 | tf_op jit(solution)/shard_map/ppermute | solution.py:264
  143.9 46.9 %collective-permute-start.13 = (bf16[4,64,2048]{2,1,0:T(8,128)(2,1)}, bf16[4,64,2048]{2,1,0:T(8,128)(2,1)}, u32[]{:S(2)}, u32[]{:S(2)}) collective-permute-start(bf16[4,64,2048]{2,1,0:T(8,128)(2,1)} %get-tuple-element.103.refs_2_), channel_id=1, source_target_pairs={{0,8},{8,0},{1,9},{9,1},{2,10},{10,2},{3,11},{11,3},{4,12},{12,4},... | collective-permute-start | bytes 3145736 | tf_op jit(solution)/shard_map/ppermute | solution.py:264
  146.5 38.3 %collective-permute-start.14 = (bf16[4,32,2816]{2,1,0:T(8,128)(2,1)S(1)}, bf16[4,32,2816]{2,1,0:T(8,128)(2,1)S(1)}, u32[]{:S(2)}, u32[]{:S(2)}) collective-permute-start(bf16[4,32,2816]{2,1,0:T(8,128)(2,1)S(1)} %copy-done.26), channel_id=1, source_target_pairs={{0,8},{8,0},{1,9},{9,1},{2,10},{10,2},{3,11},{11,3},{4,12},{12,4},... | collective-permute-start | bytes 2162696 | tf_op jit(solution)/shard_map/ppermute | solution.py:264
  147.1 37.8 %collective-permute-start.15 = (bf16[4,32,2816]{2,1,0:T(8,128)(2,1)S(1)}, bf16[4,32,2816]{2,1,0:T(8,128)(2,1)S(1)}, u32[]{:S(2)}, u32[]{:S(2)}) collective-permute-start(bf16[4,32,2816]{2,1,0:T(8,128)(2,1)S(1)} %copy-done.45), channel_id=1, source_target_pairs={{0,16},{16,0},{1,17},{17,1},{2,18},{18,2},{3,19},{19,3},{4,20},{20... | collective-permute-start | bytes 2162696 | tf_op jit(solution)/shard_map/ppermute | solution.py:264
  197.3 37.1 %collective-permute-start.17 = (bf16[4,64,2816]{2,1,0:T(8,128)(2,1)S(1)}, bf16[4,64,2816]{2,1,0:T(8,128)(2,1)S(1)}, u32[]{:S(2)}, u32[]{:S(2)}) collective-permute-start(bf16[4,64,2816]{2,1,0:T(8,128)(2,1)S(1)} %copy-done.20), channel_id=1, source_target_pairs={{0,16},{16,0},{1,17},{17,1},{2,18},{18,2},{3,19},{19,3},{4,20},{20... | collective-permute-start | bytes 4325384 | tf_op jit(solution)/shard_map/ppermute | solution.py:264
  197.8 36.6 %collective-permute-start.18 = (bf16[4,64,2816]{2,1,0:T(8,128)(2,1)S(1)}, bf16[4,64,2816]{2,1,0:T(8,128)(2,1)}, u32[]{:S(2)}, u32[]{:S(2)}) collective-permute-start(bf16[4,64,2816]{2,1,0:T(8,128)(2,1)S(1)} %copy-done.34), channel_id=1, source_target_pairs={{0,8},{8,0},{1,9},{9,1},{2,10},{10,2},{3,11},{11,3},{4,12},{12,4},... | collective-permute-start | bytes 4325384 | tf_op jit(solution)/shard_map/ppermute | solution.py:264
  287.2 16.5 %collective-permute-start.21 = (bf16[512,2816]{1,0:T(8,128)(2,1)}, bf16[512,2816]{1,0:T(8,128)(2,1)S(1)}, u32[]{:S(2)}, u32[]{:S(2)}) collective-permute-start(bf16[512,2816]{1,0:T(8,128)(2,1)} %shard_map.333.refs_5_), channel_id=1, source_target_pairs={{0,4},{4,0},{1,5},{5,1},{2,6},{6,2},{3,7},{7,3},{8,12},{12,8},{9,1... | collective-permute-start | bytes 8650760 | tf_op jit(solution)/shard_map/ppermute | solution.py:264
  294.1 18.7 %collective-permute-start.20 = (bf16[512,2816]{1,0:T(8,128)(2,1)}, bf16[512,2816]{1,0:T(8,128)(2,1)S(1)}, u32[]{:S(2)}, u32[]{:S(2)}) collective-permute-start(bf16[512,2816]{1,0:T(8,128)(2,1)} %shard_map.334.refs_2_), channel_id=1, source_target_pairs={{0,4},{4,0},{1,5},{5,1},{2,6},{6,2},{3,7},{7,3},{8,12},{12,8},{9,1... | collective-permute-start | bytes 8650760 | tf_op jit(solution)/shard_map/ppermute | solution.py:264
  303.6 60.9 %collective-permute-start.25 = (bf16[2816,512]{1,0:T(8,128)(2,1)}, bf16[2816,512]{1,0:T(8,128)(2,1)}, u32[]{:S(2)}, u32[]{:S(2)}) collective-permute-start(bf16[2816,512]{1,0:T(8,128)(2,1)} %shard_map.335.refs_6_), channel_id=1, source_target_pairs={{0,4},{4,0},{1,5},{5,1},{2,6},{6,2},{3,7},{7,3},{8,12},{12,8},{9,1... | collective-permute-start | bytes 8650760 | tf_op jit(solution)/shard_map/ppermute | solution.py:264
  312.3 60.5 %collective-permute-start.23 = (bf16[4,64,2816]{2,1,0:T(8,128)(2,1)}, bf16[4,64,2816]{2,1,0:T(8,128)(2,1)S(1)}, u32[]{:S(2)}, u32[]{:S(2)}) collective-permute-start(bf16[4,64,2816]{2,1,0:T(8,128)(2,1)} %get-tuple-element.111.refs_6_), channel_id=1, source_target_pairs={{0,8},{8,0},{1,9},{9,1},{2,10},{10,2},{3,11},{11,3},{4,12},{12,4},... | collective-permute-start | bytes 4325384 | tf_op jit(solution)/shard_map/ppermute | solution.py:264
  321.9 50.8 %collective-permute-start.24 = (bf16[4,64,2816]{2,1,0:T(8,128)(2,1)}, bf16[4,64,2816]{2,1,0:T(8,128)(2,1)S(1)}, u32[]{:S(2)}, u32[]{:S(2)}) collective-permute-start(bf16[4,64,2816]{2,1,0:T(8,128)(2,1)} %get-tuple-element.112.refs_6_), channel_id=1, source_target_pairs={{0,16},{16,0},{1,17},{17,1},{2,18},{18,2},{3,19},{19,3},{4,20},{20... | collective-permute-start | bytes 4325384 | tf_op jit(solution)/shard_map/ppermute | solution.py:264
  364.5 46.4 %collective-permute-start.22 = (bf16[512,4096]{1,0:T(8,128)(2,1)}, bf16[512,4096]{1,0:T(8,128)(2,1)S(1)}, u32[]{:S(2)}, u32[]{:S(2)}) collective-permute-start(bf16[512,4096]{1,0:T(8,128)(2,1)} %shard_map.340.refs_3_), channel_id=1, source_target_pairs={{0,4},{4,0},{1,5},{5,1},{2,6},{6,2},{3,7},{7,3},{8,12},{12,8},{9,1... | collective-permute-start | bytes 12582920 | tf_op jit(solution)/shard_map/ppermute | solution.py:264
  371.3 54.1 %collective-permute-start.31 = (bf16[2816,256]{1,0:T(8,128)(2,1)}, bf16[2816,256]{1,0:T(8,128)(2,1)}, u32[]{:S(2)}, u32[]{:S(2)}) collective-permute-start(bf16[2816,256]{1,0:T(8,128)(2,1)} %get-tuple-element.122.refs_4_), channel_id=1, source_target_pairs={{0,8},{8,0},{1,9},{9,1},{2,10},{10,2},{3,11},{11,3},{4,12},{12,4},... | collective-permute-start | bytes 4325384 | tf_op jit(solution)/shard_map/ppermute | solution.py:264
  379.0 50.7 %collective-permute-start.29 = (bf16[4,32,2816]{2,1,0:T(8,128)(2,1)}, bf16[4,32,2816]{2,1,0:T(8,128)(2,1)S(1)}, u32[]{:S(2)}, u32[]{:S(2)}) collective-permute-start(bf16[4,32,2816]{2,1,0:T(8,128)(2,1)} %get-tuple-element.123.refs_6_), channel_id=1, source_target_pairs={{0,16},{16,0},{1,17},{17,1},{2,18},{18,2},{3,19},{19,3},{4,20},{20... | collective-permute-start | bytes 2162696 | tf_op jit(solution)/shard_map/ppermute | solution.py:264
  379.5 50.7 %collective-permute-start.30 = (bf16[4,32,2816]{2,1,0:T(8,128)(2,1)}, bf16[4,32,2816]{2,1,0:T(8,128)(2,1)S(1)}, u32[]{:S(2)}, u32[]{:S(2)}) collective-permute-start(bf16[4,32,2816]{2,1,0:T(8,128)(2,1)} %get-tuple-element.133), channel_id=1, source_target_pairs={{0,8},{8,0},{1,9},{9,1},{2,10},{10,2},{3,11},{11,3},{4,12},{12,4},... | collective-permute-start | bytes 2162696 | tf_op jit(solution)/shard_map/ppermute | solution.py:264
  410.9 32.9 %collective-permute-start.28 = (bf16[512,4096]{1,0:T(8,128)(2,1)}, bf16[512,4096]{1,0:T(8,128)(2,1)}, u32[]{:S(2)}, u32[]{:S(2)}) collective-permute-start(bf16[512,4096]{1,0:T(8,128)(2,1)} %shard_map.345.refs_16_), channel_id=1, source_target_pairs={{0,4},{4,0},{1,5},{5,1},{2,6},{6,2},{3,7},{7,3},{8,12},{12,8},{9,1... | collective-permute-start | bytes 12582920 | tf_op jit(solution)/shard_map/ppermute | solution.py:264
  423.8 30.9 %collective-permute-start.26 = (bf16[4,64,2048]{2,1,0:T(8,128)(2,1)}, bf16[4,64,2048]{2,1,0:T(8,128)(2,1)S(1)}, u32[]{:S(2)}, u32[]{:S(2)}) collective-permute-start(bf16[4,64,2048]{2,1,0:T(8,128)(2,1)} %get-tuple-element.128.refs_2_), channel_id=1, source_target_pairs={{0,8},{8,0},{1,9},{9,1},{2,10},{10,2},{3,11},{11,3},{4,12},{12,4},... | collective-permute-start | bytes 3145736 | tf_op jit(solution)/shard_map/ppermute | solution.py:264
  425.3 29.4 %collective-permute-start.27 = (bf16[4,64,2048]{2,1,0:T(8,128)(2,1)}, bf16[4,64,2048]{2,1,0:T(8,128)(2,1)S(1)}, u32[]{:S(2)}, u32[]{:S(2)}) collective-permute-start(bf16[4,64,2048]{2,1,0:T(8,128)(2,1)} %get-tuple-element.130), channel_id=1, source_target_pairs={{0,16},{16,0},{1,17},{17,1},{2,18},{18,2},{3,19},{19,3},{4,20},{20... | collective-permute-start | bytes 3145736 | tf_op jit(solution)/shard_map/ppermute | solution.py:264
  429.6 37.5 %collective-permute-start.34 = (bf16[2816,128]{1,0:T(8,128)(2,1)}, bf16[2816,128]{1,0:T(8,128)(2,1)}, u32[]{:S(2)}, u32[]{:S(2)}) collective-permute-start(bf16[2816,128]{1,0:T(8,128)(2,1)} %get-tuple-element.135.refs_4_), channel_id=1, source_target_pairs={{0,16},{16,0},{1,17},{17,1},{2,18},{18,2},{3,19},{19,3},{4,20},{20... | collective-permute-start | bytes 2162696 | tf_op jit(solution)/shard_map/ppermute | solution.py:264
  434.5 57.2 %reduce-scatter.5.cloned.1.call-start = ((), (), s32[]{:S(2)}) async-start(), calls=%async_computation.4 | async-start | bytes 901120 | tf_op jit(solution)/shard_map/reduce_scatter | solution.py:929
  454.0 43.1 %collective-permute-start.35 = (bf16[4,64,2048]{2,1,0:T(8,128)(2,1)}, bf16[4,64,2048]{2,1,0:T(8,128)(2,1)S(1)}, u32[]{:S(2)}, u32[]{:S(2)}) collective-permute-start(bf16[4,64,2048]{2,1,0:T(8,128)(2,1)} %get-tuple-element.136.refs_4_), channel_id=1, source_target_pairs={{0,8},{8,0},{1,9},{9,1},{2,10},{10,2},{3,11},{11,3},{4,12},{12,4},... | collective-permute-start | bytes 3145736 | tf_op jit(solution)/shard_map/ppermute | solution.py:264
  460.0 33.2 %collective-permute-start.32 = (bf16[4,32,2048]{2,1,0:T(8,128)(2,1)}, bf16[4,32,2048]{2,1,0:T(8,128)(2,1)S(1)}, u32[]{:S(2)}, u32[]{:S(2)}) collective-permute-start(bf16[4,32,2048]{2,1,0:T(8,128)(2,1)} %get-tuple-element.138.refs_2_), channel_id=1, source_target_pairs={{0,16},{16,0},{1,17},{17,1},{2,18},{18,2},{3,19},{19,3},{4,20},{20... | collective-permute-start | bytes 1572872 | tf_op jit(solution)/shard_map/ppermute | solution.py:264
  461.5 31.8 %collective-permute-start.33 = (bf16[4,32,2048]{2,1,0:T(8,128)(2,1)}, bf16[4,32,2048]{2,1,0:T(8,128)(2,1)}, u32[]{:S(2)}, u32[]{:S(2)}) collective-permute-start(bf16[4,32,2048]{2,1,0:T(8,128)(2,1)} %get-tuple-element.140), channel_id=1, source_target_pairs={{0,8},{8,0},{1,9},{9,1},{2,10},{10,2},{3,11},{11,3},{4,12},{12,4},... | collective-permute-start | bytes 1572872 | tf_op jit(solution)/shard_map/ppermute | solution.py:264
  462.9 37.8 %collective-permute-start.36 = (bf16[4,64,2048]{2,1,0:T(8,128)(2,1)}, bf16[4,64,2048]{2,1,0:T(8,128)(2,1)S(1)}, u32[]{:S(2)}, u32[]{:S(2)}) collective-permute-start(bf16[4,64,2048]{2,1,0:T(8,128)(2,1)} %get-tuple-element.146), channel_id=1, source_target_pairs={{0,16},{16,0},{1,17},{17,1},{2,18},{18,2},{3,19},{19,3},{4,20},{20... | collective-permute-start | bytes 3145736 | tf_op jit(solution)/shard_map/ppermute | solution.py:264
  469.2 65.2 %reduce-scatter.9.cloned.1.call-start = ((), (), s32[]{:S(2)}) async-start(), calls=%async_computation.6 | async-start | bytes 1310720 | tf_op jit(solution)/shard_map/reduce_scatter | solution.py:929
  482.2 26.0 %collective-permute-start.39 = (bf16[32,5632]{1,0:T(8,128)(2,1)S(1)}, bf16[32,5632]{1,0:T(8,128)(2,1)S(1)}, u32[]{:S(2)}, u32[]{:S(2)}) collective-permute-start(bf16[32,5632]{1,0:T(8,128)(2,1)S(1)} %shard_map.354.refs_1_.own_ref), channel_id=1, source_target_pairs={{0,16},{16,0},{1,17},{17,1},{2,18},{18,2},{3,19},{19,3},{4,20},{20... | collective-permute-start | bytes 1081352 | tf_op jit(solution)/shard_map/ppermute | solution.py:264
  505.6 13.3 %collective-permute-start.37 = (bf16[4,32,2048]{2,1,0:T(8,128)(2,1)}, bf16[4,32,2048]{2,1,0:T(8,128)(2,1)S(1)}, u32[]{:S(2)}, u32[]{:S(2)}) collective-permute-start(bf16[4,32,2048]{2,1,0:T(8,128)(2,1)} %get-tuple-element.148.refs_0_), channel_id=1, source_target_pairs={{0,16},{16,0},{1,17},{17,1},{2,18},{18,2},{3,19},{19,3},{4,20},{20... | collective-permute-start | bytes 1572872 | tf_op jit(solution)/shard_map/ppermute | solution.py:264
  507.2 15.1 %collective-permute-start.38 = (bf16[4,32,2048]{2,1,0:T(8,128)(2,1)}, bf16[4,32,2048]{2,1,0:T(8,128)(2,1)S(1)}, u32[]{:S(2)}, u32[]{:S(2)}) collective-permute-start(bf16[4,32,2048]{2,1,0:T(8,128)(2,1)} %get-tuple-element.150), channel_id=1, source_target_pairs={{0,8},{8,0},{1,9},{9,1},{2,10},{10,2},{3,11},{11,3},{4,12},{12,4},... | collective-permute-start | bytes 1572872 | tf_op jit(solution)/shard_map/ppermute | solution.py:264
  507.8 73.4 %reduce-scatter.11.cloned.1.call-start = ((), (), s32[]{:S(2)}) async-start(), calls=%async_computation.7 | async-start | bytes 1351680 | tf_op jit(solution)/shard_map/reduce_scatter | solution.py:929
  510.9 35.1 %collective-permute-start.41 = (bf16[64,5632]{1,0:T(8,128)(2,1)}, bf16[64,5632]{1,0:T(8,128)(2,1)S(1)}, u32[]{:S(2)}, u32[]{:S(2)}) collective-permute-start(bf16[64,5632]{1,0:T(8,128)(2,1)} %shard_map.358.refs_4_.own_ref), channel_id=1, source_target_pairs={{0,8},{8,0},{1,9},{9,1},{2,10},{10,2},{3,11},{11,3},{4,12},{12,4},... | collective-permute-start | bytes 2162696 | tf_op jit(solution)/shard_map/ppermute | solution.py:264
  549.3 22.4 %collective-permute-start.43 = (bf16[128,5632]{1,0:T(8,128)(2,1)}, bf16[128,5632]{1,0:T(8,128)(2,1)S(1)}, u32[]{:S(2)}, u32[]{:S(2)}) collective-permute-start(bf16[128,5632]{1,0:T(8,128)(2,1)} %shard_map.362.refs_0_.own_ref), channel_id=1, source_target_pairs={{0,4},{4,0},{1,5},{5,1},{2,6},{6,2},{3,7},{7,3},{8,12},{12,8},{9,1... | collective-permute-start | bytes 4325384 | tf_op jit(solution)/shard_map/ppermute | solution.py:264
  561.8 15.8 %collective-permute-start.42 = (bf16[64,4096]{1,0:T(8,128)(2,1)}, bf16[64,4096]{1,0:T(8,128)(2,1)S(1)}, u32[]{:S(2)}, u32[]{:S(2)}) collective-permute-start(bf16[64,4096]{1,0:T(8,128)(2,1)} %shard_map.363.refs_0_.own_ref), channel_id=1, source_target_pairs={{0,8},{8,0},{1,9},{9,1},{2,10},{10,2},{3,11},{11,3},{4,12},{12,4},... | collective-permute-start | bytes 1572872 | tf_op jit(solution)/shard_map/ppermute | solution.py:264
  580.6 13.6 %collective-permute-start.46 = (bf16[128,4096]{1,0:T(8,128)(2,1)}, bf16[128,4096]{1,0:T(8,128)(2,1)S(1)}, u32[]{:S(2)}, u32[]{:S(2)}) collective-permute-start(bf16[128,4096]{1,0:T(8,128)(2,1)} %shard_map.366.refs_1_.own_ref), channel_id=1, source_target_pairs={{0,4},{4,0},{1,5},{5,1},{2,6},{6,2},{3,7},{7,3},{8,12},{12,8},{9,1... | collective-permute-start | bytes 3145736 | tf_op jit(solution)/shard_map/ppermute | solution.py:264
  580.6 10.8 %collective-permute-start.47 = (bf16[704,256]{1,0:T(8,128)(2,1)S(1)}, bf16[704,256]{1,0:T(8,128)(2,1)S(1)}, u32[]{:S(2)}, u32[]{:S(2)}) collective-permute-start(bf16[704,256]{1,0:T(8,128)(2,1)S(1)} %copy-done.23), channel_id=1, source_target_pairs={{0,8},{8,0},{1,9},{9,1},{2,10},{10,2},{3,11},{11,3},{4,12},{12,4},... | collective-permute-start | bytes 1081352 | tf_op jit(solution)/shard_map/ppermute | solution.py:264
  583.4 15.6 %collective-permute-start.45 = (bf16[32,4224]{1,0:T(8,128)(2,1)S(1)}, bf16[32,4224]{1,0:T(8,128)(2,1)S(1)}, u32[]{:S(2)}, u32[]{:S(2)}) collective-permute-start(bf16[32,4224]{1,0:T(8,128)(2,1)S(1)} %shard_map.367.refs_0_.own_ref), channel_id=1, source_target_pairs={{0,16},{16,0},{1,17},{17,1},{2,18},{18,2},{3,19},{19,3},{4,20},{20... | collective-permute-start | bytes 811016 | tf_op jit(solution)/shard_map/ppermute | solution.py:264
  601.6 14.9 %collective-permute-start.48 = (bf16[64,4224]{1,0:T(8,128)(2,1)}, bf16[64,4224]{1,0:T(8,128)(2,1)S(1)}, u32[]{:S(2)}, u32[]{:S(2)}) collective-permute-start(bf16[64,4224]{1,0:T(8,128)(2,1)} %shard_map.370.refs_0_.own_ref), channel_id=1, source_target_pairs={{0,8},{8,0},{1,9},{9,1},{2,10},{10,2},{3,11},{11,3},{4,12},{12,4},... | collective-permute-start | bytes 1622024 | tf_op jit(solution)/shard_map/ppermute | solution.py:264
  (87 other events, 442.6 us)
Sparse Core Ops, SparseCore 0:
  17.1 53.2 all-gather.5
  89.3 35.3 all-gather.7
  434.6 32.6 reduce-scatter.6
  470.0 21.6 reduce-scatter.4
  507.9 26.4 reduce-scatter.8
  550.6 26.4 reduce-scatter.10

commit v4 on v3

--- a/solution.py
+++ b/solution.py
@@ -16,7 +16,9 @@
 VMEM_LIMIT = 56 * 1024 * 1024
 
 C_LONG = 100
-C_SEG1 = 20
+MLP_TILE = 256
+C_SEG2 = 11
+C_MID = 8
 
 BF16 = jnp.bfloat16
 F32 = jnp.float32
@@ -528,25 +530,30 @@
     return out
 
 
-def segment_kernel(steps, has_next, waits, *refs):
+def segment_kernel(steps, has_next, split, waits, flag, *refs):
     x_ref, w_ref, v_ref, b_ref, g_ref = refs[:5]
     n_ref = refs[5] if has_next else None
-    refs = refs[5 + has_next + waits :]
+    u_ref = refs[5 + has_next] if split else None
+    refs = refs[5 + has_next + split + waits :]
     if has_next:
         d_ref, gg_ref, e_ref, o_ref, acc = refs
     else:
         d_ref, gg_ref, acc = refs
     step = pl.program_id(0)
     x = x_ref[0] if len(x_ref.shape) == 3 else x_ref[...]
-    partial = dot(x, w_ref[...], ((1,), (1,)))
-
-    @pl.when(step == 0)
-    def _():
-        acc[...] = partial
-
-    @pl.when(step > 0)
-    def _():
-        acc[...] += partial
+    size = w_ref.shape[0]
+    for at, ref in ((0, w_ref), (size, u_ref)):
+        if ref is None:
+            continue
+        partial = dot(x, ref[...], ((1,), (1,)))
+
+        @pl.when(step == 0)
+        def _(at=at, partial=partial):
+            acc[:, at : at + size] = partial
+
+        @pl.when(step > 0)
+        def _(at=at, partial=partial):
+            acc[:, at : at + size] += partial
 
     @pl.when(step == steps - 1)
     def _():
@@ -558,6 +565,13 @@
         def _(i):
             at = pl.ds(pl.multiple_of(i * chunk, chunk), chunk)
             grad = acc[at, :]
+            if split:
+                own, other = grad[:, :size], grad[:, size:]
+                low, high = jnp.where(flag[0] == 0, own, other), jnp.where(flag[0] == 0, other, own)
+                blocks = []
+                for k in range(0, size, 128):
+                    blocks += [low[:, k : k + 128], high[:, k : k + 128]]
+                grad = jnp.concatenate(blocks, axis=1)
             value = v_ref[at, :].astype(F32)
             factor = lax.rsqrt(jnp.mean(value * value, axis=-1, keepdims=True) + EPSILON)
             scaled = gain * grad
@@ -573,18 +587,21 @@
             o_ref[...] = dot(e_ref[...], n_ref[...], ((1,), (1,))).astype(BF16)
 
 
-def segment(order, x, w, column, tile, value, base, gain, after=None):
+def segment(order, core, x, w, column, tile, value, base, gain, after=None):
     rows, width = value.shape
     steps = x.shape[-1] * (x.shape[0] if x.ndim == 3 else 1) // tile
     if x.ndim == 3:
         per = x.shape[-1] // tile
-        x_spec = pl.BlockSpec((1, rows, tile), lambda k: (k // per, 0, k % per))
+        x_spec = pl.BlockSpec((1, rows, tile), lambda k, f: (k // per, 0, k % per))
     else:
-        x_spec = pl.BlockSpec((rows, tile), lambda k: (0, k))
-    whole = pl.BlockSpec((rows, width), lambda k: (0, 0))
-    line = pl.BlockSpec((1, width), lambda k: (0, 0))
-    specs = [x_spec, pl.BlockSpec((width, tile), lambda k: (0, k + column)), whole, whole, line]
-    operands = [x, w, value, base, gain.reshape(1, width)]
+        x_spec = pl.BlockSpec((rows, tile), lambda k, f: (0, k))
+    whole = pl.BlockSpec((rows, width), lambda k, f: (0, 0))
+    line = pl.BlockSpec((1, width), lambda k, f: (0, 0))
+    split = isinstance(w, tuple)
+    w = w if split else (w,)
+    w_spec = pl.BlockSpec((w[0].shape[0], tile), lambda k, f: (0, k + column))
+    specs = [x_spec, w_spec, whole, whole, line]
+    operands = [x, w[0], value, base, gain.reshape(1, width)]
     shapes = [
         jax.ShapeDtypeStruct((rows, width), F32),
         jax.ShapeDtypeStruct((1, width), F32),
@@ -592,29 +609,51 @@
     outs = [whole, line]
     if after is not None:
         matrix, at = after
-        specs.append(pl.BlockSpec((width, width), lambda k: (0, at)))
+        specs.append(pl.BlockSpec((width, width), lambda k, f: (0, at)))
         operands.append(matrix)
         shapes += [jax.ShapeDtypeStruct((rows, width), BF16)] * 2
         outs += [whole, whole]
+    if split:
+        specs.append(w_spec)
+        operands.append(w[1])
     waits = order.take()
     out = pl.pallas_call(
-        functools.partial(segment_kernel, steps, after is not None, len(waits)),
-        grid=(steps,),
-        in_specs=specs + [pl.BlockSpec(memory_space=pl.ANY)] * len(waits),
-        out_specs=outs,
+        functools.partial(segment_kernel, steps, after is not None, split, len(waits)),
+        grid_spec=pltpu.PrefetchScalarGridSpec(
+            num_scalar_prefetch=1,
+            grid=(steps,),
+            in_specs=specs + [pl.BlockSpec(memory_space=pl.ANY)] * len(waits),
+            out_specs=outs,
+            scratch_shapes=[pltpu.VMEM((rows, width), F32)],
+        ),
         out_shape=shapes,
-        scratch_shapes=[pltpu.VMEM((rows, width), F32)],
         compiler_params=params(),
         cost_estimate=cost(order.long()),
-    )(*operands, *waits)
+    )(core.reshape(1), *operands, *waits)
     order.after(out[1])
     return out
 
 
-def mlp_kernel(a_ref, e_ref, wg_ref, wu_ref, wd_ref, i_ref, d_ref):
+def halves_of(value):
+    starts = range(0, value.shape[1], 256)
+    return [
+        jnp.concatenate([value[:, k + j : k + j + 128] for k in starts], axis=1)
+        for j in (0, 128)
+    ]
+
+
+def mlp_kernel(flag, a_ref, e_ref, wg_ref, wu_ref, vg_ref, vu_ref, wd_ref, i_ref, d_ref, mine):
+    @pl.when(pl.program_id(0) == 0)
+    def _():
+        def put(own, other):
+            mine[0] = own
+            mine[1] = other
+
+        either(flag[0], put, *halves_of(a_ref[...]))
+
     grad = dot(e_ref[...], wd_ref[...], ((1,), (1,)))
-    gate = dot(a_ref[...], wg_ref[...], ((1,), (0,)))
-    up = dot(a_ref[...], wu_ref[...], ((1,), (0,)))
+    product = lambda w, v: dot(mine[0], w[...], ((1,), (0,))) + dot(mine[1], v[...], ((1,), (0,)))
+    gate, up = product(wg_ref, vg_ref), product(wu_ref, vu_ref)
     slope, cubic = 0.7978845608028654, 0.044715
     square = gate * gate
     bend = jnp.tanh(slope * gate * (1.0 + cubic * square))
@@ -626,33 +665,41 @@
     d_ref[1] = (grad * act).astype(BF16)
 
 
-def mlp(order, a3, e3, w_wide, w_down):
+def mlp(order, core, a3, e3, own, other, w_down):
     rows, width = a3.shape
     hidden = w_down.shape[0]
-    tile = 256
+    tile = MLP_TILE
     count = hidden // tile
-    whole = pl.BlockSpec((rows, width), lambda j: (0, 0))
+    whole = pl.BlockSpec((rows, width), lambda j, f: (0, 0))
+    gate = pl.BlockSpec((width // 2, tile), lambda j, f: (0, j))
+    up = pl.BlockSpec((width // 2, tile), lambda j, f: (0, count + j))
     return pl.pallas_call(
         mlp_kernel,
-        grid=(count,),
-        in_specs=[
-            whole,
-            whole,
-            pl.BlockSpec((width, tile), lambda j: (0, j)),
-            pl.BlockSpec((width, tile), lambda j: (0, count + j)),
-            pl.BlockSpec((tile, width), lambda j: (j, 0)),
-        ],
-        out_specs=[
-            pl.BlockSpec((rows, tile), lambda j: (0, j)),
-            pl.BlockSpec((2, rows, tile), lambda j: (0, 0, j)),
-        ],
+        grid_spec=pltpu.PrefetchScalarGridSpec(
+            num_scalar_prefetch=1,
+            grid=(count,),
+            in_specs=[
+                whole,
+                whole,
+                gate,
+                up,
+                gate,
+                up,
+                pl.BlockSpec((tile, width), lambda j, f: (j, 0)),
+            ],
+            out_specs=[
+                pl.BlockSpec((rows, tile), lambda j, f: (0, j)),
+                pl.BlockSpec((2, rows, tile), lambda j, f: (0, 0, j)),
+            ],
+            scratch_shapes=[pltpu.VMEM((2, rows, width // 2), BF16)],
+        ),
         out_shape=[
             jax.ShapeDtypeStruct((rows, hidden), BF16),
             jax.ShapeDtypeStruct((2, rows, hidden), BF16),
         ],
         compiler_params=params(),
         cost_estimate=cost(order.long()),
-    )(a3, e3, w_wide, w_wide, w_down)
+    )(core.reshape(1), a3, e3, own, own, other, other, w_down)
 
 
 def forward_out_kernel(steps, waits, x_ref, w_ref, b_ref, *refs):
@@ -799,10 +846,43 @@
     return out
 
 
-def eighth(spot, shard, axis):
-    size = shard.shape[axis] // 8
+def pack_kernel(tall, place, *refs):
+    refs = list(refs)
+    if tall:
+        last_in, last_out = refs.pop(len(refs) - 3), refs.pop()
+        last_out[...] = last_in[...]
+    column = 0
+    for ref in refs[:-1]:
+        refs[-1][:, column : column + ref.shape[1]] = ref[...]
+        column += ref.shape[1]
+
+
+def pack(spot, shards, last=None, tall=None):
+    n = shards[0].shape[0] // 8
     seat = 4 * bit_of(spot, 1) + 2 * bit_of(spot, 4) + bit_of(spot, 2)
-    return lax.dynamic_slice_in_dim(shard, seat * size, size, axis)
+    specs = [pl.BlockSpec((n, w.shape[1]), lambda j, f: (f[0], 0)) for w in shards]
+    total = sum(w.shape[1] for w in shards)
+    operands = list(shards)
+    if last is not None:
+        specs.append(pl.BlockSpec(last.shape, lambda j, f: (0, 0)))
+        operands.append(last)
+        total += last.shape[1]
+    outs, shapes = [pl.BlockSpec((n, total), lambda j, f: (0, 0))], [(n, total)]
+    if tall is not None:
+        piece = (tall.shape[0], tall.shape[1] // 8)
+        specs.append(pl.BlockSpec(piece, lambda j, f: (0, f[0])))
+        operands.append(tall)
+        outs.append(pl.BlockSpec(piece, lambda j, f: (0, 0)))
+        shapes.append(piece)
+    return pl.pallas_call(
+        functools.partial(pack_kernel, tall is not None),
+        grid_spec=pltpu.PrefetchScalarGridSpec(
+            num_scalar_prefetch=1, grid=(1,), in_specs=specs, out_specs=outs
+        ),
+        out_shape=[jax.ShapeDtypeStruct(shape, BF16) for shape in shapes],
+        compiler_params=params(),
+        cost_estimate=cost(1),
+    )(seat.reshape(1), *operands)
 
 
 def pairs_kernel(axis, flags, *refs):
@@ -996,9 +1076,7 @@
     spot = 4 * lax.axis_index("y") + 2 * lax.axis_index("x") + lax.axis_index("core")
 
     order = Order()
-    join = lambda *parts: jnp.concatenate(parts, axis=1)
     gather = lambda value: lax.all_gather(value, "fsdp", axis=0)
-    g_down = Gather(order, spot, gather(eighth(spot, mlp_down, 1)), 1)
     own = self_gain.shape[0]
     lines = jnp.stack([self_gain, cross_gain, mlp_gain]).reshape(-1, 128)
     squares = [
@@ -1012,15 +1090,15 @@
         cross_output,
     ]
     lines = jnp.pad(lines, ((0, width // 32 - lines.shape[0]), (0, 0)))
-    both = gather(join(*[eighth(spot, w, 0) for w in squares], lines))
+    piece, piece_down = pack(spot, squares, lines, mlp_down)
+    both = gather(piece)
+    g_down = Gather(order, spot, gather(piece_down), 1)
     g_self = Gather(order, spot, both, 0, 0, 4 * width)
     g_cross = Gather(order, spot, both, 0, 1, 4 * width)
     shards = both.shape[0]
     gains = both[:, : 3 * own // 128, 8 * width :].reshape(shards, 3, own)
     gains = gains.transpose(1, 0, 2).reshape(3, width).astype(F32)
-    g_wide = Gather(
-        order, spot, gather(join(eighth(spot, mlp_gate, 0), eighth(spot, mlp_up, 0))), 0
-    )
+    g_wide = Gather(order, spot, gather(*pack(spot, [mlp_gate, mlp_up])), 0)
     hidden = mlp_gate.shape[1]
 
     x = text.reshape(-1, width).astype(F32)
@@ -1065,22 +1143,19 @@
     h2 = h1 + matmul(o2, w_co)
     c3 = factor_of(h2)
     a3 = (h2 * c3 * gains[2]).astype(BF16)
-    order.after(a3)
-    w_wide = g_wide.four()
-    inner, d_wide = mlp(order, a3, e3, w_wide, w_down)
+    core = bit_of(spot, 1)
+    flat = lambda value: value.reshape(-1, 2 * hidden)
+    w_wide = flat(g_wide.half), flat(g_wide.got)
+    inner, d_wide = mlp(order, core, a3, e3, *w_wide, w_down)
     order.take()
 
-    sum_of = lambda first, second, pairs: Sum(
-        order, spot, 0, functools.partial(grad_rows, order, pairs), first, second
-    )
-    s_gate = sum_of(2, 4, [(a3, d_wide, 0, hidden)])
-    s_up = sum_of(4, 2, [(a3, d_wide, 1, hidden)])
+    s_wide = Pair(order, spot, [(a3, d_wide, 0, hidden), (a3, d_wide, 1, hidden)])
     s_down = Sum(order, spot, 1, functools.partial(grad_columns, order, inner, e3), 2, 4)
-    s_gate.core()
-    s_up.core()
+    wide = s_wide.core()
+    s_down.core()
     order.micros = C_LONG
     d_h2, gg3, e2, d_o2 = segment(
-        order, d_wide, w_wide, 0, hidden // 2, h2, e3, gains[2], (w_cross, 3)
+        order, core, d_wide, w_wide, 0, hidden // 2, h2, e3, gains[2], (w_cross, 3)
     )
     d_q2, d_kv = cross_backward(order, q2, kv, p2, d_o2.reshape(text.shape), mask)
     d_q2 = d_q2.reshape(-1, width)
@@ -1094,13 +1169,16 @@
             (o2, e2, 0, width),
         ],
     )
-    s_down.core()
-    land_first(order, s_gate, s_up)
+    land_first(order, *wide)
+    order.micros = C_SEG2
+    d_h1, gg2, e1, d_o1 = segment(
+        order, core, d_q2, w_cross, 4, width // 2, h1, d_h2, gains[1], (w_self, 3)
+    )
+    land_first(order, s_down)
     order.micros = C_LONG
-    d_h1, gg2, e1, d_o1 = segment(
-        order, d_q2, w_cross, 4, width // 2, h1, d_h2, gains[1], (w_self, 3)
-    )
+    z_wide = land_second(order, *wide)
     d_qkv = self_backward(order, qkv, p1, d_o1.reshape(text.shape)).reshape(-1, 3 * width)
+    z_down = land_second(order, s_down)
     s_self = Pair(
         order,
         spot,
@@ -1111,47 +1189,46 @@
         ],
     )
     cross = s_cross.core()
-    land_first(order, s_down)
-    z_wide = over_shards(land_second(order, s_gate, s_up))
+    z_wide = over_shards(z_wide)
     order.micros = C_LONG
-    grad_memory = back_product(order, d_kv, w_cross)
     both = s_self.core()
+    order.micros = C_LONG
+    grad_text, gg1 = segment(order, core, d_qkv, w_self, 0, width, x, d_h1, gains[0])
     land_first(order, *cross)
-    z_down = over_shards(land_second(order, s_down))
-    order.micros = C_SEG1
-    grad_text, gg1 = segment(order, d_qkv, w_self, 0, width, x, d_h1, gains[0])
+    order.micros = C_MID
     z_wide = hold(order, z_wide)
-    t_wide = Spread(order, spot, z_wide, [hidden, hidden], [False, True])
+    z_down = over_shards(z_down)
+    land_first(order, *both)
     z_down = hold(order, z_down)
     z_cross = over_shards(land_second(order, *cross))
-    land_first(order, *both)
+    t_wide = Spread(order, spot, z_wide, [hidden, hidden], [False, True])
     lines = jnp.concatenate([gg1, gg2, gg3]).reshape(3, shards, own).transpose(1, 0, 2)
     lines = lines.reshape(shards, -1, 128)
     lines = jnp.pad(lines, ((0, 0), (0, width // 32 - lines.shape[1]), (0, 0)))
     lines = order.after(lines.astype(BF16).reshape(-1, 128))
-    order.micros = C_LONG
+    z_self = land_second(order, *both)
+    z_self = order.after(jnp.concatenate([z_self, lines], axis=1))
     t_wide.land()
-    z_self = land_second(order, *both)
-    z_self = over_shards(jnp.concatenate([z_self, lines], axis=1))
+    t_down = Spread(order, spot, z_down, [width], [False], 1)
     z_cross = hold(order, z_cross)
-    order.micros = C_LONG
-    block_out = forward_out(order, inner, w_down, h2)
+    z_self = over_shards(z_self)
     squares = [width] * 4
     t_cross = Spread(order, spot, z_cross, squares, [False, False, True, True])
-    t_down = Spread(order, spot, z_down, [width], [False], 1)
+    block_out = forward_out(order, inner, w_down, h2)
+    t_down.land()
+    t_cross.land()
     t_wide.land()
-    t_cross.land()
-    t_down.land()
-    t_wide.land()
-    t_cross.land()
+    grad_memory = back_product(order, d_kv, w_cross)
     z_self = hold(order, z_self)
     t_self = Spread(
         order, spot, z_self, [*squares, 128], [False, False, True, True, False]
     )
     t_down.land()
     t_cross.land()
+    t_wide.land()
     t_self.land()
     t_down.land()
+    t_cross.land()
     t_self.land()
     t_self.land()
     g_gate, g_up = t_wide.values

time: 649 us -> 624 us (0.961)
  Pallas kernels: 345 us -> 336 us
  local copies, waits for them, and re-layouts: 52.7 us -> 43.7 us
    reduce_scatter x4, waiting for transfers between devices: 15.6 us -> 0.01 us  [over_shards(): value = lax.psum_scatter(value, 'fsdp', scatter_dimension=0, tiled=True)]
    ppermute x51 -> x50, waiting for transfers between devices: 90.1 us -> 101 us  [swap(): return lax.ppermute(value, AXES[bit], [(0, 1), (1, 0)])]
    pallas_call x12 -> x11, Pallas kernels: 72.2 us -> 62.5 us  [by_shard(): pl.pallas_call(functools.partial(kernel, axis), grid_spec=pltpu.PrefetchS...]
    unnamed x164 -> x156, local copies, waits for them, and re-layouts: 47 us -> 38.6 us
    pallas_call x10 -> x8, Pallas kernels: 79.2 us -> 74.8 us  [call_product(): pl.pallas_call(functools.partial(product_kernel, jobs, has_add, axis, len...]
    pallas_call x1 -> x3, Pallas kernels: 19.9 us -> 23.9 us  [the longest x1 20.1 us: mlp(): pl.pallas_call(mlp_kernel, grid_spec=pltpu.PrefetchScalarGridSpec(num_sca...]
    ppermute x51 -> x50, starting transfers between devices: 43.5 us -> 40.6 us  [swap(): return lax.ppermute(value, AXES[bit], [(0, 1), (1, 0)])]
  transfers between devices with their start and end apart: 57 -> 56, of which waited for: 23 -> 27; matrix products, arithmetic and copies ran while one was open for 6% -> 6% of each run, Pallas kernels for 44% -> 44%
where the time goes in v4:
time: 624 us; the launch traced here: 612 us
  Pallas kernels  336 us (54%)
  waiting for transfers between devices  111 us (18%)
  local copies, waits for them, and re-layouts  43.7 us (7%)
  starting transfers between devices  40.8 us (7%)
  blocking collectives  26.6 us (4%)
  matrix products  26.6 us (4%)
  between operations  15.1 us (2%)
  other arithmetic  11.4 us (2%)
    ppermute x50, waiting for transfers between devices, swap(): return lax.ppermute(value, AXES[bit], [(0, 1), (1, 0)])  101 us
    pallas_call x8, Pallas kernels, call_product(): pl.pallas_call(functools.partial(product_kernel, jobs, has_add, axis, len...  74.8 us
    pallas_call x11, Pallas kernels, by_shard(): pl.pallas_call(functools.partial(kernel, axis), grid_spec=pltpu.PrefetchS...  62.5 us
    pallas_call x3, Pallas kernels, segment(): pl.pallas_call(functools.partial(segment_kernel, steps, after is not None...  40.8 us
    ppermute x50, starting transfers between devices, swap(): return lax.ppermute(value, AXES[bit], [(0, 1), (1, 0)])  40.6 us
    unnamed x156, local copies, waits for them, and re-layouts  38.6 us
    pallas_call x12, Pallas kernels, land_join(): pl.pallas_call(functools.partial(join_kernel, axis, parts, turned), grid_...  32.4 us
    pallas_call x8, Pallas kernels, land_sums(): pl.pallas_call(functools.partial(land_kernel, len(pairs), axis), grid_spe...  27 us
  transfers between devices with their start and end apart: 56, of which 27 were waited for; matrix products, arithmetic and copies ran while one was open for 6% of the time, Pallas kernels for 44%

profile of v4, /device:TPU:0, one launch (start us, length us, event | category | flops | bytes accessed | tf_op | source)
XLA Modules:
  0.0 611.9 jit_solution(13196590364159407793)
XLA Ops:
  12.1 26.6 %all-gather.1 = bf16[2816,128]{1,0:T(8,128)(2,1)} all-gather(bf16[704,128]{1,0:T(8,128)(2,1)} %get-tuple-element.93), channel_id=3, replica_groups=mesh['group'=1,'y'=2,'x'=2,'core'=2,'fsdp'=4] {'fsdp'}, dimensions={0}, use_global_device_ids=true | all-gather | bytes 901120 | tf_op jit(solution)/shard_map/all_gather | solution.py:1079
  45.5 4.0 collective-permute-done.refs_1_
  51.7 4.4 shard_map.316
  58.3 8.2 %all-gather.6.cloned.1.call-done = bf16[128,8320]{1,0:T(8,128)(2,1)} async-done(((bf16[32,8320]{1,0:T(8,128)(2,1)}), bf16[128,8320]{1,0:T(8,128)(2,1)}) %all-gather.6.cloned.1.call-update) | async-done | bytes 2129936 | tf_op jit(solution)/shard_map/all_gather | solution.py:1079
  74.4 5.0 shard_map.319.refs_4_.own_ref
  85.4 8.8 %collective-permute-done.2.refs_1_ = bf16[4,32,2048]{2,1,0:T(8,128)(2,1)S(1)} collective-permute-done((bf16[4,32,2048]{2,1,0:T(8,128)(2,1)S(1)}, bf16[4,32,2048]{2,1,0:T(8,128)(2,1)S(1)}, u32[]{:S(2)}, u32[]{:S(2)}) %collective-permute-start.2) | collective-permute-done | bytes 524320 | tf_op jit(solution)/shard_map/ppermute | solution.py:266
  96.6 4.5 shard_map.320
  107.1 4.5 shard_map.322
  111.6 6.3 %shard_map.323.refs_0_ = bf16[4,704,1024]{2,1,0:T(8,128)(2,1)} custom-call(s32[3]{0:T(128)} %pad_add_fusion.flags, bf16[4,704,512]{2,1,0:T(8,128)(2,1)} %shard_map.319.refs_4_.own_ref, bf16[4,704,512]{2,1,0:T(8,128)(2,1)} %collective-permute-done.8.got_ref, bf16[4,64,2048]{2,1,0:T(8,128)(2,1)} %get-tuple-element.104.refs_0_), custom_call_target="tpu_custom_call" | custom-call | flops 115000000512 | bytes 360000000 | tf_op jit(solution)/shard_map/pallas_call | solution.py:936
  123.3 5.4 collective-permute-done.6.refs_1_
  130.0 5.5 shard_map.325.own_ref.refs_0_
  143.0 7.6 %shard_map.326.refs_4_ = bf16[4,256,4096]{2,1,0:T(8,128)(2,1)} custom-call(s32[3]{0:T(128)} %pad_add_fusion.flags, bf16[4,128,4096]{2,1,0:T(8,128)(2,1)} %shard_map.325.own_ref.refs_0_, bf16[4,128,4096]{2,1,0:T(8,128)(2,1)} %collective-permute-done.11.got_ref, bf16[4,128,4096]{2,1,0:T(8,128)(2,1)} %shard_map.325.own_ref.refs_0_), custom_call_target="tpu_custom_call" | custom-call | flops 115000000 | bytes 360000 | tf_op jit(solution)/shard_map/pallas_call | solution.py:936
  150.6 8.0 %fusion.2 = bf16[576,3072]{1,0:T(8,128)(2,1)} fusion(bf16[576,1024]{1,0:T(8,128)(2,1)S(1)} %get-tuple-element.167.refs_0_.refs_1_.refs_2_.refs_3_.refs_5_.refs_6_.refs_7_.refs_8_, bf16[1024,4096]{1,0:T(8,128)(2,1)} %bitcast.96), kind=kOutput, calls=%fused_computation.2 | convolution fusion | flops 3625648128 | bytes 11010048 | tf_op jit(solution)/shard_map/dot_general | solution.py:259
  158.6 9.6 %shard_map.327 = (bf16[4,144,1024]{2,1,0:T(8,128)(2,1)}, bf16[4,4,576,144]{3,2,1,0:T(8,128)(2,1)}) custom-call(s32[4]{0:T(128)} %lengths.1, bf16[4,144,3072]{2,1,0:T(8,128)(2,1)} %bitcast.111), custom_call_target="tpu_custom_call" | custom-call | flops 115000000 | bytes 360000 | tf_op jit(solution)/shard_map/pallas_call | solution.py:104
  168.2 11.5 %collective-permute-done.14.refs_1_ = bf16[4,32,2816]{2,1,0:T(8,128)(2,1)S(1)} collective-permute-done((bf16[4,32,2816]{2,1,0:T(8,128)(2,1)S(1)}, bf16[4,32,2816]{2,1,0:T(8,128)(2,1)S(1)}, u32[]{:S(2)}, u32[]{:S(2)}) %collective-permute-start.14) | collective-permute-done | bytes 720928 | tf_op jit(solution)/shard_map/ppermute | solution.py:266
  180.5 4.8 shard_map.328
  186.7 5.5 shard_map.329.own_ref.refs_0_
  199.7 7.7 %shard_map.330.refs_4_ = bf16[4,256,4096]{2,1,0:T(8,128)(2,1)} custom-call(s32[3]{0:T(128)} %pad_add_fusion.flags, bf16[4,128,4096]{2,1,0:T(8,128)(2,1)} %shard_map.329.own_ref.refs_0_, bf16[4,128,4096]{2,1,0:T(8,128)(2,1)} %collective-permute-done.16.got_ref, bf16[4,128,4096]{2,1,0:T(8,128)(2,1)} %shard_map.329.own_ref.refs_0_, ...), custom_call_target="tpu_custom_call" | custom-call | flops 115000000512 | bytes 360000000 | tf_op jit(solution)/shard_map/pallas_call | solution.py:936
  207.4 4.2 fusion.22
  211.6 8.2 %fusion.7 = bf16[2048,1024]{0,1:T(8,128)(2,1)} fusion(bf16[1024,1024]{1,0:T(8,128)(2,1)S(1)} %bitcast.67, bf16[1024,4096]{1,0:T(8,128)(2,1)} %bitcast.91), kind=kOutput, calls=%fused_computation.5 | convolution fusion | flops 4297064448 | bytes 10485760 | tf_op jit(solution)/shard_map/dot_general | solution.py:259
  219.8 9.2 %shard_map.331 = (bf16[4,144,1024]{2,1,0:T(8,128)(2,1)}, bf16[4,4,576,256]{3,2,1,0:T(8,128)(2,1)}) custom-call(bf16[4,144,1024]{2,1,0:T(8,128)(2,1)} %bitcast.127, bf16[4,256,2048]{2,1,0:T(8,128)(2,1)} %bitcast.109, s32[4,1,256]{2,1,0:T(1,128)} %broadcast_in_dim.2.m_ref), custom_call_target="tpu_custom_call" | custom-call | flops 115000000 | bytes 360000 | tf_op jit(solution)/shard_map/pallas_call | solution.py:183
  229.0 6.6 %shard_map.332 = bf16[4,128,5632]{2,1,0:T(8,128)(2,1)} custom-call(s32[3]{0:T(128)} %pad_add_fusion.flags, bf16[4,64,2816]{2,1,0:T(8,128)(2,1)} %get-tuple-element.109.refs_4_.refs_0_, bf16[4,64,2816]{2,1,0:T(8,128)(2,1)} %collective-permute-done.17.refs_1_, bf16[4,64,2816]{2,1,0:T(8,128)(2,1)} %get-tuple-element.111.refs_2_, ...), custom_call_target="tpu_custom_call" | custom-call | flops 115000000 | bytes 360000 | tf_op jit(solution)/shard_map/pallas_call | solution.py:936
  241.1 4.3 collective-permute-done.19
  245.4 20.1 %shard_map.333 = (bf16[576,2816]{1,0:T(8,128)(2,1)}, bf16[2,576,2816]{2,1,0:T(8,128)(2,1)}) custom-call(s32[1]{0:T(128)} %bitcast.flag, bf16[576,1024]{1,0:T(8,128)(2,1)} %multiply_convert_fusion.a_ref.refs_0_.refs_1_.refs_2_.refs_3_.refs_5_.refs_6_.refs_7_.refs_8_, bf16[576,1024]{1,0:T(8,128)(2,1)} %bitcast.113, bf16[512,5632]{1,0:T(8,128)(2,1)} %bitcast.84, ...), custom_call_target="tpu_custom_call" | custom-call | flops 115000000 | bytes 360000 | tf_op jit(solution)/shard_map/pallas_call | solution.py:676
  265.5 10.5 %shard_map.334.refs_2_ = bf16[512,5632]{1,0:T(8,128)(2,1)} custom-call(s32[3]{0:T(128)} %add_add_fusion.1.flags, bf16[576,1024]{1,0:T(8,128)(2,1)} %multiply_convert_fusion.a_ref.refs_0_.refs_1_.refs_2_.refs_3_.refs_5_.refs_6_.refs_7_.refs_8_, bf16[576,1024]{1,0:T(8,128)(2,1)} %multiply_convert_fusion.a_ref.refs_0_.refs_1_.refs_2_.refs_3_.refs_5_.refs_6_.refs_7_.refs_8_, ...), custom_call_target="tpu_custom_call" | custom-call | flops 115000000 | bytes 360000 | tf_op jit(solution)/shard_map/pallas_call | solution.py:362
  276.8 6.0 shard_map.335.refs_11_
  288.1 11.9 %shard_map.336 = (bf16[4,64,2816]{2,1,0:T(8,128)(2,1)}, bf16[4,64,2816]{2,1,0:T(8,128)(2,1)}, bf16[4,64,2816]{2,1,0:T(8,128)(2,1)}, bf16[4,64,2816]{2,1,0:T(8,128)(2,1)}) custom-call(s32[3]{0:T(128)} %add_add_fusion.flags, bf16[576,1024]{1,0:T(8,128)(2,1)} %multiply_convert_fusion.a_ref.refs_0_.refs_1_.refs_2_.refs_3_.refs_5_.refs_6_.refs_7_.refs_8_, ...), custom_call_target="tpu_custom_call" | custom-call | flops 115000000 | bytes 360000 | tf_op jit(solution)/shard_map/pallas_call | solution.py:362
  302.0 6.9 %shard_map.337 = (bf16[2816,256]{1,0:T(8,128)(2,1)}, bf16[2816,256]{1,0:T(8,128)(2,1)}) custom-call(s32[2]{0:T(128)} %pad_add_fusion.2.flags, bf16[576,2816]{1,0:T(8,128)(2,1)} %get-tuple-element.112.refs_0_.x_ref, bf16[576,1024]{1,0:T(8,128)(2,1)} %bitcast.115, bf16[2816,512]{1,0:T(8,128)(2,1)} %collective-permute-done.20.refs_2_, ...), custom_call_target="tpu_custom_call" | custom-call | flops 115000000 | bytes 360000 | tf_op jit(solution)/shard_map/pallas_call | solution.py:362
  309.6 19.2 %shard_map.338 = (f32[576,1024]{1,0:T(8,128)}, f32[1,1024]{1,0:T(1,128)}, bf16[576,1024]{1,0:T(8,128)(2,1)}, bf16[576,1024]{1,0:T(8,128)(2,1)}) custom-call(s32[1]{0:T(128)} %bitcast.flag, bf16[2,576,2816]{2,1,0:T(8,128)(2,1)} %get-tuple-element.114.refs_4_.refs_9_.refs_0_, bf16[512,5632]{1,0:T(8,128)(2,1)} %bitcast.86, f32[576,1024]{1,0:T(8,128)} %copy-done.21, ...), custom_call_target="tpu_custom_call" | custom-call | flops 115000000512 | bytes 360000000 | tf_op jit(solution)/shard_map/pallas_call | solution.py:620
  328.8 13.5 %shard_map.339 = (bf16[4,144,1024]{2,1,0:T(8,128)(2,1)}, bf16[4,256,2048]{2,1,0:T(8,128)(2,1)}) custom-call(bf16[4,144,1024]{2,1,0:T(8,128)(2,1)} %bitcast.128, bf16[4,256,2048]{2,1,0:T(8,128)(2,1)} %bitcast.110, bf16[4,4,576,256]{3,2,1,0:T(8,128)(2,1)} %get-tuple-element.113.p_ref, bf16[4,144,1024]{2,1,0:T(8,128)(2,1)} %bitcast.134, ...), custom_call_target="tpu_custom_call" | custom-call | flops 115000000 | bytes 360000 | tf_op jit(solution)/shard_map/pallas_call | solution.py:228
  342.3 9.6 %shard_map.340.refs_4_ = bf16[512,4096]{1,0:T(8,128)(2,1)} custom-call(s32[3]{0:T(128)} %add_add_fusion.1.flags, bf16[1024,1024]{1,0:T(8,128)(2,1)} %bitcast.59, bf16[1024,1024]{1,0:T(8,128)(2,1)} %bitcast.60, bf16[1024,1024]{1,0:T(8,128)(2,1)} %bitcast.61, bf16[1024,1024]{1,0:T(8,128)(2,1)} %bitcast.62, bf16[1024,2048]{1,0:T(8,128)(2,1)} %bitcast.87, ...), custom_call_target="tpu_custom_call" | custom-call | flops 115000000 | bytes 360000 | tf_op jit(solution)/shard_map/pallas_call | solution.py:362
  353.5 4.6 shard_map.341
  360.3 10.4 %shard_map.342 = (f32[576,1024]{1,0:T(8,128)}, f32[1,1024]{1,0:T(1,128)}, bf16[576,1024]{1,0:T(8,128)(2,1)}, bf16[576,1024]{1,0:T(8,128)(2,1)}) custom-call(s32[1]{0:T(128)} %bitcast.flag, bf16[576,1024]{1,0:T(8,128)(2,1)} %bitcast.118, bf16[1024,4096]{1,0:T(8,128)(2,1)} %bitcast.94, f32[576,1024]{1,0:T(8,128)} %copy-done.30, ...), custom_call_target="tpu_custom_call" | custom-call | flops 12650000384 | bytes 39600000 | tf_op jit(solution)/shard_map/pallas_call | solution.py:620
  384.5 11.5 %shard_map.345.refs_2_ = bf16[4,144,3072]{2,1,0:T(8,128)(2,1)} custom-call(bf16[4,144,3072]{2,1,0:T(8,128)(2,1)} %bitcast.112, bf16[4,4,576,144]{3,2,1,0:T(8,128)(2,1)} %get-tuple-element.122.p_ref, bf16[4,144,1024]{2,1,0:T(8,128)(2,1)} %bitcast.133, bf16[4,32,5632]{2,1,0:T(8,128)(2,1)} %shard_map.344.refs_0_), custom_call_target="tpu_custom_call" | custom-call | flops 115000000 | bytes 360000 | tf_op jit(solution)/shard_map/pallas_call | solution.py:147
  399.0 8.7 %shard_map.347.refs_16_ = bf16[512,4096]{1,0:T(8,128)(2,1)} custom-call(s32[3]{0:T(128)} %add_add_fusion.1.flags, bf16[576,1024]{1,0:T(8,128)(2,1)} %copy-done.19, bf16[576,1024]{1,0:T(8,128)(2,1)} %copy-done.19, bf16[576,1024]{1,0:T(8,128)(2,1)} %copy-done.19, bf16[576,1024]{1,0:T(8,128)(2,1)} %copy-done.19, bf16[576,3072]{1,0:T(8,128)(2,1)} %bitcast.77, ...), custom_call_target="tpu_custom_call" | custom-call | flops 115000000 | bytes 360000 | tf_op jit(solution)/shard_map/pallas_call | solution.py:362
  408.4 11.0 %shard_map.348 = (bf16[4,64,2048]{2,1,0:T(8,128)(2,1)}, bf16[4,64,2048]{2,1,0:T(8,128)(2,1)}, bf16[4,64,2048]{2,1,0:T(8,128)(2,1)}, bf16[4,64,2048]{2,1,0:T(8,128)(2,1)}) custom-call(s32[3]{0:T(128)} %add_add_fusion.flags, bf16[1024,1024]{1,0:T(8,128)(2,1)} %bitcast.63, bf16[1024,1024]{1,0:T(8,128)(2,1)} %bitcast.64, bf16[1024,1024]{1,0:T(8,128)(2,1)} %bitcast.65, ...), custom_call_target="tpu_custom_call" | custom-call | flops 115000000 | bytes 360000 | tf_op jit(solution)/shard_map/pallas_call | solution.py:362
  421.3 10.2 %shard_map.349 = (bf16[4,64,2048]{2,1,0:T(8,128)(2,1)}, bf16[4,64,2048]{2,1,0:T(8,128)(2,1)}, bf16[4,64,2048]{2,1,0:T(8,128)(2,1)}, bf16[4,64,2048]{2,1,0:T(8,128)(2,1)}) custom-call(s32[3]{0:T(128)} %add_add_fusion.flags, bf16[576,1024]{1,0:T(8,128)(2,1)} %copy-done.19, bf16[576,1024]{1,0:T(8,128)(2,1)} %copy-done.19, bf16[576,1024]{1,0:T(8,128)(2,1)} %copy-done.19, ...), custom_call_target="tpu_custom_call" | custom-call | flops 115000000512 | bytes 360000000 | tf_op jit(solution)/shard_map/pallas_call | solution.py:362
  433.8 11.2 %shard_map.350 = (f32[576,1024]{1,0:T(8,128)}, f32[1,1024]{1,0:T(1,128)}) custom-call(s32[1]{0:T(128)} %bitcast.flag, bf16[576,3072]{1,0:T(8,128)(2,1)} %bitcast.81, bf16[1024,4096]{1,0:T(8,128)(2,1)} %bitcast.99, f32[576,1024]{1,0:T(8,128)} %bitcast.131, f32[576,1024]{1,0:T(8,128)} %get-tuple-element.141.refs_3_, f32[1,1024]{1,0:T(1,128)} %bitcast.141, ...), custom_call_target="tpu_custom_call" | custom-call | flops 115000000512 | bytes 360000000 | tf_op jit(solution)/shard_map/pallas_call | solution.py:620
  446.4 4.0 shard_map.351
  455.3 12.8 %collective-permute-done.34.refs_1_ = bf16[4,64,2048]{2,1,0:T(8,128)(2,1)S(1)} collective-permute-done((bf16[4,64,2048]{2,1,0:T(8,128)(2,1)}, bf16[4,64,2048]{2,1,0:T(8,128)(2,1)S(1)}, u32[]{:S(2)}, u32[]{:S(2)}) %collective-permute-start.34) | collective-permute-done | bytes 1048608 | tf_op jit(solution)/shard_map/ppermute | solution.py:266
  469.7 4.0 shard_map.353
  486.1 10.6 %collective-permute-done.37.refs_1_ = bf16[4,32,2048]{2,1,0:T(8,128)(2,1)S(1)} collective-permute-done((bf16[4,32,2048]{2,1,0:T(8,128)(2,1)S(1)}, bf16[4,32,2048]{2,1,0:T(8,128)(2,1)S(1)}, u32[]{:S(2)}, u32[]{:S(2)}) %collective-permute-start.37) | collective-permute-done | bytes 524320 | tf_op jit(solution)/shard_map/ppermute | solution.py:266
  505.0 7.7 %collective-permute-done.36.got_ref = bf16[32,5632]{1,0:T(8,128)(2,1)S(1)} collective-permute-done((bf16[32,5632]{1,0:T(8,128)(2,1)S(1)}, bf16[32,5632]{1,0:T(8,128)(2,1)S(1)}, u32[]{:S(2)}, u32[]{:S(2)}) %collective-permute-start.36) | collective-permute-done | bytes 360480 | tf_op jit(solution)/shard_map/ppermute | solution.py:266
  521.4 8.7 %shard_map.359.refs_0_ = bf16[576,1024]{1,0:T(8,128)(2,1)} custom-call(bf16[576,2816]{1,0:T(8,128)(2,1)} %get-tuple-element.112.refs_0_.x_ref, bf16[2816,1024]{1,0:T(8,128)(2,1)} %bitcast.83, f32[576,1024]{1,0:T(8,128)} %copy-done.21, bf16[32,4096]{1,0:T(8,128)(2,1)} %copy-done.6), custom_call_target="tpu_custom_call" | custom-call | flops 115000000 | bytes 360000 | tf_op jit(solution)/shard_map/pallas_call | solution.py:729
  540.8 9.1 %shard_map.363.refs_1_ = f32[1024,1024]{1,0:T(8,128)} custom-call(bf16[1024,2048]{1,0:T(8,128)(2,1)} %bitcast.89, bf16[1024,4096]{1,0:T(8,128)(2,1)} %bitcast.95, bf16[128,5632]{1,0:T(8,128)(2,1)} %shard_map.362.refs_0_.own_ref), custom_call_target="tpu_custom_call" | custom-call | flops 115000000 | bytes 360000 | tf_op jit(solution)/shard_map/pallas_call | solution.py:756
  553.7 7.1 %collective-permute-done.45.got_ref = bf16[704,256]{1,0:T(8,128)(2,1)S(1)} collective-permute-done((bf16[704,256]{1,0:T(8,128)(2,1)S(1)}, bf16[704,256]{1,0:T(8,128)(2,1)S(1)}, u32[]{:S(2)}, u32[]{:S(2)}) %collective-permute-start.45) | collective-permute-done | bytes 360480 | tf_op jit(solution)/shard_map/ppermute | solution.py:266
  569.5 4.7 shard_map.367
  587.9 4.4 collective-permute-done.46.got_ref
  (324 shorter events, 188.0 us)
Async XLA Ops:
  7.2 59.4 %all-gather.6.cloned.1.call-start = ((), (), s32[]{:S(2)}) async-start(), calls=%async_computation.8 | async-start | bytes 2662400 | tf_op jit(solution)/shard_map/all_gather | solution.py:1079
  12.0 107.8 %all-gather.8.cloned.1.call-start = ((), (), s32[]{:S(2)}) async-start(), calls=%async_computation.9 | async-start | bytes 1802240 | tf_op jit(solution)/shard_map/all_gather | solution.py:1079
  56.1 17.2 %collective-permute-start.4 = (bf16[4,352,256]{2,1,0:T(8,128)(2,1)}, bf16[4,352,256]{2,1,0:T(8,128)(2,1)S(1)}, u32[]{:S(2)}, u32[]{:S(2)}) collective-permute-start(bf16[4,352,256]{2,1,0:T(8,128)(2,1)} %get-tuple-element.96.refs_0_), channel_id=1, source_target_pairs={{0,16},{16,0},{1,17},{17,1},{2,18},{18,2},{3,19},{19,3},{4,20},{20... | collective-permute-start | bytes 2162696 | tf_op jit(solution)/shard_map/ppermute | solution.py:266
  57.6 15.7 %collective-permute-start.5 = (bf16[4,352,256]{2,1,0:T(8,128)(2,1)}, bf16[4,352,256]{2,1,0:T(8,128)(2,1)S(1)}, u32[]{:S(2)}, u32[]{:S(2)}) collective-permute-start(bf16[4,352,256]{2,1,0:T(8,128)(2,1)} %get-tuple-element.99.refs_2_), channel_id=1, source_target_pairs={{0,8},{8,0},{1,9},{9,1},{2,10},{10,2},{3,11},{11,3},{4,12},{12,4},... | collective-permute-start | bytes 2162696 | tf_op jit(solution)/shard_map/ppermute | solution.py:266
  79.4 32.2 %collective-permute-start.8 = (bf16[4,704,512]{2,1,0:T(8,128)(2,1)}, bf16[4,704,512]{2,1,0:T(8,128)(2,1)}, u32[]{:S(2)}, u32[]{:S(2)}) collective-permute-start(bf16[4,704,512]{2,1,0:T(8,128)(2,1)} %shard_map.319.refs_4_.own_ref), channel_id=1, source_target_pairs={{0,4},{4,0},{1,5},{5,1},{2,6},{6,2},{3,7},{7,3},{8,12},{12,8},{9,1... | collective-permute-start | bytes 8650760 | tf_op jit(solution)/shard_map/ppermute | solution.py:266
  79.5 14.7 %collective-permute-start.2 = (bf16[4,32,2048]{2,1,0:T(8,128)(2,1)S(1)}, bf16[4,32,2048]{2,1,0:T(8,128)(2,1)S(1)}, u32[]{:S(2)}, u32[]{:S(2)}) collective-permute-start(bf16[4,32,2048]{2,1,0:T(8,128)(2,1)S(1)} %copy-done.32), channel_id=1, source_target_pairs={{0,8},{8,0},{1,9},{9,1},{2,10},{10,2},{3,11},{11,3},{4,12},{12,4},... | collective-permute-start | bytes 1572872 | tf_op jit(solution)/shard_map/ppermute | solution.py:266
  81.0 14.8 %collective-permute-start.3 = (bf16[4,32,2048]{2,1,0:T(8,128)(2,1)S(1)}, bf16[4,32,2048]{2,1,0:T(8,128)(2,1)S(1)}, u32[]{:S(2)}, u32[]{:S(2)}) collective-permute-start(bf16[4,32,2048]{2,1,0:T(8,128)(2,1)S(1)} %copy-done.51), channel_id=1, source_target_pairs={{0,16},{16,0},{1,17},{17,1},{2,18},{18,2},{3,19},{19,3},{4,20},{20... | collective-permute-start | bytes 1572872 | tf_op jit(solution)/shard_map/ppermute | solution.py:266
  82.5 24.6 %collective-permute-start.10 = (bf16[4,32,2048]{2,1,0:T(8,128)(2,1)}, bf16[4,32,2048]{2,1,0:T(8,128)(2,1)}, u32[]{:S(2)}, u32[]{:S(2)}) collective-permute-start(bf16[4,32,2048]{2,1,0:T(8,128)(2,1)} %get-tuple-element.103.refs_2_), channel_id=1, source_target_pairs={{0,16},{16,0},{1,17},{17,1},{2,18},{18,2},{3,19},{19,3},{4,20},{20... | collective-permute-start | bytes 1572872 | tf_op jit(solution)/shard_map/ppermute | solution.py:266
  83.0 24.1 %collective-permute-start.9 = (bf16[4,32,2048]{2,1,0:T(8,128)(2,1)}, bf16[4,32,2048]{2,1,0:T(8,128)(2,1)}, u32[]{:S(2)}, u32[]{:S(2)}) collective-permute-start(bf16[4,32,2048]{2,1,0:T(8,128)(2,1)} %get-tuple-element.100.refs_4_.refs_0_), channel_id=1, source_target_pairs={{0,8},{8,0},{1,9},{9,1},{2,10},{10,2},{3,11},{11,3},{4,12},{12,4},... | collective-permute-start | bytes 1572872 | tf_op jit(solution)/shard_map/ppermute | solution.py:266
  85.3 367.1 %reduce-scatter.7.cloned.1.call-start = ((), (), s32[]{:S(2)}) async-start(), calls=%async_computation.5 | async-start | bytes 1802240 | tf_op jit(solution)/shard_map/reduce_scatter | solution.py:1009
  101.1 27.6 %collective-permute-start.6 = (bf16[4,64,2048]{2,1,0:T(8,128)(2,1)}, bf16[4,64,2048]{2,1,0:T(8,128)(2,1)S(1)}, u32[]{:S(2)}, u32[]{:S(2)}) collective-permute-start(bf16[4,64,2048]{2,1,0:T(8,128)(2,1)} %get-tuple-element.101.refs_4_.refs_0_), channel_id=1, source_target_pairs={{0,16},{16,0},{1,17},{17,1},{2,18},{18,2},{3,19},{19,3},{4,20},{20... | collective-permute-start | bytes 3145736 | tf_op jit(solution)/shard_map/ppermute | solution.py:266
  102.6 26.1 %collective-permute-start.7 = (bf16[4,64,2048]{2,1,0:T(8,128)(2,1)}, bf16[4,64,2048]{2,1,0:T(8,128)(2,1)S(1)}, u32[]{:S(2)}, u32[]{:S(2)}) collective-permute-start(bf16[4,64,2048]{2,1,0:T(8,128)(2,1)} %get-tuple-element.102.refs_2_), channel_id=1, source_target_pairs={{0,8},{8,0},{1,9},{9,1},{2,10},{10,2},{3,11},{11,3},{4,12},{12,4},... | collective-permute-start | bytes 3145736 | tf_op jit(solution)/shard_map/ppermute | solution.py:266
  137.2 48.1 %collective-permute-start.12 = (bf16[4,64,2048]{2,1,0:T(8,128)(2,1)}, bf16[4,64,2048]{2,1,0:T(8,128)(2,1)S(1)}, u32[]{:S(2)}, u32[]{:S(2)}) collective-permute-start(bf16[4,64,2048]{2,1,0:T(8,128)(2,1)} %get-tuple-element.104.refs_0_), channel_id=1, source_target_pairs={{0,16},{16,0},{1,17},{17,1},{2,18},{18,2},{3,19},{19,3},{4,20},{20... | collective-permute-start | bytes 3145736 | tf_op jit(solution)/shard_map/ppermute | solution.py:266
  138.7 46.6 %collective-permute-start.13 = (bf16[4,64,2048]{2,1,0:T(8,128)(2,1)}, bf16[4,64,2048]{2,1,0:T(8,128)(2,1)S(1)}, u32[]{:S(2)}, u32[]{:S(2)}) collective-permute-start(bf16[4,64,2048]{2,1,0:T(8,128)(2,1)} %get-tuple-element.107.refs_2_), channel_id=1, source_target_pairs={{0,8},{8,0},{1,9},{9,1},{2,10},{10,2},{3,11},{11,3},{4,12},{12,4},... | collective-permute-start | bytes 3145736 | tf_op jit(solution)/shard_map/ppermute | solution.py:266
  140.4 39.3 %collective-permute-start.14 = (bf16[4,32,2816]{2,1,0:T(8,128)(2,1)S(1)}, bf16[4,32,2816]{2,1,0:T(8,128)(2,1)S(1)}, u32[]{:S(2)}, u32[]{:S(2)}) collective-permute-start(bf16[4,32,2816]{2,1,0:T(8,128)(2,1)S(1)} %copy-done.28), channel_id=1, source_target_pairs={{0,8},{8,0},{1,9},{9,1},{2,10},{10,2},{3,11},{11,3},{4,12},{12,4},... | collective-permute-start | bytes 2162696 | tf_op jit(solution)/shard_map/ppermute | solution.py:266
  141.9 37.8 %collective-permute-start.15 = (bf16[4,32,2816]{2,1,0:T(8,128)(2,1)S(1)}, bf16[4,32,2816]{2,1,0:T(8,128)(2,1)}, u32[]{:S(2)}, u32[]{:S(2)}) collective-permute-start(bf16[4,32,2816]{2,1,0:T(8,128)(2,1)S(1)} %copy-done.46), channel_id=1, source_target_pairs={{0,16},{16,0},{1,17},{17,1},{2,18},{18,2},{3,19},{19,3},{4,20},{20... | collective-permute-start | bytes 2162696 | tf_op jit(solution)/shard_map/ppermute | solution.py:266
  192.8 36.2 %collective-permute-start.17 = (bf16[4,64,2816]{2,1,0:T(8,128)(2,1)S(1)}, bf16[4,64,2816]{2,1,0:T(8,128)(2,1)}, u32[]{:S(2)}, u32[]{:S(2)}) collective-permute-start(bf16[4,64,2816]{2,1,0:T(8,128)(2,1)S(1)} %copy-done.23), channel_id=1, source_target_pairs={{0,16},{16,0},{1,17},{17,1},{2,18},{18,2},{3,19},{19,3},{4,20},{20... | collective-permute-start | bytes 4325384 | tf_op jit(solution)/shard_map/ppermute | solution.py:266
  193.3 35.7 %collective-permute-start.18 = (bf16[4,64,2816]{2,1,0:T(8,128)(2,1)}, bf16[4,64,2816]{2,1,0:T(8,128)(2,1)}, u32[]{:S(2)}, u32[]{:S(2)}) collective-permute-start(bf16[4,64,2816]{2,1,0:T(8,128)(2,1)} %get-tuple-element.111.refs_2_), channel_id=1, source_target_pairs={{0,8},{8,0},{1,9},{9,1},{2,10},{10,2},{3,11},{11,3},{4,12},{12,4},... | collective-permute-start | bytes 4325384 | tf_op jit(solution)/shard_map/ppermute | solution.py:266
  235.6 9.8 %collective-permute-start.19 = (bf16[4,128,5632]{2,1,0:T(8,128)(2,1)}, bf16[4,128,5632]{2,1,0:T(8,128)(2,1)}, u32[]{:S(2)}, u32[]{:S(2)}) collective-permute-start(bf16[4,128,5632]{2,1,0:T(8,128)(2,1)} %shard_map.332), channel_id=1, source_target_pairs={{0,4},{4,0},{1,5},{5,1},{2,6},{6,2},{3,7},{7,3},{8,12},{12,8},{9,1... | collective-permute-start | bytes 17301512 | tf_op jit(solution)/shard_map/ppermute | solution.py:266
  276.0 9.6 %collective-permute-start.21 = (bf16[512,5632]{1,0:T(8,128)(2,1)}, bf16[512,5632]{1,0:T(8,128)(2,1)S(1)}, u32[]{:S(2)}, u32[]{:S(2)}) collective-permute-start(bf16[512,5632]{1,0:T(8,128)(2,1)} %shard_map.334.refs_2_), channel_id=1, source_target_pairs={{0,4},{4,0},{1,5},{5,1},{2,6},{6,2},{3,7},{7,3},{8,12},{12,8},{9,1... | collective-permute-start | bytes 17301512 | tf_op jit(solution)/shard_map/ppermute | solution.py:266
  282.8 19.2 %collective-permute-start.20 = (bf16[2816,512]{1,0:T(8,128)(2,1)}, bf16[2816,512]{1,0:T(8,128)(2,1)}, u32[]{:S(2)}, u32[]{:S(2)}) collective-permute-start(bf16[2816,512]{1,0:T(8,128)(2,1)} %shard_map.335.refs_11_), channel_id=1, source_target_pairs={{0,4},{4,0},{1,5},{5,1},{2,6},{6,2},{3,7},{7,3},{8,12},{12,8},{9,1... | collective-permute-start | bytes 8650760 | tf_op jit(solution)/shard_map/ppermute | solution.py:266
  300.0 51.9 %collective-permute-start.23 = (bf16[4,64,2816]{2,1,0:T(8,128)(2,1)}, bf16[4,64,2816]{2,1,0:T(8,128)(2,1)S(1)}, u32[]{:S(2)}, u32[]{:S(2)}) collective-permute-start(bf16[4,64,2816]{2,1,0:T(8,128)(2,1)} %get-tuple-element.115.refs_3_), channel_id=1, source_target_pairs={{0,8},{8,0},{1,9},{9,1},{2,10},{10,2},{3,11},{11,3},{4,12},{12,4},... | collective-permute-start | bytes 4325384 | tf_op jit(solution)/shard_map/ppermute | solution.py:266
  300.7 51.3 %collective-permute-start.24 = (bf16[4,64,2816]{2,1,0:T(8,128)(2,1)}, bf16[4,64,2816]{2,1,0:T(8,128)(2,1)S(1)}, u32[]{:S(2)}, u32[]{:S(2)}) collective-permute-start(bf16[4,64,2816]{2,1,0:T(8,128)(2,1)} %get-tuple-element.126), channel_id=1, source_target_pairs={{0,16},{16,0},{1,17},{17,1},{2,18},{18,2},{3,19},{19,3},{4,20},{20... | collective-permute-start | bytes 4325384 | tf_op jit(solution)/shard_map/ppermute | solution.py:266
  308.9 61.8 %collective-permute-start.27 = (bf16[2816,256]{1,0:T(8,128)(2,1)}, bf16[2816,256]{1,0:T(8,128)(2,1)S(1)}, u32[]{:S(2)}, u32[]{:S(2)}) collective-permute-start(bf16[2816,256]{1,0:T(8,128)(2,1)} %get-tuple-element.116.refs_7_), channel_id=1, source_target_pairs={{0,8},{8,0},{1,9},{9,1},{2,10},{10,2},{3,11},{11,3},{4,12},{12,4},... | collective-permute-start | bytes 4325384 | tf_op jit(solution)/shard_map/ppermute | solution.py:266
  351.9 56.5 %collective-permute-start.22 = (bf16[512,4096]{1,0:T(8,128)(2,1)}, bf16[512,4096]{1,0:T(8,128)(2,1)}, u32[]{:S(2)}, u32[]{:S(2)}) collective-permute-start(bf16[512,4096]{1,0:T(8,128)(2,1)} %shard_map.340.refs_4_), channel_id=1, source_target_pairs={{0,4},{4,0},{1,5},{5,1},{2,6},{6,2},{3,7},{7,3},{8,12},{12,8},{9,1... | collective-permute-start | bytes 12582920 | tf_op jit(solution)/shard_map/ppermute | solution.py:266
  358.2 18.7 %collective-permute-start.25 = (bf16[4,32,2816]{2,1,0:T(8,128)(2,1)}, bf16[4,32,2816]{2,1,0:T(8,128)(2,1)S(1)}, u32[]{:S(2)}, u32[]{:S(2)}) collective-permute-start(bf16[4,32,2816]{2,1,0:T(8,128)(2,1)} %get-tuple-element.127.refs_6_), channel_id=1, source_target_pairs={{0,16},{16,0},{1,17},{17,1},{2,18},{18,2},{3,19},{19,3},{4,20},{20... | collective-permute-start | bytes 2162696 | tf_op jit(solution)/shard_map/ppermute | solution.py:266
  359.6 20.7 %collective-permute-start.26 = (bf16[4,32,2816]{2,1,0:T(8,128)(2,1)}, bf16[4,32,2816]{2,1,0:T(8,128)(2,1)S(1)}, u32[]{:S(2)}, u32[]{:S(2)}) collective-permute-start(bf16[4,32,2816]{2,1,0:T(8,128)(2,1)} %get-tuple-element.131), channel_id=1, source_target_pairs={{0,8},{8,0},{1,9},{9,1},{2,10},{10,2},{3,11},{11,3},{4,12},{12,4},... | collective-permute-start | bytes 2162696 | tf_op jit(solution)/shard_map/ppermute | solution.py:266
  374.6 21.4 %collective-permute-start.28 = (bf16[2816,128]{1,0:T(8,128)(2,1)}, bf16[2816,128]{1,0:T(8,128)(2,1)S(1)}, u32[]{:S(2)}, u32[]{:S(2)}) collective-permute-start(bf16[2816,128]{1,0:T(8,128)(2,1)} %get-tuple-element.134.refs_4_), channel_id=1, source_target_pairs={{0,16},{16,0},{1,17},{17,1},{2,18},{18,2},{3,19},{19,3},{4,20},{20... | collective-permute-start | bytes 2162696 | tf_op jit(solution)/shard_map/ppermute | solution.py:266
  407.7 13.6 %collective-permute-start.31 = (bf16[512,4096]{1,0:T(8,128)(2,1)}, bf16[512,4096]{1,0:T(8,128)(2,1)}, u32[]{:S(2)}, u32[]{:S(2)}) collective-permute-start(bf16[512,4096]{1,0:T(8,128)(2,1)} %shard_map.347.refs_16_), channel_id=1, source_target_pairs={{0,4},{4,0},{1,5},{5,1},{2,6},{6,2},{3,7},{7,3},{8,12},{12,8},{9,1... | collective-permute-start | bytes 12582920 | tf_op jit(solution)/shard_map/ppermute | solution.py:266
  407.8 65.9 %reduce-scatter.5.cloned.1.call-start = ((), (), s32[]{:S(2)}) async-start(), calls=%async_computation.4 | async-start | bytes 901120 | tf_op jit(solution)/shard_map/reduce_scatter | solution.py:1009
  408.3 108.2 %reduce-scatter.9.cloned.1.call-start = ((), (), s32[]{:S(2)}) async-start(), calls=%async_computation.6 | async-start | bytes 1310720 | tf_op jit(solution)/shard_map/reduce_scatter | solution.py:1009
  419.4 26.3 %collective-permute-start.29 = (bf16[4,64,2048]{2,1,0:T(8,128)(2,1)}, bf16[4,64,2048]{2,1,0:T(8,128)(2,1)}, u32[]{:S(2)}, u32[]{:S(2)}) collective-permute-start(bf16[4,64,2048]{2,1,0:T(8,128)(2,1)} %get-tuple-element.138.refs_16_), channel_id=1, source_target_pairs={{0,8},{8,0},{1,9},{9,1},{2,10},{10,2},{3,11},{11,3},{4,12},{12,4},... | collective-permute-start | bytes 3145736 | tf_op jit(solution)/shard_map/ppermute | solution.py:266
  420.1 26.3 %collective-permute-start.30 = (bf16[4,64,2048]{2,1,0:T(8,128)(2,1)}, bf16[4,64,2048]{2,1,0:T(8,128)(2,1)}, u32[]{:S(2)}, u32[]{:S(2)}) collective-permute-start(bf16[4,64,2048]{2,1,0:T(8,128)(2,1)} %get-tuple-element.140), channel_id=1, source_target_pairs={{0,16},{16,0},{1,17},{17,1},{2,18},{18,2},{3,19},{19,3},{4,20},{20... | collective-permute-start | bytes 3145736 | tf_op jit(solution)/shard_map/ppermute | solution.py:266
  431.5 36.6 %collective-permute-start.34 = (bf16[4,64,2048]{2,1,0:T(8,128)(2,1)}, bf16[4,64,2048]{2,1,0:T(8,128)(2,1)S(1)}, u32[]{:S(2)}, u32[]{:S(2)}) collective-permute-start(bf16[4,64,2048]{2,1,0:T(8,128)(2,1)} %get-tuple-element.142.refs_5_), channel_id=1, source_target_pairs={{0,8},{8,0},{1,9},{9,1},{2,10},{10,2},{3,11},{11,3},{4,12},{12,4},... | collective-permute-start | bytes 3145736 | tf_op jit(solution)/shard_map/ppermute | solution.py:266
  432.3 36.4 %collective-permute-start.35 = (bf16[4,64,2048]{2,1,0:T(8,128)(2,1)}, bf16[4,64,2048]{2,1,0:T(8,128)(2,1)S(1)}, u32[]{:S(2)}, u32[]{:S(2)}) collective-permute-start(bf16[4,64,2048]{2,1,0:T(8,128)(2,1)} %get-tuple-element.150), channel_id=1, source_target_pairs={{0,16},{16,0},{1,17},{17,1},{2,18},{18,2},{3,19},{19,3},{4,20},{20... | collective-permute-start | bytes 3145736 | tf_op jit(solution)/shard_map/ppermute | solution.py:266
  450.3 28.9 %collective-permute-start.32 = (bf16[4,32,2048]{2,1,0:T(8,128)(2,1)}, bf16[4,32,2048]{2,1,0:T(8,128)(2,1)S(1)}, u32[]{:S(2)}, u32[]{:S(2)}) collective-permute-start(bf16[4,32,2048]{2,1,0:T(8,128)(2,1)} %get-tuple-element.145.refs_1_), channel_id=1, source_target_pairs={{0,16},{16,0},{1,17},{17,1},{2,18},{18,2},{3,19},{19,3},{4,20},{20... | collective-permute-start | bytes 1572872 | tf_op jit(solution)/shard_map/ppermute | solution.py:266
  451.7 27.6 %collective-permute-start.33 = (bf16[4,32,2048]{2,1,0:T(8,128)(2,1)}, bf16[4,32,2048]{2,1,0:T(8,128)(2,1)S(1)}, u32[]{:S(2)}, u32[]{:S(2)}) collective-permute-start(bf16[4,32,2048]{2,1,0:T(8,128)(2,1)} %get-tuple-element.147), channel_id=1, source_target_pairs={{0,8},{8,0},{1,9},{9,1},{2,10},{10,2},{3,11},{11,3},{4,12},{12,4},... | collective-permute-start | bytes 1572872 | tf_op jit(solution)/shard_map/ppermute | solution.py:266
  483.3 66.6 %reduce-scatter.11.cloned.1.call-start = ((), (), s32[]{:S(2)}) async-start(), calls=%async_computation.7 | async-start | bytes 1351680 | tf_op jit(solution)/shard_map/reduce_scatter | solution.py:1009
  483.3 13.4 %collective-permute-start.37 = (bf16[4,32,2048]{2,1,0:T(8,128)(2,1)S(1)}, bf16[4,32,2048]{2,1,0:T(8,128)(2,1)S(1)}, u32[]{:S(2)}, u32[]{:S(2)}) collective-permute-start(bf16[4,32,2048]{2,1,0:T(8,128)(2,1)S(1)} %copy-done.14), channel_id=1, source_target_pairs={{0,16},{16,0},{1,17},{17,1},{2,18},{18,2},{3,19},{19,3},{4,20},{20... | collective-permute-start | bytes 1572872 | tf_op jit(solution)/shard_map/ppermute | solution.py:266
  484.7 13.2 %collective-permute-start.38 = (bf16[4,32,2048]{2,1,0:T(8,128)(2,1)}, bf16[4,32,2048]{2,1,0:T(8,128)(2,1)S(1)}, u32[]{:S(2)}, u32[]{:S(2)}) collective-permute-start(bf16[4,32,2048]{2,1,0:T(8,128)(2,1)} %get-tuple-element.154), channel_id=1, source_target_pairs={{0,8},{8,0},{1,9},{9,1},{2,10},{10,2},{3,11},{11,3},{4,12},{12,4},... | collective-permute-start | bytes 1572872 | tf_op jit(solution)/shard_map/ppermute | solution.py:266
  515.5 19.7 %collective-permute-start.39 = (bf16[64,5632]{1,0:T(8,128)(2,1)}, bf16[64,5632]{1,0:T(8,128)(2,1)S(1)}, u32[]{:S(2)}, u32[]{:S(2)}) collective-permute-start(bf16[64,5632]{1,0:T(8,128)(2,1)} %shard_map.357.refs_1_.own_ref), channel_id=1, source_target_pairs={{0,8},{8,0},{1,9},{9,1},{2,10},{10,2},{3,11},{11,3},{4,12},{12,4},... | collective-permute-start | bytes 2162696 | tf_op jit(solution)/shard_map/ppermute | solution.py:266
  519.4 13.2 %collective-permute-start.40 = (bf16[32,4096]{1,0:T(8,128)(2,1)}, bf16[32,4096]{1,0:T(8,128)(2,1)S(1)}, u32[]{:S(2)}, u32[]{:S(2)}) collective-permute-start(bf16[32,4096]{1,0:T(8,128)(2,1)} %copy-done.6), channel_id=1, source_target_pairs={{0,16},{16,0},{1,17},{17,1},{2,18},{18,2},{3,19},{19,3},{4,20},{20... | collective-permute-start | bytes 786440 | tf_op jit(solution)/shard_map/ppermute | solution.py:266
  538.8 29.6 %collective-permute-start.43 = (bf16[128,5632]{1,0:T(8,128)(2,1)}, bf16[128,5632]{1,0:T(8,128)(2,1)S(1)}, u32[]{:S(2)}, u32[]{:S(2)}) collective-permute-start(bf16[128,5632]{1,0:T(8,128)(2,1)} %shard_map.362.refs_0_.own_ref), channel_id=1, source_target_pairs={{0,4},{4,0},{1,5},{5,1},{2,6},{6,2},{3,7},{7,3},{8,12},{12,8},{9,1... | collective-permute-start | bytes 4325384 | tf_op jit(solution)/shard_map/ppermute | solution.py:266
  538.8 24.9 %collective-permute-start.44 = (bf16[64,4096]{1,0:T(8,128)(2,1)S(1)}, bf16[64,4096]{1,0:T(8,128)(2,1)S(1)}, u32[]{:S(2)}, u32[]{:S(2)}) collective-permute-start(bf16[64,4096]{1,0:T(8,128)(2,1)S(1)} %copy-done.26), channel_id=1, source_target_pairs={{0,8},{8,0},{1,9},{9,1},{2,10},{10,2},{3,11},{11,3},{4,12},{12,4},... | collective-permute-start | bytes 1572872 | tf_op jit(solution)/shard_map/ppermute | solution.py:266
  539.8 21.1 %collective-permute-start.45 = (bf16[704,256]{1,0:T(8,128)(2,1)S(1)}, bf16[704,256]{1,0:T(8,128)(2,1)S(1)}, u32[]{:S(2)}, u32[]{:S(2)}) collective-permute-start(bf16[704,256]{1,0:T(8,128)(2,1)S(1)} %copy-done.27), channel_id=1, source_target_pairs={{0,8},{8,0},{1,9},{9,1},{2,10},{10,2},{3,11},{11,3},{4,12},{12,4},... | collective-permute-start | bytes 1081352 | tf_op jit(solution)/shard_map/ppermute | solution.py:266
  566.7 16.4 %collective-permute-start.47 = (bf16[128,4096]{1,0:T(8,128)(2,1)}, bf16[128,4096]{1,0:T(8,128)(2,1)S(1)}, u32[]{:S(2)}, u32[]{:S(2)}) collective-permute-start(bf16[128,4096]{1,0:T(8,128)(2,1)} %shard_map.366.refs_0_.own_ref), channel_id=1, source_target_pairs={{0,4},{4,0},{1,5},{5,1},{2,6},{6,2},{3,7},{7,3},{8,12},{12,8},{9,1... | collective-permute-start | bytes 3145736 | tf_op jit(solution)/shard_map/ppermute | solution.py:266
  568.2 10.9 %collective-permute-start.48 = (bf16[704,512]{1,0:T(8,128)(2,1)S(1)}, bf16[704,512]{1,0:T(8,128)(2,1)S(1)}, u32[]{:S(2)}, u32[]{:S(2)}) collective-permute-start(bf16[704,512]{1,0:T(8,128)(2,1)S(1)} %copy-done.22), channel_id=1, source_target_pairs={{0,4},{4,0},{1,5},{5,1},{2,6},{6,2},{3,7},{7,3},{8,12},{12,8},{9,1... | collective-permute-start | bytes 2162696 | tf_op jit(solution)/shard_map/ppermute | solution.py:266
  578.2 14.1 %collective-permute-start.46 = (bf16[64,4224]{1,0:T(8,128)(2,1)}, bf16[64,4224]{1,0:T(8,128)(2,1)S(1)}, u32[]{:S(2)}, u32[]{:S(2)}) collective-permute-start(bf16[64,4224]{1,0:T(8,128)(2,1)} %shard_map.368.refs_0_.own_ref), channel_id=1, source_target_pairs={{0,8},{8,0},{1,9},{9,1},{2,10},{10,2},{3,11},{11,3},{4,12},{12,4},... | collective-permute-start | bytes 1622024 | tf_op jit(solution)/shard_map/ppermute | solution.py:266
  (86 other events, 432.9 us)
Sparse Core Ops, SparseCore 0:
  12.1 54.4 all-gather.5
  85.5 34.2 all-gather.7
  407.9 31.6 reduce-scatter.6
  441.7 21.7 reduce-scatter.4
  483.4 25.4 reduce-scatter.8
  511.8 26.2 reduce-scatter.10
